TPU v7x, 32 devices: a whole 2x2x4 slice. The times are simulated.
32 devices in a mesh: dp: 4 (over y, core), ulysses: 8 (over z, x).
Axes of the slice: x: 2, y: 2, z: 4, core: 2. Of those that a mesh axis runs over, the one named last changes fastest.
Arguments:
- query_rows: bfloat16 [4096, 1024], P(('dp', 'ulysses')), may hold values from -6 to 6
- key_rows: bfloat16 [4096, 128], P(('dp', 'ulysses')), may hold values from -6 to 6
- value_rows: bfloat16 [4096, 128], P(('dp', 'ulysses')), may hold values from -6 to 6
- grad_out: bfloat16 [4096, 1024], P(('dp', 'ulysses')), may hold values from -6 to 6
- doc_lengths: int32 [4, 12], replicated, may hold values from 1 to 512, 1024 in all within a row
Outputs:
- attention: bfloat16 [4096, 1024], P(('dp', 'ulysses'))
- grad_queries: bfloat16 [4096, 1024], P(('dp', 'ulysses'))
- grad_keys: bfloat16 [4096, 128], P(('dp', 'ulysses'))
- grad_values: bfloat16 [4096, 128], P(('dp', 'ulysses'))
Inputs may be any that keep to these rules, and one draw needn't show every extreme that they name: `doc_lengths`: each row's 12 lengths sum to 1024, and the longest is 512.
All inputs are finite; a program needn't handle non-finite values.
Results may differ from a plain program's by a relative error of at most 0.011.
Values may be sent and summed in bfloat16 or wider, within the bound.
No kernel may reach another device: no remote copies, remote signals or barrier semaphores. Data moves between devices by JAX's collectives and lax.ppermute only.
A program may use at most 64 MiB of HBM per device.

v0:
```python
import functools
import math

import jax
import jax.numpy as jnp
from jax import lax
from jax.experimental import pallas as pl
from jax.experimental.pallas import tpu as pltpu
from jax.sharding import PartitionSpec as P

HD = 128
PAIR = 2
masked_score = -1e30
IN_ORDER = (0, 2, 1, 4, 3)
OUT_ORDER = (0, 4, 3, 1, 2)
score_scale = 1.0 / math.sqrt(HD)
exponent_scale = score_scale * math.log2(math.e)

NN = (((1,), (0,)), ((), ()))
NT = (((1,), (1,)), ((), ()))


def dot(a, b, dims=NN):
    return lax.dot_general(a, b, dims, preferred_element_type=jnp.float32)


def block(index, size):
    return slice(index * size, (index + 1) * size)


def fetch_kernel(doc_hbm, key_hbm, value_hbm, kv_ref, first_key_ref, doc_ref, sems):
    pairs = [(doc_hbm, doc_ref)]
    for shared in range(key_hbm.shape[1] // HD):
        for part, ref in enumerate((key_hbm, value_hbm)):
            pairs.append(
                (ref.at[:, pl.ds(shared * HD, HD)], kv_ref.at[:, pl.ds((2 * shared + part) * HD, HD)])
            )
    copies = [pltpu.make_async_copy(src, dst, sems.at[i]) for i, (src, dst) in enumerate(pairs)]
    for copy in copies:
        copy.start()
    tokens = key_hbm.shape[0]
    row = lax.axis_index("dp")
    place = lax.axis_index("ulysses")
    query_pos = place * tokens + lax.broadcasted_iota(jnp.int32, (1, tokens), 1)
    first_key = jnp.zeros((1, tokens), jnp.int32)
    copies[0].wait()
    doc_end = jnp.int32(0)
    for doc in range(doc_ref.shape[1]):
        doc_end = doc_end + doc_ref[row, doc]
        first_key = jnp.where(doc_end <= query_pos, doc_end, first_key)
    first_key_ref[...] = first_key
    for copy in copies[1:]:
        copy.wait()


def prepare_kernel(reach, first_key_ref, query_ref, grad_ref, *refs):
    query_rows_ref, grad_rows_ref, query_t_ref, grad_t_ref, bias_ref = refs
    tokens = query_ref.shape[0]
    place = lax.axis_index("ulysses")
    inner = lax.broadcasted_iota(jnp.int32, (tokens, tokens), 0)
    lanes = lax.broadcasted_iota(jnp.int32, (tokens, tokens), 1)
    first_key = first_key_ref[...] - place * tokens
    for back in range(reach + 1):
        key_pos = inner - back * tokens
        allowed = (key_pos >= first_key) & (key_pos <= lanes)
        bias_ref[block(back, tokens), :] = jnp.where(allowed, 0.0, masked_score).astype(
            jnp.bfloat16
        )
    identity = jnp.where(inner == lanes, 1.0, 0.0).astype(jnp.bfloat16)
    for head in range(query_ref.shape[1] // HD):
        own = block(head, tokens)
        queries = query_ref[:, block(head, HD)]
        grads = grad_ref[:, block(head, HD)]
        query_rows_ref[own, :] = queries
        grad_rows_ref[own, :] = grads
        query_t_ref[:HD, own] = queries.T
        query_t_ref[HD:, own] = identity
        grad_t_ref[:, own] = grads.T


def gradient_terms(weights, scores_grad, queries, grads):
    key_terms = dot(scores_grad, queries) * score_scale
    value_terms = dot(weights, grads)
    return jnp.concatenate([key_terms, value_terms], axis=1)


def parts(columns, tokens):
    width = min(columns, PAIR * tokens)
    return [slice(start, start + width) for start in range(0, columns, width)]


def biased_keys(kv_refs, bias_ref, places):
    tokens = kv_refs[0].shape[0]
    keys = jnp.concatenate([ref[:, :HD] for ref in kv_refs], axis=0)
    bias = jnp.concatenate([bias_ref[block(back, tokens), :] for back in places], axis=0)
    return jnp.concatenate([keys, bias], axis=1)


def early_kernel(early, query_t_ref, grad_t_ref, bias_ref, *refs):
    kv_refs = refs[: len(early)]
    weights_ref, grad_weights_ref, stats_ref, out_t_ref, scores_ref = refs[len(early) :]
    tokens = kv_refs[0].shape[0]
    columns = parts(query_t_ref.shape[1], tokens)
    keys = biased_keys(kv_refs, bias_ref, early)
    values = jnp.concatenate([ref[:, HD:] for ref in kv_refs], axis=0)
    values_t = values.T
    for part in columns:
        scores_ref[:, part] = dot(keys, query_t_ref[:, part])
    for part in columns:
        grad_weights_ref[:, part] = dot(values, grad_t_ref[:, part])
        top = jnp.max(scores_ref[:, part], axis=0, keepdims=True) * exponent_scale
        weights = jnp.exp2(scores_ref[:, part] * exponent_scale - top)
        stats_ref[0:1, part] = top
        stats_ref[1:2, part] = jnp.sum(weights, axis=0, keepdims=True)
        stats_ref[2:3, part] = jnp.sum(weights * grad_weights_ref[:, part], axis=0, keepdims=True)
        weights_ref[:, part] = weights.astype(jnp.bfloat16)
    for part in columns:
        out_t_ref[:, part] = dot(values_t, weights_ref[:, part])


def late_kernel(early, late, query_ref, grad_ref, query_t_ref, grad_t_ref, bias_ref, *refs):
    late_kv_ref, early_weights_ref, grad_weights_ref, stats_ref = refs[:4]
    weights_ref, scores_grad_ref, rescale_ref, *term_refs = refs[4:]
    tokens = late_kv_ref.shape[0]
    columns = parts(query_t_ref.shape[1], tokens)
    early_rows = slice(0, len(early) * tokens)
    late_rows = block(len(early), tokens)
    keys = biased_keys([late_kv_ref], bias_ref, [late])
    values = late_kv_ref[:, HD:]
    scores = [dot(keys, query_t_ref[:, part]) for part in columns]
    grad_weights = [dot(values, grad_t_ref[:, part]) for part in columns]
    for part, own, own_grad in zip(columns, scores, grad_weights):
        early_top = stats_ref[0:1, part]
        top = jnp.maximum(early_top, jnp.max(own, axis=0, keepdims=True) * exponent_scale)
        rescale = jnp.exp2(early_top - top)
        own = jnp.exp2(own * exponent_scale - top)
        total = rescale * stats_ref[1:2, part] + jnp.sum(own, axis=0, keepdims=True)
        inverse = 1.0 / total
        own = own * inverse
        rescale = rescale * inverse
        row_dots = rescale * stats_ref[2:3, part] + jnp.sum(own * own_grad, axis=0, keepdims=True)
        rescale_ref[:, part] = rescale
        weights_ref[late_rows, part] = own.astype(jnp.bfloat16)
        scores_grad_ref[late_rows, part] = (own * (own_grad - row_dots)).astype(jnp.bfloat16)
        own = early_weights_ref[:, part].astype(jnp.float32) * rescale
        weights_ref[early_rows, part] = own.astype(jnp.bfloat16)
        scores_grad_ref[early_rows, part] = (
            own * (grad_weights_ref[:, part] - row_dots)
        ).astype(jnp.bfloat16)
    terms = gradient_terms(
        weights_ref[tokens:, :], scores_grad_ref[tokens:, :], query_ref[...], grad_ref[...]
    ).astype(jnp.bfloat16)
    for place, ref in enumerate(term_refs):
        ref[...] = terms[block(place, tokens)]


def near_kernel(query_ref, grad_ref, weights_ref, scores_grad_ref, rescale_ref, *refs):
    early_out_t_ref, *kv_refs, out_ref, query_grad_ref, near_ref = refs
    tokens = kv_refs[0].shape[0]
    late_out_t = dot(kv_refs[-1][:, HD:].T, weights_ref[-tokens:, :])
    out_t = (early_out_t_ref[...] * rescale_ref[...] + late_out_t).astype(jnp.bfloat16)
    near_ref[...] = gradient_terms(
        weights_ref[:tokens, :], scores_grad_ref[:tokens, :], query_ref[...], grad_ref[...]
    )
    keys_t = jnp.concatenate([ref[:, :HD] for ref in kv_refs], axis=0).T
    query_grad_t = (dot(keys_t, scores_grad_ref[...]) * score_scale).astype(jnp.bfloat16)
    for head in range(out_ref.shape[1] // HD):
        own = block(head, tokens)
        query_grad_ref[:, block(head, HD)] = query_grad_t[:, own].T
        out_ref[:, block(head, HD)] = out_t[:, own].T


def call(body, name, outs, scratch, flops, *operands, fetched=False):
    vmem = pl.BlockSpec(memory_space=pltpu.VMEM)
    if fetched:
        operands = [pltpu.with_memory_space_constraint(a, pltpu.HBM) for a in operands]
    held = sum(math.prod(a.shape) * a.dtype.itemsize for a in operands)
    held += sum(math.prod(shape) * dtype.dtype.itemsize for shape, dtype in outs)
    held += sum(math.prod(s.shape) * 4 for s in scratch if hasattr(s, "shape"))
    return pl.pallas_call(
        body,
        out_shape=[jax.ShapeDtypeStruct(shape, dtype) for shape, dtype in outs],
        in_specs=[pl.BlockSpec(memory_space=pltpu.HBM) if fetched else vmem] * len(operands),
        out_specs=[vmem] * len(outs),
        scratch_shapes=scratch,
        compiler_params=pltpu.CompilerParams(
            vmem_limit_bytes=held + 12 * 1024 * 1024
        ),
        cost_estimate=pl.CostEstimate(flops=flops, bytes_accessed=held, transcendentals=0),
        name=name,
    )(*operands)


def ordered(values, order):
    first = [values[place] for place in order if place < len(values)]
    return first + [v for place, v in enumerate(values) if place not in order]


def per_device(devices, query_rows, key_rows, value_rows, grad_out, doc_lengths):
    tokens, query_width = query_rows.shape
    shared_heads = key_rows.shape[1] // HD
    length = tokens * devices
    reach = min(devices - 1, (length // 2 - 1 + tokens - 1) // tokens)
    blocks = reach + 1
    window = blocks * tokens
    low = jnp.bfloat16

    group_width = query_width // shared_heads
    columns = group_width // HD * tokens
    product = 2 * window * columns * HD
    kv, first_key = call(
        fetch_kernel,
        "fetch",
        [
            ((tokens, 2 * shared_heads * HD), low),
            ((1, tokens), jnp.int32),
        ],
        [
            pltpu.SMEM(doc_lengths.shape, jnp.int32),
            pltpu.SemaphoreType.DMA((2 * shared_heads + 1,)),
        ],
        16 * product,
        doc_lengths,
        key_rows,
        value_rows,
        fetched=True,
    )
    kv_blocks = {0: kv}
    for back in ordered(list(range(blocks)), IN_ORDER)[1:]:
        kv_blocks[back] = lax.ppermute(
            kv, "ulysses", [(d, d + back) for d in range(devices - back)]
        )
    late = list(kv_blocks)[1]
    early = [0] + [back for back in kv_blocks if back not in (0, late)]
    places = early + [late]
    window_early = len(early) * tokens

    attention, grad_queries, totals, far = [], [], [], []
    for shared in range(shared_heads):
        own_queries = query_rows[:, block(shared, group_width)]
        own_grads = grad_out[:, block(shared, group_width)]
        own_kv = [kv_blocks[back][:, block(shared, 2 * HD)] for back in places]
        queries, grads, queries_t, grads_t, bias = call(
            functools.partial(prepare_kernel, reach),
            "prepare",
            [
                ((columns, HD), low),
                ((columns, HD), low),
                ((HD + tokens, columns), low),
                ((HD, columns), low),
                ((window, tokens), low),
            ],
            [],
            product // 4,
            first_key,
            own_queries,
            own_grads,
        )
        weights, grad_weights, stats, early_out_t = call(
            functools.partial(early_kernel, early),
            "early",
            [
                ((window_early, columns), low),
                ((window_early, columns), jnp.float32),
                ((3, columns), jnp.float32),
                ((HD, columns), jnp.float32),
            ],
            [pltpu.VMEM((window_early, columns), jnp.float32)],
            3 * product,
            queries_t,
            grads_t,
            bias,
            *own_kv[:-1],
        )
        weights, scores_grad, rescale, *own_far = call(
            functools.partial(late_kernel, early, late),
            "late",
            [((window, columns), low), ((window, columns), low), ((1, columns), jnp.float32)]
            + [((tokens, 2 * HD), low)] * reach,
            [],
            2 * product,
            queries,
            grads,
            queries_t,
            grads_t,
            bias,
            own_kv[-1],
            weights,
            grad_weights,
            stats,
        )
        own_out, own_query_grad, own_total = call(
            near_kernel,
            "near",
            [((tokens, group_width), low)] * 2 + [((tokens, 2 * HD), jnp.float32)],
            [],
            2 * product,
            queries,
            grads,
            weights,
            scores_grad,
            rescale,
            early_out_t,
            *own_kv,
        )
        attention.append(own_out)
        grad_queries.append(own_query_grad)
        totals.append(own_total)
        far.append(own_far)

    def side_by_side(parts):
        return parts[0] if len(parts) == 1 else jnp.concatenate(parts, axis=1)

    far_places = places[1:]
    total = side_by_side(totals)
    for back in ordered(list(range(blocks)), OUT_ORDER)[1:]:
        terms = side_by_side([own[far_places.index(back)] for own in far])
        terms = lax.ppermute(terms, "ulysses", [(d, d - back) for d in range(back, devices)])
        total = total + terms.astype(jnp.float32)
    total = total.astype(low)
    grad_keys = side_by_side([total[:, block(2 * g, HD)] for g in range(shared_heads)])
    grad_values = side_by_side([total[:, block(2 * g + 1, HD)] for g in range(shared_heads)])
    return (side_by_side(attention), side_by_side(grad_queries), grad_keys, grad_values)


def solution(mesh):
    rows = P(("dp", "ulysses"), None)
    return jax.shard_map(
        functools.partial(per_device, mesh.shape["ulysses"]),
        mesh=mesh,
        in_specs=(rows, rows, rows, rows, P()),
        out_specs=(rows, rows, rows, rows),
        check_vma=False,
    )
```

profile of v0, /device:TPU:20, one launch (start us, length us, event | category | flops | bytes accessed | tf_op | source)
XLA Modules:
  0.0 31.7 jit_solution(6055393692115202049)
XLA Ops:
  0.6 0.0 copy-start.1
  0.6 0.0 copy-start
  0.7 0.9 %fetch.1 = (bf16[128,256]{1,0:T(8,128)(2,1)S(1)}, s32[1,128]{1,0:T(1,128)S(1)}) custom-call(s32[4,12]{1,0:T(4,128)} %doc_hbm.1, bf16[128,128]{1,0:T(8,128)(2,1)} %key_hbm.1, bf16[128,128]{1,0:T(8,128)(2,1)} %value_hbm.1), custom_call_target="tpu_custom_call" | custom-call | flops 2684354560 | bytes 131980 | tf_op jit(solution)/shard_map/fetch/pallas_call | solution.py:180
  1.5 4.4 %collective-permute-start.3 = (bf16[128,256]{1,0:T(8,128)(2,1)S(1)}, bf16[128,256]{1,0:T(8,128)(2,1)S(1)}, u32[]{:S(2)}, u32[]{:S(2)}) collective-permute-start(bf16[128,256]{1,0:T(8,128)(2,1)S(1)} %get-tuple-element.31.refs_0_.refs_1_), channel_id=1, source_target_pairs={{0,3},{1,4},{2,5},{3,6},{4,7},{8,11},{9,12},{10,13},{11,14},{12,15... | collective-permute-start | bytes 196616 | tf_op jit(solution)/shard_map/ppermute | solution.py:230
  5.9 1.3 %collective-permute-start.2 = (bf16[128,256]{1,0:T(8,128)(2,1)S(1)}, bf16[128,256]{1,0:T(8,128)(2,1)S(1)}, u32[]{:S(2)}, u32[]{:S(2)}) collective-permute-start(bf16[128,256]{1,0:T(8,128)(2,1)S(1)} %get-tuple-element.31.refs_0_.refs_1_), channel_id=1, source_target_pairs={{0,4},{1,5},{2,6},{3,7},{8,12},{9,13},{10,14},{11,15},{16,20},{17,... | collective-permute-start | bytes 196616 | tf_op jit(solution)/shard_map/ppermute | solution.py:230
  7.2 1.9 %collective-permute-start.1 = (bf16[128,256]{1,0:T(8,128)(2,1)S(1)}, bf16[128,256]{1,0:T(8,128)(2,1)S(1)}, u32[]{:S(2)}, u32[]{:S(2)}) collective-permute-start(bf16[128,256]{1,0:T(8,128)(2,1)S(1)} %get-tuple-element.31.refs_0_.refs_1_), channel_id=1, source_target_pairs={{0,1},{1,2},{2,3},{3,4},{4,5},{5,6},{6,7},{8,9},{9,10},{10,11},{11... | collective-permute-start | bytes 196616 | tf_op jit(solution)/shard_map/ppermute | solution.py:230
  9.2 1.9 %collective-permute-start = (bf16[128,256]{1,0:T(8,128)(2,1)S(1)}, bf16[128,256]{1,0:T(8,128)(2,1)S(1)}, u32[]{:S(2)}, u32[]{:S(2)}) collective-permute-start(bf16[128,256]{1,0:T(8,128)(2,1)S(1)} %get-tuple-element.31.refs_0_.refs_1_), channel_id=1, source_target_pairs={{0,2},{1,3},{2,4},{3,5},{4,6},{5,7},{8,10},{9,11},{10,12},{11,13},... | collective-permute-start | bytes 196616 | tf_op jit(solution)/shard_map/ppermute | solution.py:230
  11.1 0.0 copy-done.1
  11.1 0.0 copy-done
  11.1 0.3 prepare.1
  11.4 0.0 collective-permute-done.3.refs_3_.refs_4_
  11.4 1.6 %collective-permute-done.2.refs_2_.refs_3_ = bf16[128,256]{1,0:T(8,128)(2,1)S(1)} collective-permute-done((bf16[128,256]{1,0:T(8,128)(2,1)S(1)}, bf16[128,256]{1,0:T(8,128)(2,1)S(1)}, u32[]{:S(2)}, u32[]{:S(2)}) %collective-permute-start.2) | collective-permute-done | bytes 65568 | tf_op jit(solution)/shard_map/ppermute | solution.py:230
  13.0 2.2 %collective-permute-done.1.refs_1_.refs_2_ = bf16[128,256]{1,0:T(8,128)(2,1)S(1)} collective-permute-done((bf16[128,256]{1,0:T(8,128)(2,1)S(1)}, bf16[128,256]{1,0:T(8,128)(2,1)S(1)}, u32[]{:S(2)}, u32[]{:S(2)}) %collective-permute-start.1) | collective-permute-done | bytes 65568 | tf_op jit(solution)/shard_map/ppermute | solution.py:230
  15.2 1.4 %early.1 = (bf16[512,1024]{1,0:T(8,128)(2,1)S(1)}, f32[512,1024]{1,0:T(8,128)S(1)}, f32[3,1024]{1,0:T(4,128)S(1)}, f32[128,1024]{1,0:T(8,128)S(1)}) custom-call(bf16[256,1024]{1,0:T(8,128)(2,1)S(1)} %get-tuple-element.28.query_t_ref, bf16[128,1024]{1,0:T(8,128)(2,1)S(1)} %get-tuple-element.29.grad_t_ref, bf16[640,128]{1,0:T(8,128)(2,1)S(1)} %get-tuple-element.30.bias_ref, ...), custom_call_target="tpu_custom_call" | custom-call | flops 503316480 | bytes 6991872 | tf_op jit(solution)/shard_map/early/pallas_call | solution.py:180
  16.5 0.0 collective-permute-done.refs_0_.refs_5_
  16.5 1.4 %late.1 = (bf16[640,1024]{1,0:T(8,128)(2,1)S(1)}, bf16[640,1024]{1,0:T(8,128)(2,1)S(1)}, f32[1,1024]{1,0:T(1,128)S(1)}, bf16[128,256]{1,0:T(8,128)(2,1)S(1)}, bf...) custom-call(bf16[1024,128]{1,0:T(8,128)(2,1)S(1)} %get-tuple-element.26.query_ref, ...), custom_call_target="tpu_custom_call" | custom-call | flops 335544320 | bytes 7585792 | tf_op jit(solution)/shard_map/late/pallas_call | solution.py:180
  18.0 1.8 %collective-permute-start.4 = (bf16[128,256]{1,0:T(8,128)(2,1)S(1)}, bf16[128,256]{1,0:T(8,128)(2,1)S(1)}, u32[]{:S(2)}, u32[]{:S(2)}) collective-permute-start(bf16[128,256]{1,0:T(8,128)(2,1)S(1)} %get-tuple-element.42), channel_id=1, source_target_pairs={{4,0},{5,1},{6,2},{7,3},{12,8},{13,9},{14,10},{15,11},{20,16},{21,... | collective-permute-start | bytes 196616 | tf_op jit(solution)/shard_map/ppermute | solution.py:318
  19.8 2.2 %collective-permute-start.5 = (bf16[128,256]{1,0:T(8,128)(2,1)S(1)}, bf16[128,256]{1,0:T(8,128)(2,1)S(1)}, u32[]{:S(2)}, u32[]{:S(2)}) collective-permute-start(bf16[128,256]{1,0:T(8,128)(2,1)S(1)} %get-tuple-element.43), channel_id=1, source_target_pairs={{3,0},{4,1},{5,2},{6,3},{7,4},{11,8},{12,9},{13,10},{14,11},{15,12... | collective-permute-start | bytes 196616 | tf_op jit(solution)/shard_map/ppermute | solution.py:318
  22.0 2.8 %collective-permute-start.6 = (bf16[128,256]{1,0:T(8,128)(2,1)S(1)}, bf16[128,256]{1,0:T(8,128)(2,1)S(1)}, u32[]{:S(2)}, u32[]{:S(2)}) collective-permute-start(bf16[128,256]{1,0:T(8,128)(2,1)S(1)} %get-tuple-element.44), channel_id=1, source_target_pairs={{1,0},{2,1},{3,2},{4,3},{5,4},{6,5},{7,6},{9,8},{10,9},{11,10},{12... | collective-permute-start | bytes 196616 | tf_op jit(solution)/shard_map/ppermute | solution.py:318
  24.8 1.9 %collective-permute-start.7 = (bf16[128,256]{1,0:T(8,128)(2,1)S(1)}, bf16[128,256]{1,0:T(8,128)(2,1)S(1)}, u32[]{:S(2)}, u32[]{:S(2)}) collective-permute-start(bf16[128,256]{1,0:T(8,128)(2,1)S(1)} %get-tuple-element.45), channel_id=1, source_target_pairs={{2,0},{3,1},{4,2},{5,3},{6,4},{7,5},{10,8},{11,9},{12,10},{13,11},... | collective-permute-start | bytes 196616 | tf_op jit(solution)/shard_map/ppermute | solution.py:318
  26.8 1.5 %near.1 = (bf16[128,1024]{1,0:T(8,128)(2,1)}, bf16[128,1024]{1,0:T(8,128)(2,1)}, f32[128,256]{1,0:T(8,128)S(1)}) custom-call(bf16[1024,128]{1,0:T(8,128)(2,1)S(1)} %get-tuple-element.26.query_ref, bf16[1024,128]{1,0:T(8,128)(2,1)S(1)} %get-tuple-element.27.grad_ref, bf16[640,1024]{1,0:T(8,128)(2,1)S(1)} %get-tuple-element.35.weights_ref, ...), custom_call_target="tpu_custom_call" | custom-call | flops 335544320 | bytes 4657152 | tf_op jit(solution)/shard_map/near/pallas_call | solution.py:180
  28.2 0.0 collective-permute-done.4
  28.2 0.0 collective-permute-done.5
  28.2 0.0 collective-permute-done.6
  28.2 2.8 %collective-permute-done.7 = bf16[128,256]{1,0:T(8,128)(2,1)S(1)} collective-permute-done((bf16[128,256]{1,0:T(8,128)(2,1)S(1)}, bf16[128,256]{1,0:T(8,128)(2,1)S(1)}, u32[]{:S(2)}, u32[]{:S(2)}) %collective-permute-start.7) | collective-permute-done | bytes 65568 | tf_op jit(solution)/shard_map/ppermute | solution.py:318
  31.0 0.6 %fusion = (bf16[128,128]{1,0:T(8,128)(2,1)}, bf16[128,128]{1,0:T(8,128)(2,1)}) fusion(bf16[128,256]{1,0:T(8,128)(2,1)S(1)} %add_convert_fusion), kind=kLoop, calls=%fused_computation.1 | loop fusion | bytes 131072 | tf_op jit(solution)/shard_map/slice | solution.py:322
  (1 shorter events, 0.0 us)
Async XLA Ops:
  0.6 10.5 %copy-start.1 = (bf16[128,1024]{1,0:T(8,128)(2,1)S(1)}, bf16[128,1024]{1,0:T(8,128)(2,1)}, u32[]{:S(2)}) copy-start(bf16[128,1024]{1,0:T(8,128)(2,1)} %grad_ref.1) | copy-start | bytes 786436
  0.6 10.5 %copy-start = (bf16[128,1024]{1,0:T(8,128)(2,1)S(1)}, bf16[128,1024]{1,0:T(8,128)(2,1)}, u32[]{:S(2)}) copy-start(bf16[128,1024]{1,0:T(8,128)(2,1)} %query_ref.1) | copy-start | bytes 786436
  1.5 9.9 %collective-permute-start.3 = (bf16[128,256]{1,0:T(8,128)(2,1)S(1)}, bf16[128,256]{1,0:T(8,128)(2,1)S(1)}, u32[]{:S(2)}, u32[]{:S(2)}) collective-permute-start(bf16[128,256]{1,0:T(8,128)(2,1)S(1)} %get-tuple-element.31.refs_0_.refs_1_), channel_id=1, source_target_pairs={{0,3},{1,4},{2,5},{3,6},{4,7},{8,11},{9,12},{10,13},{11,14},{12,15... | collective-permute-start | bytes 196616 | tf_op jit(solution)/shard_map/ppermute | solution.py:230
  5.9 7.1 %collective-permute-start.2 = (bf16[128,256]{1,0:T(8,128)(2,1)S(1)}, bf16[128,256]{1,0:T(8,128)(2,1)S(1)}, u32[]{:S(2)}, u32[]{:S(2)}) collective-permute-start(bf16[128,256]{1,0:T(8,128)(2,1)S(1)} %get-tuple-element.31.refs_0_.refs_1_), channel_id=1, source_target_pairs={{0,4},{1,5},{2,6},{3,7},{8,12},{9,13},{10,14},{11,15},{16,20},{17,... | collective-permute-start | bytes 196616 | tf_op jit(solution)/shard_map/ppermute | solution.py:230
  7.2 7.9 %collective-permute-start.1 = (bf16[128,256]{1,0:T(8,128)(2,1)S(1)}, bf16[128,256]{1,0:T(8,128)(2,1)S(1)}, u32[]{:S(2)}, u32[]{:S(2)}) collective-permute-start(bf16[128,256]{1,0:T(8,128)(2,1)S(1)} %get-tuple-element.31.refs_0_.refs_1_), channel_id=1, source_target_pairs={{0,1},{1,2},{2,3},{3,4},{4,5},{5,6},{6,7},{8,9},{9,10},{10,11},{11... | collective-permute-start | bytes 196616 | tf_op jit(solution)/shard_map/ppermute | solution.py:230
  9.2 7.4 %collective-permute-start = (bf16[128,256]{1,0:T(8,128)(2,1)S(1)}, bf16[128,256]{1,0:T(8,128)(2,1)S(1)}, u32[]{:S(2)}, u32[]{:S(2)}) collective-permute-start(bf16[128,256]{1,0:T(8,128)(2,1)S(1)} %get-tuple-element.31.refs_0_.refs_1_), channel_id=1, source_target_pairs={{0,2},{1,3},{2,4},{3,5},{4,6},{5,7},{8,10},{9,11},{10,12},{11,13},... | collective-permute-start | bytes 196616 | tf_op jit(solution)/shard_map/ppermute | solution.py:230
  18.0 10.2 %collective-permute-start.4 = (bf16[128,256]{1,0:T(8,128)(2,1)S(1)}, bf16[128,256]{1,0:T(8,128)(2,1)S(1)}, u32[]{:S(2)}, u32[]{:S(2)}) collective-permute-start(bf16[128,256]{1,0:T(8,128)(2,1)S(1)} %get-tuple-element.42), channel_id=1, source_target_pairs={{4,0},{5,1},{6,2},{7,3},{12,8},{13,9},{14,10},{15,11},{20,16},{21,... | collective-permute-start | bytes 196616 | tf_op jit(solution)/shard_map/ppermute | solution.py:318
  19.8 8.4 %collective-permute-start.5 = (bf16[128,256]{1,0:T(8,128)(2,1)S(1)}, bf16[128,256]{1,0:T(8,128)(2,1)S(1)}, u32[]{:S(2)}, u32[]{:S(2)}) collective-permute-start(bf16[128,256]{1,0:T(8,128)(2,1)S(1)} %get-tuple-element.43), channel_id=1, source_target_pairs={{3,0},{4,1},{5,2},{6,3},{7,4},{11,8},{12,9},{13,10},{14,11},{15,12... | collective-permute-start | bytes 196616 | tf_op jit(solution)/shard_map/ppermute | solution.py:318
  22.0 6.2 %collective-permute-start.6 = (bf16[128,256]{1,0:T(8,128)(2,1)S(1)}, bf16[128,256]{1,0:T(8,128)(2,1)S(1)}, u32[]{:S(2)}, u32[]{:S(2)}) collective-permute-start(bf16[128,256]{1,0:T(8,128)(2,1)S(1)} %get-tuple-element.44), channel_id=1, source_target_pairs={{1,0},{2,1},{3,2},{4,3},{5,4},{6,5},{7,6},{9,8},{10,9},{11,10},{12... | collective-permute-start | bytes 196616 | tf_op jit(solution)/shard_map/ppermute | solution.py:318
  24.8 6.2 %collective-permute-start.7 = (bf16[128,256]{1,0:T(8,128)(2,1)S(1)}, bf16[128,256]{1,0:T(8,128)(2,1)S(1)}, u32[]{:S(2)}, u32[]{:S(2)}) collective-permute-start(bf16[128,256]{1,0:T(8,128)(2,1)S(1)} %get-tuple-element.45), channel_id=1, source_target_pairs={{2,0},{3,1},{4,2},{5,3},{6,4},{7,5},{10,8},{11,9},{12,10},{13,11},... | collective-permute-start | bytes 196616 | tf_op jit(solution)/shard_map/ppermute | solution.py:318
where the time goes:
time: 32 us; the launch traced here: 31.7 us
  starting transfers between devices  18.3 us (57%)
  waiting for transfers between devices  6.51 us (20%)
  Pallas kernels  5.41 us (17%)
  between operations  0.78 us (2%)
  local copies, waits for them, and re-layouts  0.64 us (2%)
    ppermute x4, starting transfers between devices, per_device(): lax.ppermute(kv, 'ulysses', [(d, d + back) for d in range(devices - back)])  9.55 us
    ppermute x4, starting transfers between devices, per_device(): lax.ppermute(terms, 'ulysses', [(d, d - back) for d in range(back, device...  8.74 us
    pallas_call x5, Pallas kernels, call(): pl.pallas_call(body, out_shape=[jax.ShapeDtypeStruct(shape, dtype) for sh...  5.41 us
    ppermute x4, waiting for transfers between devices, per_device(): lax.ppermute(kv, 'ulysses', [(d, d + back) for d in range(devices - back)])  3.74 us
    ppermute x4, waiting for transfers between devices, per_device(): lax.ppermute(terms, 'ulysses', [(d, d - back) for d in range(back, device...  2.76 us
  transfers between devices with their start and end apart: 8, of which 3 were waited for; matrix products, arithmetic and copies ran while one was open for 0% of the time, Pallas kernels for 10%

commit v1 on v0

--- a/solution.py
+++ b/solution.py
@@ -12,7 +12,7 @@
 PAIR = 2
 masked_score = -1e30
 IN_ORDER = (0, 2, 1, 4, 3)
-OUT_ORDER = (0, 4, 3, 1, 2)
+OUT_ORDER = (0, 4, 3, 2, 1)
 score_scale = 1.0 / math.sqrt(HD)
 exponent_scale = score_scale * math.log2(math.e)
 
@@ -89,20 +89,26 @@
     return [slice(start, start + width) for start in range(0, columns, width)]
 
 
-def biased_keys(kv_refs, bias_ref, places):
-    tokens = kv_refs[0].shape[0]
-    keys = jnp.concatenate([ref[:, :HD] for ref in kv_refs], axis=0)
+def joined(early, kv_refs):
+    *kv_blocks, more = [ref[...] for ref in kv_refs]
+    kv_blocks[early.index(1)] += more
+    return kv_blocks
+
+
+def biased_keys(kv_blocks, bias_ref, places):
+    tokens = kv_blocks[0].shape[0]
+    keys = jnp.concatenate([rows[:, :HD] for rows in kv_blocks], axis=0)
     bias = jnp.concatenate([bias_ref[block(back, tokens), :] for back in places], axis=0)
     return jnp.concatenate([keys, bias], axis=1)
 
 
 def early_kernel(early, query_t_ref, grad_t_ref, bias_ref, *refs):
-    kv_refs = refs[: len(early)]
-    weights_ref, grad_weights_ref, stats_ref, out_t_ref, scores_ref = refs[len(early) :]
-    tokens = kv_refs[0].shape[0]
+    *kv_refs, weights_ref, grad_weights_ref, stats_ref, out_t_ref, scores_ref = refs
+    kv_blocks = joined(early, kv_refs)
+    tokens = kv_blocks[0].shape[0]
     columns = parts(query_t_ref.shape[1], tokens)
-    keys = biased_keys(kv_refs, bias_ref, early)
-    values = jnp.concatenate([ref[:, HD:] for ref in kv_refs], axis=0)
+    keys = biased_keys(kv_blocks, bias_ref, early)
+    values = jnp.concatenate([rows[:, HD:] for rows in kv_blocks], axis=0)
     values_t = values.T
     for part in columns:
         scores_ref[:, part] = dot(keys, query_t_ref[:, part])
@@ -125,7 +131,7 @@
     columns = parts(query_t_ref.shape[1], tokens)
     early_rows = slice(0, len(early) * tokens)
     late_rows = block(len(early), tokens)
-    keys = biased_keys([late_kv_ref], bias_ref, [late])
+    keys = biased_keys([late_kv_ref[...]], bias_ref, [late])
     values = late_kv_ref[:, HD:]
     scores = [dot(keys, query_t_ref[:, part]) for part in columns]
     grad_weights = [dot(values, grad_t_ref[:, part]) for part in columns]
@@ -154,15 +160,16 @@
         ref[...] = terms[block(place, tokens)]
 
 
-def near_kernel(query_ref, grad_ref, weights_ref, scores_grad_ref, rescale_ref, *refs):
-    early_out_t_ref, *kv_refs, out_ref, query_grad_ref, near_ref = refs
-    tokens = kv_refs[0].shape[0]
-    late_out_t = dot(kv_refs[-1][:, HD:].T, weights_ref[-tokens:, :])
+def near_kernel(early, query_ref, grad_ref, weights_ref, scores_grad_ref, rescale_ref, *refs):
+    early_out_t_ref, late_kv_ref, *kv_refs, out_ref, query_grad_ref, near_ref = refs
+    tokens = late_kv_ref.shape[0]
+    late_out_t = dot(late_kv_ref[:, HD:].T, weights_ref[-tokens:, :])
     out_t = (early_out_t_ref[...] * rescale_ref[...] + late_out_t).astype(jnp.bfloat16)
     near_ref[...] = gradient_terms(
         weights_ref[:tokens, :], scores_grad_ref[:tokens, :], query_ref[...], grad_ref[...]
     )
-    keys_t = jnp.concatenate([ref[:, :HD] for ref in kv_refs], axis=0).T
+    kv_blocks = joined(early, kv_refs) + [late_kv_ref[...]]
+    keys_t = jnp.concatenate([rows[:, :HD] for rows in kv_blocks], axis=0).T
     query_grad_t = (dot(keys_t, scores_grad_ref[...]) * score_scale).astype(jnp.bfloat16)
     for head in range(out_ref.shape[1] // HD):
         own = block(head, tokens)
@@ -225,11 +232,13 @@
         value_rows,
         fetched=True,
     )
+    def forward(back, first, last):
+        return lax.ppermute(kv, "ulysses", [(d - back, d) for d in range(max(first, back), last)])
+
+    previous = [forward(1, reach + 1, devices), forward(1, 0, reach + 1)]
     kv_blocks = {0: kv}
     for back in ordered(list(range(blocks)), IN_ORDER)[1:]:
-        kv_blocks[back] = lax.ppermute(
-            kv, "ulysses", [(d, d + back) for d in range(devices - back)]
-        )
+        kv_blocks[back] = previous[0] if back == 1 else forward(back, 0, devices)
     late = list(kv_blocks)[1]
     early = [0] + [back for back in kv_blocks if back not in (0, late)]
     places = early + [late]
@@ -239,7 +248,13 @@
     for shared in range(shared_heads):
         own_queries = query_rows[:, block(shared, group_width)]
         own_grads = grad_out[:, block(shared, group_width)]
-        own_kv = [kv_blocks[back][:, block(shared, 2 * HD)] for back in places]
+        if attention:
+            own_queries, attention[-1] = lax.optimization_barrier((own_queries, attention[-1]))
+        own_kv = [
+            rows[:, block(shared, 2 * HD)]
+            for rows in [kv_blocks[back] for back in places] + previous[1:]
+        ]
+        early_kv = own_kv[:-2] + own_kv[-1:]
         queries, grads, queries_t, grads_t, bias = call(
             functools.partial(prepare_kernel, reach),
             "prepare",
@@ -270,7 +285,7 @@
             queries_t,
             grads_t,
             bias,
-            *own_kv[:-1],
+            *early_kv,
         )
         weights, scores_grad, rescale, *own_far = call(
             functools.partial(late_kernel, early, late),
@@ -284,13 +299,13 @@
             queries_t,
             grads_t,
             bias,
-            own_kv[-1],
+            own_kv[-2],
             weights,
             grad_weights,
             stats,
         )
         own_out, own_query_grad, own_total = call(
-            near_kernel,
+            functools.partial(near_kernel, early),
             "near",
             [((tokens, group_width), low)] * 2 + [((tokens, 2 * HD), jnp.float32)],
             [],
@@ -301,7 +316,8 @@
             scores_grad,
             rescale,
             early_out_t,
-            *own_kv,
+            own_kv[-2],
+            *early_kv,
         )
         attention.append(own_out)
         grad_queries.append(own_query_grad)

time: 32 us -> 30.8 us (0.963)
  the two profiles are of different devices: /device:TPU:20 before, /device:TPU:18 now
where the time goes in v1:
time: 30.8 us; the launch traced here: 30.5 us
  starting transfers between devices  17.3 us (56%)
  waiting for transfers between devices  6.24 us (20%)
  Pallas kernels  5.46 us (18%)
  between operations  0.78 us (3%)
  local copies, waits for them, and re-layouts  0.64 us (2%)
    ppermute x4, starting transfers between devices, per_device(): lax.ppermute(terms, 'ulysses', [(d, d - back) for d in range(back, device...  8.7 us
    ppermute x5, starting transfers between devices, forward(): lax.ppermute(kv, 'ulysses', [(d - back, d) for d in range(max(first, back...  8.63 us
    pallas_call x5, Pallas kernels, call(): pl.pallas_call(body, out_shape=[jax.ShapeDtypeStruct(shape, dtype) for sh...  5.46 us
    ppermute x4, waiting for transfers between devices, per_device(): lax.ppermute(terms, 'ulysses', [(d, d - back) for d in range(back, device...  3.39 us
    ppermute x5, waiting for transfers between devices, forward(): lax.ppermute(kv, 'ulysses', [(d - back, d) for d in range(max(first, back...  2.85 us
    slice x1, local copies, waits for them, and re-layouts, per_device(): total[:, block(2 * g + 1, HD)]  0.63 us
  transfers between devices with their start and end apart: 9, of which 5 were waited for; matrix products, arithmetic and copies ran while one was open for 0% of the time, Pallas kernels for 10%

profile of v1, /device:TPU:18, one launch (start us, length us, event | category | flops | bytes accessed | tf_op | source)
XLA Modules:
  0.0 30.5 jit_solution(7184075035864404392)
XLA Ops:
  0.6 0.0 copy-start.1
  0.6 0.0 copy-start
  0.7 0.9 %fetch.1 = (bf16[128,256]{1,0:T(8,128)(2,1)S(1)}, s32[1,128]{1,0:T(1,128)S(1)}) custom-call(s32[4,12]{1,0:T(4,128)} %doc_hbm.1, bf16[128,128]{1,0:T(8,128)(2,1)} %key_hbm.1, bf16[128,128]{1,0:T(8,128)(2,1)} %value_hbm.1), custom_call_target="tpu_custom_call" | custom-call | flops 2684354560 | bytes 131980 | tf_op jit(solution)/shard_map/fetch/pallas_call | solution.py:187
  1.5 0.7 %collective-permute-start.4 = (bf16[128,256]{1,0:T(8,128)(2,1)S(1)}, bf16[128,256]{1,0:T(8,128)(2,1)S(1)}, u32[]{:S(2)}, u32[]{:S(2)}) collective-permute-start(bf16[128,256]{1,0:T(8,128)(2,1)S(1)} %get-tuple-element.31.refs_0_.refs_2_), channel_id=1, source_target_pairs={{0,1},{1,2},{2,3},{3,4},{8,9},{9,10},{10,11},{11,12},{16,17},{17,1... | collective-permute-start | bytes 196616 | tf_op jit(solution)/shard_map/ppermute | solution.py:236
  2.2 1.3 %collective-permute-start.3 = (bf16[128,256]{1,0:T(8,128)(2,1)S(1)}, bf16[128,256]{1,0:T(8,128)(2,1)S(1)}, u32[]{:S(2)}, u32[]{:S(2)}) collective-permute-start(bf16[128,256]{1,0:T(8,128)(2,1)S(1)} %get-tuple-element.31.refs_0_.refs_2_), channel_id=1, source_target_pairs={{0,3},{1,4},{2,5},{3,6},{4,7},{8,11},{9,12},{10,13},{11,14},{12,15... | collective-permute-start | bytes 196616 | tf_op jit(solution)/shard_map/ppermute | solution.py:236
  3.5 1.3 %collective-permute-start.2 = (bf16[128,256]{1,0:T(8,128)(2,1)S(1)}, bf16[128,256]{1,0:T(8,128)(2,1)S(1)}, u32[]{:S(2)}, u32[]{:S(2)}) collective-permute-start(bf16[128,256]{1,0:T(8,128)(2,1)S(1)} %get-tuple-element.31.refs_0_.refs_2_), channel_id=1, source_target_pairs={{0,4},{1,5},{2,6},{3,7},{8,12},{9,13},{10,14},{11,15},{16,20},{17,... | collective-permute-start | bytes 196616 | tf_op jit(solution)/shard_map/ppermute | solution.py:236
  4.8 3.5 %collective-permute-start.1 = (bf16[128,256]{1,0:T(8,128)(2,1)S(1)}, bf16[128,256]{1,0:T(8,128)(2,1)S(1)}, u32[]{:S(2)}, u32[]{:S(2)}) collective-permute-start(bf16[128,256]{1,0:T(8,128)(2,1)S(1)} %get-tuple-element.31.refs_0_.refs_2_), channel_id=1, source_target_pairs={{4,5},{5,6},{6,7},{12,13},{13,14},{14,15},{20,21},{21,22},{22,23},... | collective-permute-start | bytes 196616 | tf_op jit(solution)/shard_map/ppermute | solution.py:236
  8.3 1.9 %collective-permute-start = (bf16[128,256]{1,0:T(8,128)(2,1)S(1)}, bf16[128,256]{1,0:T(8,128)(2,1)S(1)}, u32[]{:S(2)}, u32[]{:S(2)}) collective-permute-start(bf16[128,256]{1,0:T(8,128)(2,1)S(1)} %get-tuple-element.31.refs_0_.refs_2_), channel_id=1, source_target_pairs={{0,2},{1,3},{2,4},{3,5},{4,6},{5,7},{8,10},{9,11},{10,12},{11,13},... | collective-permute-start | bytes 196616 | tf_op jit(solution)/shard_map/ppermute | solution.py:236
  10.2 0.0 copy-done.1
  10.2 0.0 copy-done
  10.2 0.3 prepare.1
  10.5 0.0 collective-permute-done.4.refs_4_.refs_6_
  10.5 0.0 collective-permute-done.3.refs_3_.refs_5_
  10.5 0.7 %collective-permute-done.2.refs_2_.refs_4_ = bf16[128,256]{1,0:T(8,128)(2,1)S(1)} collective-permute-done((bf16[128,256]{1,0:T(8,128)(2,1)S(1)}, bf16[128,256]{1,0:T(8,128)(2,1)S(1)}, u32[]{:S(2)}, u32[]{:S(2)}) %collective-permute-start.2) | collective-permute-done | bytes 65568 | tf_op jit(solution)/shard_map/ppermute | solution.py:236
  11.3 0.7 %collective-permute-done.1.refs_1_.refs_3_ = bf16[128,256]{1,0:T(8,128)(2,1)S(1)} collective-permute-done((bf16[128,256]{1,0:T(8,128)(2,1)S(1)}, bf16[128,256]{1,0:T(8,128)(2,1)S(1)}, u32[]{:S(2)}, u32[]{:S(2)}) %collective-permute-start.1) | collective-permute-done | bytes 65568 | tf_op jit(solution)/shard_map/ppermute | solution.py:236
  12.0 1.4 %early.1 = (bf16[512,1024]{1,0:T(8,128)(2,1)S(1)}, f32[512,1024]{1,0:T(8,128)S(1)}, f32[3,1024]{1,0:T(4,128)S(1)}, f32[128,1024]{1,0:T(8,128)S(1)}) custom-call(bf16[256,1024]{1,0:T(8,128)(2,1)S(1)} %get-tuple-element.28.query_t_ref, bf16[128,1024]{1,0:T(8,128)(2,1)S(1)} %get-tuple-element.29.grad_t_ref, bf16[640,128]{1,0:T(8,128)(2,1)S(1)} %get-tuple-element.30.bias_ref, ...), custom_call_target="tpu_custom_call" | custom-call | flops 503316480 | bytes 7057408 | tf_op jit(solution)/shard_map/early/pallas_call | solution.py:187
  13.4 1.4 %collective-permute-done.refs_0_.refs_1_ = bf16[128,256]{1,0:T(8,128)(2,1)S(1)} collective-permute-done((bf16[128,256]{1,0:T(8,128)(2,1)S(1)}, bf16[128,256]{1,0:T(8,128)(2,1)S(1)}, u32[]{:S(2)}, u32[]{:S(2)}) %collective-permute-start) | collective-permute-done | bytes 65568 | tf_op jit(solution)/shard_map/ppermute | solution.py:236
  14.8 1.4 %late.1 = (bf16[640,1024]{1,0:T(8,128)(2,1)S(1)}, bf16[640,1024]{1,0:T(8,128)(2,1)S(1)}, f32[1,1024]{1,0:T(1,128)S(1)}, bf16[128,256]{1,0:T(8,128)(2,1)S(1)}, bf...) custom-call(bf16[1024,128]{1,0:T(8,128)(2,1)S(1)} %get-tuple-element.26.query_ref, ...), custom_call_target="tpu_custom_call" | custom-call | flops 335544320 | bytes 7585792 | tf_op jit(solution)/shard_map/late/pallas_call | solution.py:187
  16.2 1.7 %collective-permute-start.5 = (bf16[128,256]{1,0:T(8,128)(2,1)S(1)}, bf16[128,256]{1,0:T(8,128)(2,1)S(1)}, u32[]{:S(2)}, u32[]{:S(2)}) collective-permute-start(bf16[128,256]{1,0:T(8,128)(2,1)S(1)} %get-tuple-element.42), channel_id=1, source_target_pairs={{4,0},{5,1},{6,2},{7,3},{12,8},{13,9},{14,10},{15,11},{20,16},{21,... | collective-permute-start | bytes 196616 | tf_op jit(solution)/shard_map/ppermute | solution.py:334
  17.9 2.9 %collective-permute-start.6 = (bf16[128,256]{1,0:T(8,128)(2,1)S(1)}, bf16[128,256]{1,0:T(8,128)(2,1)S(1)}, u32[]{:S(2)}, u32[]{:S(2)}) collective-permute-start(bf16[128,256]{1,0:T(8,128)(2,1)S(1)} %get-tuple-element.43), channel_id=1, source_target_pairs={{3,0},{4,1},{5,2},{6,3},{7,4},{11,8},{12,9},{13,10},{14,11},{15,12... | collective-permute-start | bytes 196616 | tf_op jit(solution)/shard_map/ppermute | solution.py:334
  20.8 1.9 %collective-permute-start.7 = (bf16[128,256]{1,0:T(8,128)(2,1)S(1)}, bf16[128,256]{1,0:T(8,128)(2,1)S(1)}, u32[]{:S(2)}, u32[]{:S(2)}) collective-permute-start(bf16[128,256]{1,0:T(8,128)(2,1)S(1)} %get-tuple-element.44), channel_id=1, source_target_pairs={{2,0},{3,1},{4,2},{5,3},{6,4},{7,5},{10,8},{11,9},{12,10},{13,11},... | collective-permute-start | bytes 196616 | tf_op jit(solution)/shard_map/ppermute | solution.py:334
  22.8 2.2 %collective-permute-start.8 = (bf16[128,256]{1,0:T(8,128)(2,1)S(1)}, bf16[128,256]{1,0:T(8,128)(2,1)S(1)}, u32[]{:S(2)}, u32[]{:S(2)}) collective-permute-start(bf16[128,256]{1,0:T(8,128)(2,1)S(1)} %get-tuple-element.45), channel_id=1, source_target_pairs={{1,0},{2,1},{3,2},{4,3},{5,4},{6,5},{7,6},{9,8},{10,9},{11,10},{12... | collective-permute-start | bytes 196616 | tf_op jit(solution)/shard_map/ppermute | solution.py:334
  25.0 1.5 %near.1 = (bf16[128,1024]{1,0:T(8,128)(2,1)}, bf16[128,1024]{1,0:T(8,128)(2,1)}, f32[128,256]{1,0:T(8,128)S(1)}) custom-call(bf16[1024,128]{1,0:T(8,128)(2,1)S(1)} %get-tuple-element.26.query_ref, bf16[1024,128]{1,0:T(8,128)(2,1)S(1)} %get-tuple-element.27.grad_ref, bf16[640,1024]{1,0:T(8,128)(2,1)S(1)} %get-tuple-element.35.weights_ref, ...), custom_call_target="tpu_custom_call" | custom-call | flops 335544320 | bytes 4722688 | tf_op jit(solution)/shard_map/near/pallas_call | solution.py:187
  26.4 0.0 collective-permute-done.5
  26.4 0.0 collective-permute-done.6
  26.4 0.6 %collective-permute-done.7 = bf16[128,256]{1,0:T(8,128)(2,1)S(1)} collective-permute-done((bf16[128,256]{1,0:T(8,128)(2,1)S(1)}, bf16[128,256]{1,0:T(8,128)(2,1)S(1)}, u32[]{:S(2)}, u32[]{:S(2)}) %collective-permute-start.7) | collective-permute-done | bytes 65568 | tf_op jit(solution)/shard_map/ppermute | solution.py:334
  27.0 2.8 %collective-permute-done.8 = bf16[128,256]{1,0:T(8,128)(2,1)S(1)} collective-permute-done((bf16[128,256]{1,0:T(8,128)(2,1)S(1)}, bf16[128,256]{1,0:T(8,128)(2,1)S(1)}, u32[]{:S(2)}, u32[]{:S(2)}) %collective-permute-start.8) | collective-permute-done | bytes 65568 | tf_op jit(solution)/shard_map/ppermute | solution.py:334
  29.9 0.6 %fusion = (bf16[128,128]{1,0:T(8,128)(2,1)}, bf16[128,128]{1,0:T(8,128)(2,1)}) fusion(bf16[128,256]{1,0:T(8,128)(2,1)S(1)} %add_convert_fusion), kind=kLoop, calls=%fused_computation.1 | loop fusion | bytes 131072 | tf_op jit(solution)/shard_map/slice | solution.py:338
  (1 shorter events, 0.0 us)
Async XLA Ops:
  0.6 9.6 %copy-start.1 = (bf16[128,1024]{1,0:T(8,128)(2,1)S(1)}, bf16[128,1024]{1,0:T(8,128)(2,1)}, u32[]{:S(2)}) copy-start(bf16[128,1024]{1,0:T(8,128)(2,1)} %grad_ref.1) | copy-start | bytes 786436
  0.6 9.6 %copy-start = (bf16[128,1024]{1,0:T(8,128)(2,1)S(1)}, bf16[128,1024]{1,0:T(8,128)(2,1)}, u32[]{:S(2)}) copy-start(bf16[128,1024]{1,0:T(8,128)(2,1)} %query_ref.1) | copy-start | bytes 786436
  1.5 9.0 %collective-permute-start.4 = (bf16[128,256]{1,0:T(8,128)(2,1)S(1)}, bf16[128,256]{1,0:T(8,128)(2,1)S(1)}, u32[]{:S(2)}, u32[]{:S(2)}) collective-permute-start(bf16[128,256]{1,0:T(8,128)(2,1)S(1)} %get-tuple-element.31.refs_0_.refs_2_), channel_id=1, source_target_pairs={{0,1},{1,2},{2,3},{3,4},{8,9},{9,10},{10,11},{11,12},{16,17},{17,1... | collective-permute-start | bytes 196616 | tf_op jit(solution)/shard_map/ppermute | solution.py:236
  2.2 8.3 %collective-permute-start.3 = (bf16[128,256]{1,0:T(8,128)(2,1)S(1)}, bf16[128,256]{1,0:T(8,128)(2,1)S(1)}, u32[]{:S(2)}, u32[]{:S(2)}) collective-permute-start(bf16[128,256]{1,0:T(8,128)(2,1)S(1)} %get-tuple-element.31.refs_0_.refs_2_), channel_id=1, source_target_pairs={{0,3},{1,4},{2,5},{3,6},{4,7},{8,11},{9,12},{10,13},{11,14},{12,15... | collective-permute-start | bytes 196616 | tf_op jit(solution)/shard_map/ppermute | solution.py:236
  3.5 7.8 %collective-permute-start.2 = (bf16[128,256]{1,0:T(8,128)(2,1)S(1)}, bf16[128,256]{1,0:T(8,128)(2,1)S(1)}, u32[]{:S(2)}, u32[]{:S(2)}) collective-permute-start(bf16[128,256]{1,0:T(8,128)(2,1)S(1)} %get-tuple-element.31.refs_0_.refs_2_), channel_id=1, source_target_pairs={{0,4},{1,5},{2,6},{3,7},{8,12},{9,13},{10,14},{11,15},{16,20},{17,... | collective-permute-start | bytes 196616 | tf_op jit(solution)/shard_map/ppermute | solution.py:236
  4.8 7.2 %collective-permute-start.1 = (bf16[128,256]{1,0:T(8,128)(2,1)S(1)}, bf16[128,256]{1,0:T(8,128)(2,1)S(1)}, u32[]{:S(2)}, u32[]{:S(2)}) collective-permute-start(bf16[128,256]{1,0:T(8,128)(2,1)S(1)} %get-tuple-element.31.refs_0_.refs_2_), channel_id=1, source_target_pairs={{4,5},{5,6},{6,7},{12,13},{13,14},{14,15},{20,21},{21,22},{22,23},... | collective-permute-start | bytes 196616 | tf_op jit(solution)/shard_map/ppermute | solution.py:236
  8.3 6.6 %collective-permute-start = (bf16[128,256]{1,0:T(8,128)(2,1)S(1)}, bf16[128,256]{1,0:T(8,128)(2,1)S(1)}, u32[]{:S(2)}, u32[]{:S(2)}) collective-permute-start(bf16[128,256]{1,0:T(8,128)(2,1)S(1)} %get-tuple-element.31.refs_0_.refs_2_), channel_id=1, source_target_pairs={{0,2},{1,3},{2,4},{3,5},{4,6},{5,7},{8,10},{9,11},{10,12},{11,13},... | collective-permute-start | bytes 196616 | tf_op jit(solution)/shard_map/ppermute | solution.py:236
  16.2 10.2 %collective-permute-start.5 = (bf16[128,256]{1,0:T(8,128)(2,1)S(1)}, bf16[128,256]{1,0:T(8,128)(2,1)S(1)}, u32[]{:S(2)}, u32[]{:S(2)}) collective-permute-start(bf16[128,256]{1,0:T(8,128)(2,1)S(1)} %get-tuple-element.42), channel_id=1, source_target_pairs={{4,0},{5,1},{6,2},{7,3},{12,8},{13,9},{14,10},{15,11},{20,16},{21,... | collective-permute-start | bytes 196616 | tf_op jit(solution)/shard_map/ppermute | solution.py:334
  17.9 8.5 %collective-permute-start.6 = (bf16[128,256]{1,0:T(8,128)(2,1)S(1)}, bf16[128,256]{1,0:T(8,128)(2,1)S(1)}, u32[]{:S(2)}, u32[]{:S(2)}) collective-permute-start(bf16[128,256]{1,0:T(8,128)(2,1)S(1)} %get-tuple-element.43), channel_id=1, source_target_pairs={{3,0},{4,1},{5,2},{6,3},{7,4},{11,8},{12,9},{13,10},{14,11},{15,12... | collective-permute-start | bytes 196616 | tf_op jit(solution)/shard_map/ppermute | solution.py:334
  20.8 6.2 %collective-permute-start.7 = (bf16[128,256]{1,0:T(8,128)(2,1)S(1)}, bf16[128,256]{1,0:T(8,128)(2,1)S(1)}, u32[]{:S(2)}, u32[]{:S(2)}) collective-permute-start(bf16[128,256]{1,0:T(8,128)(2,1)S(1)} %get-tuple-element.44), channel_id=1, source_target_pairs={{2,0},{3,1},{4,2},{5,3},{6,4},{7,5},{10,8},{11,9},{12,10},{13,11},... | collective-permute-start | bytes 196616 | tf_op jit(solution)/shard_map/ppermute | solution.py:334
  22.8 7.1 %collective-permute-start.8 = (bf16[128,256]{1,0:T(8,128)(2,1)S(1)}, bf16[128,256]{1,0:T(8,128)(2,1)S(1)}, u32[]{:S(2)}, u32[]{:S(2)}) collective-permute-start(bf16[128,256]{1,0:T(8,128)(2,1)S(1)} %get-tuple-element.45), channel_id=1, source_target_pairs={{1,0},{2,1},{3,2},{4,3},{5,4},{6,5},{7,6},{9,8},{10,9},{11,10},{12... | collective-permute-start | bytes 196616 | tf_op jit(solution)/shard_map/ppermute | solution.py:334

commit v2 on v1

--- a/solution.py
+++ b/solution.py
@@ -135,6 +135,7 @@
     values = late_kv_ref[:, HD:]
     scores = [dot(keys, query_t_ref[:, part]) for part in columns]
     grad_weights = [dot(values, grad_t_ref[:, part]) for part in columns]
+    key_terms = value_terms = jnp.zeros((len(early) * tokens, HD), jnp.float32)
     for part, own, own_grad in zip(columns, scores, grad_weights):
         early_top = stats_ref[0:1, part]
         top = jnp.maximum(early_top, jnp.max(own, axis=0, keepdims=True) * exponent_scale)
@@ -153,11 +154,13 @@
         scores_grad_ref[early_rows, part] = (
             own * (grad_weights_ref[:, part] - row_dots)
         ).astype(jnp.bfloat16)
-    terms = gradient_terms(
-        weights_ref[tokens:, :], scores_grad_ref[tokens:, :], query_ref[...], grad_ref[...]
-    ).astype(jnp.bfloat16)
+        key_terms += dot(scores_grad_ref[tokens:, part], query_ref[part, :])
+        value_terms += dot(weights_ref[tokens:, part], grad_ref[part, :])
+    key_terms = (key_terms * score_scale).astype(jnp.bfloat16)
+    value_terms = value_terms.astype(jnp.bfloat16)
     for place, ref in enumerate(term_refs):
-        ref[...] = terms[block(place, tokens)]
+        ref[:, :HD] = key_terms[block(place, tokens)]
+        ref[:, HD:] = value_terms[block(place, tokens)]
 
 
 def near_kernel(early, query_ref, grad_ref, weights_ref, scores_grad_ref, rescale_ref, *refs):

time: 30.8 us -> 30.7 us (level)
  no operation moved by 1% of the time
where the time goes in v2:
time: 30.7 us; the launch traced here: 30.4 us
  starting transfers between devices  17.3 us (56%)
  waiting for transfers between devices  6.24 us (20%)
  Pallas kernels  5.38 us (18%)
  between operations  0.78 us (3%)
  local copies, waits for them, and re-layouts  0.64 us (2%)
    ppermute x4, starting transfers between devices, per_device(): lax.ppermute(terms, 'ulysses', [(d, d - back) for d in range(back, device...  8.69 us
    ppermute x5, starting transfers between devices, forward(): lax.ppermute(kv, 'ulysses', [(d - back, d) for d in range(max(first, back...  8.63 us
    pallas_call x5, Pallas kernels, call(): pl.pallas_call(body, out_shape=[jax.ShapeDtypeStruct(shape, dtype) for sh...  5.38 us
    ppermute x4, waiting for transfers between devices, per_device(): lax.ppermute(terms, 'ulysses', [(d, d - back) for d in range(back, device...  3.39 us
    ppermute x5, waiting for transfers between devices, forward(): lax.ppermute(kv, 'ulysses', [(d - back, d) for d in range(max(first, back...  2.85 us
    slice x1, local copies, waits for them, and re-layouts, per_device(): total[:, block(2 * g + 1, HD)]  0.63 us
  transfers between devices with their start and end apart: 9, of which 5 were waited for; matrix products, arithmetic and copies ran while one was open for 0% of the time, Pallas kernels for 10%

profile of v2, /device:TPU:18, one launch (start us, length us, event | category | flops | bytes accessed | tf_op | source)
XLA Modules:
  0.0 30.4 jit_solution(12533799700095048010)
XLA Ops:
  0.6 0.0 copy-start.1
  0.6 0.0 copy-start
  0.7 0.9 %fetch.1 = (bf16[128,256]{1,0:T(8,128)(2,1)S(1)}, s32[1,128]{1,0:T(1,128)S(1)}) custom-call(s32[4,12]{1,0:T(4,128)} %doc_hbm.1, bf16[128,128]{1,0:T(8,128)(2,1)} %key_hbm.1, bf16[128,128]{1,0:T(8,128)(2,1)} %value_hbm.1), custom_call_target="tpu_custom_call" | custom-call | flops 2684354560 | bytes 131980 | tf_op jit(solution)/shard_map/fetch/pallas_call | solution.py:190
  1.5 0.7 %collective-permute-start.4 = (bf16[128,256]{1,0:T(8,128)(2,1)S(1)}, bf16[128,256]{1,0:T(8,128)(2,1)S(1)}, u32[]{:S(2)}, u32[]{:S(2)}) collective-permute-start(bf16[128,256]{1,0:T(8,128)(2,1)S(1)} %get-tuple-element.31.refs_0_.refs_2_), channel_id=1, source_target_pairs={{0,1},{1,2},{2,3},{3,4},{8,9},{9,10},{10,11},{11,12},{16,17},{17,1... | collective-permute-start | bytes 196616 | tf_op jit(solution)/shard_map/ppermute | solution.py:239
  2.2 1.3 %collective-permute-start.3 = (bf16[128,256]{1,0:T(8,128)(2,1)S(1)}, bf16[128,256]{1,0:T(8,128)(2,1)S(1)}, u32[]{:S(2)}, u32[]{:S(2)}) collective-permute-start(bf16[128,256]{1,0:T(8,128)(2,1)S(1)} %get-tuple-element.31.refs_0_.refs_2_), channel_id=1, source_target_pairs={{0,3},{1,4},{2,5},{3,6},{4,7},{8,11},{9,12},{10,13},{11,14},{12,15... | collective-permute-start | bytes 196616 | tf_op jit(solution)/shard_map/ppermute | solution.py:239
  3.5 1.3 %collective-permute-start.2 = (bf16[128,256]{1,0:T(8,128)(2,1)S(1)}, bf16[128,256]{1,0:T(8,128)(2,1)S(1)}, u32[]{:S(2)}, u32[]{:S(2)}) collective-permute-start(bf16[128,256]{1,0:T(8,128)(2,1)S(1)} %get-tuple-element.31.refs_0_.refs_2_), channel_id=1, source_target_pairs={{0,4},{1,5},{2,6},{3,7},{8,12},{9,13},{10,14},{11,15},{16,20},{17,... | collective-permute-start | bytes 196616 | tf_op jit(solution)/shard_map/ppermute | solution.py:239
  4.8 3.5 %collective-permute-start.1 = (bf16[128,256]{1,0:T(8,128)(2,1)S(1)}, bf16[128,256]{1,0:T(8,128)(2,1)S(1)}, u32[]{:S(2)}, u32[]{:S(2)}) collective-permute-start(bf16[128,256]{1,0:T(8,128)(2,1)S(1)} %get-tuple-element.31.refs_0_.refs_2_), channel_id=1, source_target_pairs={{4,5},{5,6},{6,7},{12,13},{13,14},{14,15},{20,21},{21,22},{22,23},... | collective-permute-start | bytes 196616 | tf_op jit(solution)/shard_map/ppermute | solution.py:239
  8.3 1.9 %collective-permute-start = (bf16[128,256]{1,0:T(8,128)(2,1)S(1)}, bf16[128,256]{1,0:T(8,128)(2,1)S(1)}, u32[]{:S(2)}, u32[]{:S(2)}) collective-permute-start(bf16[128,256]{1,0:T(8,128)(2,1)S(1)} %get-tuple-element.31.refs_0_.refs_2_), channel_id=1, source_target_pairs={{0,2},{1,3},{2,4},{3,5},{4,6},{5,7},{8,10},{9,11},{10,12},{11,13},... | collective-permute-start | bytes 196616 | tf_op jit(solution)/shard_map/ppermute | solution.py:239
  10.2 0.0 copy-done.1
  10.2 0.0 copy-done
  10.2 0.3 prepare.1
  10.5 0.0 collective-permute-done.4.refs_4_.refs_6_
  10.5 0.0 collective-permute-done.3.refs_3_.refs_5_
  10.5 0.7 %collective-permute-done.2.refs_2_.refs_4_ = bf16[128,256]{1,0:T(8,128)(2,1)S(1)} collective-permute-done((bf16[128,256]{1,0:T(8,128)(2,1)S(1)}, bf16[128,256]{1,0:T(8,128)(2,1)S(1)}, u32[]{:S(2)}, u32[]{:S(2)}) %collective-permute-start.2) | collective-permute-done | bytes 65568 | tf_op jit(solution)/shard_map/ppermute | solution.py:239
  11.3 0.7 %collective-permute-done.1.refs_1_.refs_3_ = bf16[128,256]{1,0:T(8,128)(2,1)S(1)} collective-permute-done((bf16[128,256]{1,0:T(8,128)(2,1)S(1)}, bf16[128,256]{1,0:T(8,128)(2,1)S(1)}, u32[]{:S(2)}, u32[]{:S(2)}) %collective-permute-start.1) | collective-permute-done | bytes 65568 | tf_op jit(solution)/shard_map/ppermute | solution.py:239
  12.0 1.4 %early.1 = (bf16[512,1024]{1,0:T(8,128)(2,1)S(1)}, f32[512,1024]{1,0:T(8,128)S(1)}, f32[3,1024]{1,0:T(4,128)S(1)}, f32[128,1024]{1,0:T(8,128)S(1)}) custom-call(bf16[256,1024]{1,0:T(8,128)(2,1)S(1)} %get-tuple-element.28.query_t_ref, bf16[128,1024]{1,0:T(8,128)(2,1)S(1)} %get-tuple-element.29.grad_t_ref, bf16[640,128]{1,0:T(8,128)(2,1)S(1)} %get-tuple-element.30.bias_ref, ...), custom_call_target="tpu_custom_call" | custom-call | flops 503316480 | bytes 7057408 | tf_op jit(solution)/shard_map/early/pallas_call | solution.py:190
  13.4 1.4 %collective-permute-done.refs_0_.refs_1_ = bf16[128,256]{1,0:T(8,128)(2,1)S(1)} collective-permute-done((bf16[128,256]{1,0:T(8,128)(2,1)S(1)}, bf16[128,256]{1,0:T(8,128)(2,1)S(1)}, u32[]{:S(2)}, u32[]{:S(2)}) %collective-permute-start) | collective-permute-done | bytes 65568 | tf_op jit(solution)/shard_map/ppermute | solution.py:239
  14.8 1.3 %late.1 = (bf16[640,1024]{1,0:T(8,128)(2,1)S(1)}, bf16[640,1024]{1,0:T(8,128)(2,1)S(1)}, f32[1,1024]{1,0:T(1,128)S(1)}, bf16[128,256]{1,0:T(8,128)(2,1)S(1)}, bf...) custom-call(bf16[1024,128]{1,0:T(8,128)(2,1)S(1)} %get-tuple-element.26.query_ref, ...), custom_call_target="tpu_custom_call" | custom-call | flops 335544320 | bytes 7585792 | tf_op jit(solution)/shard_map/late/pallas_call | solution.py:190
  16.2 1.7 %collective-permute-start.5 = (bf16[128,256]{1,0:T(8,128)(2,1)S(1)}, bf16[128,256]{1,0:T(8,128)(2,1)S(1)}, u32[]{:S(2)}, u32[]{:S(2)}) collective-permute-start(bf16[128,256]{1,0:T(8,128)(2,1)S(1)} %get-tuple-element.42), channel_id=1, source_target_pairs={{4,0},{5,1},{6,2},{7,3},{12,8},{13,9},{14,10},{15,11},{20,16},{21,... | collective-permute-start | bytes 196616 | tf_op jit(solution)/shard_map/ppermute | solution.py:337
  17.9 2.9 %collective-permute-start.6 = (bf16[128,256]{1,0:T(8,128)(2,1)S(1)}, bf16[128,256]{1,0:T(8,128)(2,1)S(1)}, u32[]{:S(2)}, u32[]{:S(2)}) collective-permute-start(bf16[128,256]{1,0:T(8,128)(2,1)S(1)} %get-tuple-element.43), channel_id=1, source_target_pairs={{3,0},{4,1},{5,2},{6,3},{7,4},{11,8},{12,9},{13,10},{14,11},{15,12... | collective-permute-start | bytes 196616 | tf_op jit(solution)/shard_map/ppermute | solution.py:337
  20.7 1.9 %collective-permute-start.7 = (bf16[128,256]{1,0:T(8,128)(2,1)S(1)}, bf16[128,256]{1,0:T(8,128)(2,1)S(1)}, u32[]{:S(2)}, u32[]{:S(2)}) collective-permute-start(bf16[128,256]{1,0:T(8,128)(2,1)S(1)} %get-tuple-element.44), channel_id=1, source_target_pairs={{2,0},{3,1},{4,2},{5,3},{6,4},{7,5},{10,8},{11,9},{12,10},{13,11},... | collective-permute-start | bytes 196616 | tf_op jit(solution)/shard_map/ppermute | solution.py:337
  22.7 2.2 %collective-permute-start.8 = (bf16[128,256]{1,0:T(8,128)(2,1)S(1)}, bf16[128,256]{1,0:T(8,128)(2,1)S(1)}, u32[]{:S(2)}, u32[]{:S(2)}) collective-permute-start(bf16[128,256]{1,0:T(8,128)(2,1)S(1)} %get-tuple-element.45), channel_id=1, source_target_pairs={{1,0},{2,1},{3,2},{4,3},{5,4},{6,5},{7,6},{9,8},{10,9},{11,10},{12... | collective-permute-start | bytes 196616 | tf_op jit(solution)/shard_map/ppermute | solution.py:337
  24.9 1.5 %near.1 = (bf16[128,1024]{1,0:T(8,128)(2,1)}, bf16[128,1024]{1,0:T(8,128)(2,1)}, f32[128,256]{1,0:T(8,128)S(1)}) custom-call(bf16[1024,128]{1,0:T(8,128)(2,1)S(1)} %get-tuple-element.26.query_ref, bf16[1024,128]{1,0:T(8,128)(2,1)S(1)} %get-tuple-element.27.grad_ref, bf16[640,1024]{1,0:T(8,128)(2,1)S(1)} %get-tuple-element.35.weights_ref, ...), custom_call_target="tpu_custom_call" | custom-call | flops 335544320 | bytes 4722688 | tf_op jit(solution)/shard_map/near/pallas_call | solution.py:190
  26.3 0.0 collective-permute-done.5
  26.3 0.0 collective-permute-done.6
  26.3 0.6 %collective-permute-done.7 = bf16[128,256]{1,0:T(8,128)(2,1)S(1)} collective-permute-done((bf16[128,256]{1,0:T(8,128)(2,1)S(1)}, bf16[128,256]{1,0:T(8,128)(2,1)S(1)}, u32[]{:S(2)}, u32[]{:S(2)}) %collective-permute-start.7) | collective-permute-done | bytes 65568 | tf_op jit(solution)/shard_map/ppermute | solution.py:337
  26.9 2.8 %collective-permute-done.8 = bf16[128,256]{1,0:T(8,128)(2,1)S(1)} collective-permute-done((bf16[128,256]{1,0:T(8,128)(2,1)S(1)}, bf16[128,256]{1,0:T(8,128)(2,1)S(1)}, u32[]{:S(2)}, u32[]{:S(2)}) %collective-permute-start.8) | collective-permute-done | bytes 65568 | tf_op jit(solution)/shard_map/ppermute | solution.py:337
  29.8 0.6 %fusion = (bf16[128,128]{1,0:T(8,128)(2,1)}, bf16[128,128]{1,0:T(8,128)(2,1)}) fusion(bf16[128,256]{1,0:T(8,128)(2,1)S(1)} %add_convert_fusion), kind=kLoop, calls=%fused_computation.1 | loop fusion | bytes 131072 | tf_op jit(solution)/shard_map/slice | solution.py:341
  (1 shorter events, 0.0 us)
Async XLA Ops:
  0.6 9.6 %copy-start.1 = (bf16[128,1024]{1,0:T(8,128)(2,1)S(1)}, bf16[128,1024]{1,0:T(8,128)(2,1)}, u32[]{:S(2)}) copy-start(bf16[128,1024]{1,0:T(8,128)(2,1)} %grad_ref.1) | copy-start | bytes 786436
  0.6 9.6 %copy-start = (bf16[128,1024]{1,0:T(8,128)(2,1)S(1)}, bf16[128,1024]{1,0:T(8,128)(2,1)}, u32[]{:S(2)}) copy-start(bf16[128,1024]{1,0:T(8,128)(2,1)} %query_ref.1) | copy-start | bytes 786436
  1.5 9.0 %collective-permute-start.4 = (bf16[128,256]{1,0:T(8,128)(2,1)S(1)}, bf16[128,256]{1,0:T(8,128)(2,1)S(1)}, u32[]{:S(2)}, u32[]{:S(2)}) collective-permute-start(bf16[128,256]{1,0:T(8,128)(2,1)S(1)} %get-tuple-element.31.refs_0_.refs_2_), channel_id=1, source_target_pairs={{0,1},{1,2},{2,3},{3,4},{8,9},{9,10},{10,11},{11,12},{16,17},{17,1... | collective-permute-start | bytes 196616 | tf_op jit(solution)/shard_map/ppermute | solution.py:239
  2.2 8.3 %collective-permute-start.3 = (bf16[128,256]{1,0:T(8,128)(2,1)S(1)}, bf16[128,256]{1,0:T(8,128)(2,1)S(1)}, u32[]{:S(2)}, u32[]{:S(2)}) collective-permute-start(bf16[128,256]{1,0:T(8,128)(2,1)S(1)} %get-tuple-element.31.refs_0_.refs_2_), channel_id=1, source_target_pairs={{0,3},{1,4},{2,5},{3,6},{4,7},{8,11},{9,12},{10,13},{11,14},{12,15... | collective-permute-start | bytes 196616 | tf_op jit(solution)/shard_map/ppermute | solution.py:239
  3.5 7.8 %collective-permute-start.2 = (bf16[128,256]{1,0:T(8,128)(2,1)S(1)}, bf16[128,256]{1,0:T(8,128)(2,1)S(1)}, u32[]{:S(2)}, u32[]{:S(2)}) collective-permute-start(bf16[128,256]{1,0:T(8,128)(2,1)S(1)} %get-tuple-element.31.refs_0_.refs_2_), channel_id=1, source_target_pairs={{0,4},{1,5},{2,6},{3,7},{8,12},{9,13},{10,14},{11,15},{16,20},{17,... | collective-permute-start | bytes 196616 | tf_op jit(solution)/shard_map/ppermute | solution.py:239
  4.8 7.2 %collective-permute-start.1 = (bf16[128,256]{1,0:T(8,128)(2,1)S(1)}, bf16[128,256]{1,0:T(8,128)(2,1)S(1)}, u32[]{:S(2)}, u32[]{:S(2)}) collective-permute-start(bf16[128,256]{1,0:T(8,128)(2,1)S(1)} %get-tuple-element.31.refs_0_.refs_2_), channel_id=1, source_target_pairs={{4,5},{5,6},{6,7},{12,13},{13,14},{14,15},{20,21},{21,22},{22,23},... | collective-permute-start | bytes 196616 | tf_op jit(solution)/shard_map/ppermute | solution.py:239
  8.3 6.6 %collective-permute-start = (bf16[128,256]{1,0:T(8,128)(2,1)S(1)}, bf16[128,256]{1,0:T(8,128)(2,1)S(1)}, u32[]{:S(2)}, u32[]{:S(2)}) collective-permute-start(bf16[128,256]{1,0:T(8,128)(2,1)S(1)} %get-tuple-element.31.refs_0_.refs_2_), channel_id=1, source_target_pairs={{0,2},{1,3},{2,4},{3,5},{4,6},{5,7},{8,10},{9,11},{10,12},{11,13},... | collective-permute-start | bytes 196616 | tf_op jit(solution)/shard_map/ppermute | solution.py:239
  16.2 10.2 %collective-permute-start.5 = (bf16[128,256]{1,0:T(8,128)(2,1)S(1)}, bf16[128,256]{1,0:T(8,128)(2,1)S(1)}, u32[]{:S(2)}, u32[]{:S(2)}) collective-permute-start(bf16[128,256]{1,0:T(8,128)(2,1)S(1)} %get-tuple-element.42), channel_id=1, source_target_pairs={{4,0},{5,1},{6,2},{7,3},{12,8},{13,9},{14,10},{15,11},{20,16},{21,... | collective-permute-start | bytes 196616 | tf_op jit(solution)/shard_map/ppermute | solution.py:337
  17.9 8.5 %collective-permute-start.6 = (bf16[128,256]{1,0:T(8,128)(2,1)S(1)}, bf16[128,256]{1,0:T(8,128)(2,1)S(1)}, u32[]{:S(2)}, u32[]{:S(2)}) collective-permute-start(bf16[128,256]{1,0:T(8,128)(2,1)S(1)} %get-tuple-element.43), channel_id=1, source_target_pairs={{3,0},{4,1},{5,2},{6,3},{7,4},{11,8},{12,9},{13,10},{14,11},{15,12... | collective-permute-start | bytes 196616 | tf_op jit(solution)/shard_map/ppermute | solution.py:337
  20.7 6.2 %collective-permute-start.7 = (bf16[128,256]{1,0:T(8,128)(2,1)S(1)}, bf16[128,256]{1,0:T(8,128)(2,1)S(1)}, u32[]{:S(2)}, u32[]{:S(2)}) collective-permute-start(bf16[128,256]{1,0:T(8,128)(2,1)S(1)} %get-tuple-element.44), channel_id=1, source_target_pairs={{2,0},{3,1},{4,2},{5,3},{6,4},{7,5},{10,8},{11,9},{12,10},{13,11},... | collective-permute-start | bytes 196616 | tf_op jit(solution)/shard_map/ppermute | solution.py:337
  22.7 7.1 %collective-permute-start.8 = (bf16[128,256]{1,0:T(8,128)(2,1)S(1)}, bf16[128,256]{1,0:T(8,128)(2,1)S(1)}, u32[]{:S(2)}, u32[]{:S(2)}) collective-permute-start(bf16[128,256]{1,0:T(8,128)(2,1)S(1)} %get-tuple-element.45), channel_id=1, source_target_pairs={{1,0},{2,1},{3,2},{4,3},{5,4},{6,5},{7,6},{9,8},{10,9},{11,10},{12... | collective-permute-start | bytes 196616 | tf_op jit(solution)/shard_map/ppermute | solution.py:337

commit v3 on v1

--- a/solution.py
+++ b/solution.py
@@ -92,7 +92,7 @@
 def joined(early, kv_refs):
     *kv_blocks, more = [ref[...] for ref in kv_refs]
     kv_blocks[early.index(1)] += more
-    return kv_blocks
+    return [kv_blocks[early.index(back)] for back in sorted(early)]
 
 
 def biased_keys(kv_blocks, bias_ref, places):
@@ -107,7 +107,7 @@
     kv_blocks = joined(early, kv_refs)
     tokens = kv_blocks[0].shape[0]
     columns = parts(query_t_ref.shape[1], tokens)
-    keys = biased_keys(kv_blocks, bias_ref, early)
+    keys = biased_keys(kv_blocks, bias_ref, sorted(early))
     values = jnp.concatenate([rows[:, HD:] for rows in kv_blocks], axis=0)
     values_t = values.T
     for part in columns:
@@ -126,38 +126,60 @@
 
 def late_kernel(early, late, query_ref, grad_ref, query_t_ref, grad_t_ref, bias_ref, *refs):
     late_kv_ref, early_weights_ref, grad_weights_ref, stats_ref = refs[:4]
-    weights_ref, scores_grad_ref, rescale_ref, *term_refs = refs[4:]
+    weights_ref, scores_grad_ref, rescale_ref, late_term_ref, *term_refs = refs[4:]
     tokens = late_kv_ref.shape[0]
     columns = parts(query_t_ref.shape[1], tokens)
-    early_rows = slice(0, len(early) * tokens)
     late_rows = block(len(early), tokens)
-    keys = biased_keys([late_kv_ref[...]], bias_ref, [late])
-    values = late_kv_ref[:, HD:]
-    scores = [dot(keys, query_t_ref[:, part]) for part in columns]
-    grad_weights = [dot(values, grad_t_ref[:, part]) for part in columns]
-    for part, own, own_grad in zip(columns, scores, grad_weights):
-        early_top = stats_ref[0:1, part]
-        top = jnp.maximum(early_top, jnp.max(own, axis=0, keepdims=True) * exponent_scale)
-        rescale = jnp.exp2(early_top - top)
-        own = jnp.exp2(own * exponent_scale - top)
-        total = rescale * stats_ref[1:2, part] + jnp.sum(own, axis=0, keepdims=True)
-        inverse = 1.0 / total
-        own = own * inverse
-        rescale = rescale * inverse
-        row_dots = rescale * stats_ref[2:3, part] + jnp.sum(own * own_grad, axis=0, keepdims=True)
-        rescale_ref[:, part] = rescale
-        weights_ref[late_rows, part] = own.astype(jnp.bfloat16)
-        scores_grad_ref[late_rows, part] = (own * (own_grad - row_dots)).astype(jnp.bfloat16)
-        own = early_weights_ref[:, part].astype(jnp.float32) * rescale
-        weights_ref[early_rows, part] = own.astype(jnp.bfloat16)
-        scores_grad_ref[early_rows, part] = (
-            own * (grad_weights_ref[:, part] - row_dots)
-        ).astype(jnp.bfloat16)
-    terms = gradient_terms(
-        weights_ref[tokens:, :], scores_grad_ref[tokens:, :], query_ref[...], grad_ref[...]
-    ).astype(jnp.bfloat16)
-    for place, ref in enumerate(term_refs):
-        ref[...] = terms[block(place, tokens)]
+    place = lax.axis_index("ulysses")
+
+    def with_blocks(count):
+        early_rows = slice(0, count * tokens)
+        far_rows = slice(tokens, count * tokens)
+        keys = biased_keys([late_kv_ref[...]], bias_ref, [late])
+        values = late_kv_ref[:, HD:]
+        scores = [dot(keys, query_t_ref[:, part]) for part in columns]
+        grad_weights = [dot(values, grad_t_ref[:, part]) for part in columns]
+        key_terms = value_terms = jnp.zeros((count * tokens, HD), jnp.float32)
+        for part, own, own_grad in zip(columns, scores, grad_weights):
+            early_top = stats_ref[0:1, part]
+            top = jnp.maximum(early_top, jnp.max(own, axis=0, keepdims=True) * exponent_scale)
+            rescale = jnp.exp2(early_top - top)
+            own = jnp.exp2(own * exponent_scale - top)
+            total = rescale * stats_ref[1:2, part] + jnp.sum(own, axis=0, keepdims=True)
+            inverse = 1.0 / total
+            own = own * inverse
+            rescale = rescale * inverse
+            row_dots = rescale * stats_ref[2:3, part]
+            row_dots += jnp.sum(own * own_grad, axis=0, keepdims=True)
+            rescale_ref[:, part] = rescale
+            weights_ref[late_rows, part] = own.astype(jnp.bfloat16)
+            scores_grad_ref[late_rows, part] = (own * (own_grad - row_dots)).astype(jnp.bfloat16)
+            own = early_weights_ref[early_rows, part].astype(jnp.float32) * rescale
+            weights_ref[early_rows, part] = own.astype(jnp.bfloat16)
+            scores_grad_ref[early_rows, part] = (
+                own * (grad_weights_ref[early_rows, part] - row_dots)
+            ).astype(jnp.bfloat16)
+            low_grad = [scores_grad_ref[rows, part] for rows in (late_rows, far_rows)]
+            low = [weights_ref[rows, part] for rows in (late_rows, far_rows)]
+            key_terms += dot(jnp.concatenate(low_grad, axis=0), query_ref[part, :])
+            value_terms += dot(jnp.concatenate(low, axis=0), grad_ref[part, :])
+        missing = len(early) - count
+        if missing:
+            scores_grad_ref[count * tokens : len(early) * tokens, :] = jnp.zeros(
+                (missing * tokens, scores_grad_ref.shape[1]), jnp.bfloat16
+            )
+        terms = jnp.concatenate([key_terms * score_scale, value_terms], axis=1)
+        terms = terms.astype(jnp.bfloat16)
+        for index, ref in enumerate([late_term_ref, *term_refs]):
+            if index < count:
+                ref[...] = terms[block(index, tokens)]
+            else:
+                ref[...] = jnp.zeros_like(ref)
+
+    exist = [sum(back <= reach for back in early) for reach in (late, max(early) - 1, max(early))]
+    pl.when(place <= late)(lambda: with_blocks(exist[0]))
+    pl.when((place > late) & (place < max(early)))(lambda: with_blocks(exist[1]))
+    pl.when(place >= max(early))(lambda: with_blocks(exist[2]))
 
 
 def near_kernel(early, query_ref, grad_ref, weights_ref, scores_grad_ref, rescale_ref, *refs):
@@ -327,7 +349,7 @@
     def side_by_side(parts):
         return parts[0] if len(parts) == 1 else jnp.concatenate(parts, axis=1)
 
-    far_places = places[1:]
+    far_places = [late] + sorted(early)[1:]
     total = side_by_side(totals)
     for back in ordered(list(range(blocks)), OUT_ORDER)[1:]:
         terms = side_by_side([own[far_places.index(back)] for own in far])

time: 30.8 us -> 30.4 us (0.987)
  transfers between devices with their start and end apart: 9 -> 9, of which waited for: 5 -> 5; matrix products, arithmetic and copies ran while one was open for 0% -> 0% of each run, Pallas kernels for 10% -> 11%
where the time goes in v3:
time: 30.4 us; the launch traced here: 30.1 us
  starting transfers between devices  17 us (56%)
  waiting for transfers between devices  6.24 us (21%)
  Pallas kernels  5.38 us (18%)
  between operations  0.78 us (3%)
  local copies, waits for them, and re-layouts  0.64 us (2%)
    ppermute x5, starting transfers between devices, forward(): lax.ppermute(kv, 'ulysses', [(d - back, d) for d in range(max(first, back...  8.63 us
    ppermute x4, starting transfers between devices, per_device(): lax.ppermute(terms, 'ulysses', [(d, d - back) for d in range(back, device...  8.4 us
    pallas_call x5, Pallas kernels, call(): pl.pallas_call(body, out_shape=[jax.ShapeDtypeStruct(shape, dtype) for sh...  5.38 us
    ppermute x4, waiting for transfers between devices, per_device(): lax.ppermute(terms, 'ulysses', [(d, d - back) for d in range(back, device...  3.39 us
    ppermute x5, waiting for transfers between devices, forward(): lax.ppermute(kv, 'ulysses', [(d - back, d) for d in range(max(first, back...  2.85 us
    slice x1, local copies, waits for them, and re-layouts, per_device(): total[:, block(2 * g + 1, HD)]  0.63 us
  transfers between devices with their start and end apart: 9, of which 5 were waited for; matrix products, arithmetic and copies ran while one was open for 0% of the time, Pallas kernels for 11%

profile of v3, /device:TPU:18, one launch (start us, length us, event | category | flops | bytes accessed | tf_op | source)
XLA Modules:
  0.0 30.1 jit_solution(766507526230181454)
XLA Ops:
  0.6 0.0 copy-start.1
  0.6 0.0 copy-start
  0.7 0.9 %fetch.1 = (bf16[128,256]{1,0:T(8,128)(2,1)S(1)}, s32[1,128]{1,0:T(1,128)S(1)}) custom-call(s32[4,12]{1,0:T(4,128)} %doc_hbm.1, bf16[128,128]{1,0:T(8,128)(2,1)} %key_hbm.1, bf16[128,128]{1,0:T(8,128)(2,1)} %value_hbm.1), custom_call_target="tpu_custom_call" | custom-call | flops 2684354560 | bytes 131980 | tf_op jit(solution)/shard_map/fetch/pallas_call | solution.py:209
  1.5 0.7 %collective-permute-start.4 = (bf16[128,256]{1,0:T(8,128)(2,1)S(1)}, bf16[128,256]{1,0:T(8,128)(2,1)S(1)}, u32[]{:S(2)}, u32[]{:S(2)}) collective-permute-start(bf16[128,256]{1,0:T(8,128)(2,1)S(1)} %get-tuple-element.31.refs_0_.refs_2_), channel_id=1, source_target_pairs={{0,1},{1,2},{2,3},{3,4},{8,9},{9,10},{10,11},{11,12},{16,17},{17,1... | collective-permute-start | bytes 196616 | tf_op jit(solution)/shard_map/ppermute | solution.py:258
  2.2 1.3 %collective-permute-start.3 = (bf16[128,256]{1,0:T(8,128)(2,1)S(1)}, bf16[128,256]{1,0:T(8,128)(2,1)S(1)}, u32[]{:S(2)}, u32[]{:S(2)}) collective-permute-start(bf16[128,256]{1,0:T(8,128)(2,1)S(1)} %get-tuple-element.31.refs_0_.refs_2_), channel_id=1, source_target_pairs={{0,3},{1,4},{2,5},{3,6},{4,7},{8,11},{9,12},{10,13},{11,14},{12,15... | collective-permute-start | bytes 196616 | tf_op jit(solution)/shard_map/ppermute | solution.py:258
  3.5 1.3 %collective-permute-start.2 = (bf16[128,256]{1,0:T(8,128)(2,1)S(1)}, bf16[128,256]{1,0:T(8,128)(2,1)S(1)}, u32[]{:S(2)}, u32[]{:S(2)}) collective-permute-start(bf16[128,256]{1,0:T(8,128)(2,1)S(1)} %get-tuple-element.31.refs_0_.refs_2_), channel_id=1, source_target_pairs={{0,4},{1,5},{2,6},{3,7},{8,12},{9,13},{10,14},{11,15},{16,20},{17,... | collective-permute-start | bytes 196616 | tf_op jit(solution)/shard_map/ppermute | solution.py:258
  4.8 3.5 %collective-permute-start.1 = (bf16[128,256]{1,0:T(8,128)(2,1)S(1)}, bf16[128,256]{1,0:T(8,128)(2,1)S(1)}, u32[]{:S(2)}, u32[]{:S(2)}) collective-permute-start(bf16[128,256]{1,0:T(8,128)(2,1)S(1)} %get-tuple-element.31.refs_0_.refs_2_), channel_id=1, source_target_pairs={{4,5},{5,6},{6,7},{12,13},{13,14},{14,15},{20,21},{21,22},{22,23},... | collective-permute-start | bytes 196616 | tf_op jit(solution)/shard_map/ppermute | solution.py:258
  8.3 1.9 %collective-permute-start = (bf16[128,256]{1,0:T(8,128)(2,1)S(1)}, bf16[128,256]{1,0:T(8,128)(2,1)S(1)}, u32[]{:S(2)}, u32[]{:S(2)}) collective-permute-start(bf16[128,256]{1,0:T(8,128)(2,1)S(1)} %get-tuple-element.31.refs_0_.refs_2_), channel_id=1, source_target_pairs={{0,2},{1,3},{2,4},{3,5},{4,6},{5,7},{8,10},{9,11},{10,12},{11,13},... | collective-permute-start | bytes 196616 | tf_op jit(solution)/shard_map/ppermute | solution.py:258
  10.2 0.0 copy-done.1
  10.2 0.0 copy-done
  10.2 0.3 prepare.1
  10.5 0.0 collective-permute-done.4.refs_4_.refs_6_
  10.5 0.0 collective-permute-done.3.refs_3_.refs_5_
  10.5 0.7 %collective-permute-done.2.refs_2_.refs_4_ = bf16[128,256]{1,0:T(8,128)(2,1)S(1)} collective-permute-done((bf16[128,256]{1,0:T(8,128)(2,1)S(1)}, bf16[128,256]{1,0:T(8,128)(2,1)S(1)}, u32[]{:S(2)}, u32[]{:S(2)}) %collective-permute-start.2) | collective-permute-done | bytes 65568 | tf_op jit(solution)/shard_map/ppermute | solution.py:258
  11.3 0.7 %collective-permute-done.1.refs_1_.refs_3_ = bf16[128,256]{1,0:T(8,128)(2,1)S(1)} collective-permute-done((bf16[128,256]{1,0:T(8,128)(2,1)S(1)}, bf16[128,256]{1,0:T(8,128)(2,1)S(1)}, u32[]{:S(2)}, u32[]{:S(2)}) %collective-permute-start.1) | collective-permute-done | bytes 65568 | tf_op jit(solution)/shard_map/ppermute | solution.py:258
  12.0 1.4 %early.1 = (bf16[512,1024]{1,0:T(8,128)(2,1)S(1)}, f32[512,1024]{1,0:T(8,128)S(1)}, f32[3,1024]{1,0:T(4,128)S(1)}, f32[128,1024]{1,0:T(8,128)S(1)}) custom-call(bf16[256,1024]{1,0:T(8,128)(2,1)S(1)} %get-tuple-element.28.query_t_ref, bf16[128,1024]{1,0:T(8,128)(2,1)S(1)} %get-tuple-element.29.grad_t_ref, bf16[640,128]{1,0:T(8,128)(2,1)S(1)} %get-tuple-element.30.bias_ref, ...), custom_call_target="tpu_custom_call" | custom-call | flops 503316480 | bytes 7057408 | tf_op jit(solution)/shard_map/early/pallas_call | solution.py:209
  13.4 1.4 %collective-permute-done.refs_0_.refs_1_ = bf16[128,256]{1,0:T(8,128)(2,1)S(1)} collective-permute-done((bf16[128,256]{1,0:T(8,128)(2,1)S(1)}, bf16[128,256]{1,0:T(8,128)(2,1)S(1)}, u32[]{:S(2)}, u32[]{:S(2)}) %collective-permute-start) | collective-permute-done | bytes 65568 | tf_op jit(solution)/shard_map/ppermute | solution.py:258
  14.8 1.3 %late.1 = (bf16[640,1024]{1,0:T(8,128)(2,1)S(1)}, bf16[640,1024]{1,0:T(8,128)(2,1)S(1)}, f32[1,1024]{1,0:T(1,128)S(1)}, bf16[128,256]{1,0:T(8,128)(2,1)S(1)}, bf...) custom-call(bf16[1024,128]{1,0:T(8,128)(2,1)S(1)} %get-tuple-element.26.query_ref, ...), custom_call_target="tpu_custom_call" | custom-call | flops 335544320 | bytes 7585792 | tf_op jit(solution)/shard_map/late/pallas_call | solution.py:209
  16.2 1.4 %collective-permute-start.5 = (bf16[128,256]{1,0:T(8,128)(2,1)S(1)}, bf16[128,256]{1,0:T(8,128)(2,1)S(1)}, u32[]{:S(2)}, u32[]{:S(2)}) collective-permute-start(bf16[128,256]{1,0:T(8,128)(2,1)S(1)} %get-tuple-element.42), channel_id=1, source_target_pairs={{4,0},{5,1},{6,2},{7,3},{12,8},{13,9},{14,10},{15,11},{20,16},{21,... | collective-permute-start | bytes 196616 | tf_op jit(solution)/shard_map/ppermute | solution.py:356
  17.6 2.9 %collective-permute-start.6 = (bf16[128,256]{1,0:T(8,128)(2,1)S(1)}, bf16[128,256]{1,0:T(8,128)(2,1)S(1)}, u32[]{:S(2)}, u32[]{:S(2)}) collective-permute-start(bf16[128,256]{1,0:T(8,128)(2,1)S(1)} %get-tuple-element.43), channel_id=1, source_target_pairs={{3,0},{4,1},{5,2},{6,3},{7,4},{11,8},{12,9},{13,10},{14,11},{15,12... | collective-permute-start | bytes 196616 | tf_op jit(solution)/shard_map/ppermute | solution.py:356
  20.4 1.9 %collective-permute-start.7 = (bf16[128,256]{1,0:T(8,128)(2,1)S(1)}, bf16[128,256]{1,0:T(8,128)(2,1)S(1)}, u32[]{:S(2)}, u32[]{:S(2)}) collective-permute-start(bf16[128,256]{1,0:T(8,128)(2,1)S(1)} %get-tuple-element.44), channel_id=1, source_target_pairs={{2,0},{3,1},{4,2},{5,3},{6,4},{7,5},{10,8},{11,9},{12,10},{13,11},... | collective-permute-start | bytes 196616 | tf_op jit(solution)/shard_map/ppermute | solution.py:356
  22.4 2.2 %collective-permute-start.8 = (bf16[128,256]{1,0:T(8,128)(2,1)S(1)}, bf16[128,256]{1,0:T(8,128)(2,1)S(1)}, u32[]{:S(2)}, u32[]{:S(2)}) collective-permute-start(bf16[128,256]{1,0:T(8,128)(2,1)S(1)} %get-tuple-element.45), channel_id=1, source_target_pairs={{1,0},{2,1},{3,2},{4,3},{5,4},{6,5},{7,6},{9,8},{10,9},{11,10},{12... | collective-permute-start | bytes 196616 | tf_op jit(solution)/shard_map/ppermute | solution.py:356
  24.6 1.5 %near.1 = (bf16[128,1024]{1,0:T(8,128)(2,1)}, bf16[128,1024]{1,0:T(8,128)(2,1)}, f32[128,256]{1,0:T(8,128)S(1)}) custom-call(bf16[1024,128]{1,0:T(8,128)(2,1)S(1)} %get-tuple-element.26.query_ref, bf16[1024,128]{1,0:T(8,128)(2,1)S(1)} %get-tuple-element.27.grad_ref, bf16[640,1024]{1,0:T(8,128)(2,1)S(1)} %get-tuple-element.35.weights_ref, ...), custom_call_target="tpu_custom_call" | custom-call | flops 335544320 | bytes 4722688 | tf_op jit(solution)/shard_map/near/pallas_call | solution.py:209
  26.0 0.0 collective-permute-done.5
  26.0 0.0 collective-permute-done.6
  26.0 0.6 %collective-permute-done.7 = bf16[128,256]{1,0:T(8,128)(2,1)S(1)} collective-permute-done((bf16[128,256]{1,0:T(8,128)(2,1)S(1)}, bf16[128,256]{1,0:T(8,128)(2,1)S(1)}, u32[]{:S(2)}, u32[]{:S(2)}) %collective-permute-start.7) | collective-permute-done | bytes 65568 | tf_op jit(solution)/shard_map/ppermute | solution.py:356
  26.6 2.8 %collective-permute-done.8 = bf16[128,256]{1,0:T(8,128)(2,1)S(1)} collective-permute-done((bf16[128,256]{1,0:T(8,128)(2,1)S(1)}, bf16[128,256]{1,0:T(8,128)(2,1)S(1)}, u32[]{:S(2)}, u32[]{:S(2)}) %collective-permute-start.8) | collective-permute-done | bytes 65568 | tf_op jit(solution)/shard_map/ppermute | solution.py:356
  29.5 0.6 %fusion = (bf16[128,128]{1,0:T(8,128)(2,1)}, bf16[128,128]{1,0:T(8,128)(2,1)}) fusion(bf16[128,256]{1,0:T(8,128)(2,1)S(1)} %add_convert_fusion), kind=kLoop, calls=%fused_computation.1 | loop fusion | bytes 131072 | tf_op jit(solution)/shard_map/slice | solution.py:360
  (1 shorter events, 0.0 us)
Async XLA Ops:
  0.6 9.6 %copy-start.1 = (bf16[128,1024]{1,0:T(8,128)(2,1)S(1)}, bf16[128,1024]{1,0:T(8,128)(2,1)}, u32[]{:S(2)}) copy-start(bf16[128,1024]{1,0:T(8,128)(2,1)} %grad_ref.1) | copy-start | bytes 786436
  0.6 9.6 %copy-start = (bf16[128,1024]{1,0:T(8,128)(2,1)S(1)}, bf16[128,1024]{1,0:T(8,128)(2,1)}, u32[]{:S(2)}) copy-start(bf16[128,1024]{1,0:T(8,128)(2,1)} %query_ref.1) | copy-start | bytes 786436
  1.5 9.0 %collective-permute-start.4 = (bf16[128,256]{1,0:T(8,128)(2,1)S(1)}, bf16[128,256]{1,0:T(8,128)(2,1)S(1)}, u32[]{:S(2)}, u32[]{:S(2)}) collective-permute-start(bf16[128,256]{1,0:T(8,128)(2,1)S(1)} %get-tuple-element.31.refs_0_.refs_2_), channel_id=1, source_target_pairs={{0,1},{1,2},{2,3},{3,4},{8,9},{9,10},{10,11},{11,12},{16,17},{17,1... | collective-permute-start | bytes 196616 | tf_op jit(solution)/shard_map/ppermute | solution.py:258
  2.2 8.3 %collective-permute-start.3 = (bf16[128,256]{1,0:T(8,128)(2,1)S(1)}, bf16[128,256]{1,0:T(8,128)(2,1)S(1)}, u32[]{:S(2)}, u32[]{:S(2)}) collective-permute-start(bf16[128,256]{1,0:T(8,128)(2,1)S(1)} %get-tuple-element.31.refs_0_.refs_2_), channel_id=1, source_target_pairs={{0,3},{1,4},{2,5},{3,6},{4,7},{8,11},{9,12},{10,13},{11,14},{12,15... | collective-permute-start | bytes 196616 | tf_op jit(solution)/shard_map/ppermute | solution.py:258
  3.5 7.8 %collective-permute-start.2 = (bf16[128,256]{1,0:T(8,128)(2,1)S(1)}, bf16[128,256]{1,0:T(8,128)(2,1)S(1)}, u32[]{:S(2)}, u32[]{:S(2)}) collective-permute-start(bf16[128,256]{1,0:T(8,128)(2,1)S(1)} %get-tuple-element.31.refs_0_.refs_2_), channel_id=1, source_target_pairs={{0,4},{1,5},{2,6},{3,7},{8,12},{9,13},{10,14},{11,15},{16,20},{17,... | collective-permute-start | bytes 196616 | tf_op jit(solution)/shard_map/ppermute | solution.py:258
  4.8 7.2 %collective-permute-start.1 = (bf16[128,256]{1,0:T(8,128)(2,1)S(1)}, bf16[128,256]{1,0:T(8,128)(2,1)S(1)}, u32[]{:S(2)}, u32[]{:S(2)}) collective-permute-start(bf16[128,256]{1,0:T(8,128)(2,1)S(1)} %get-tuple-element.31.refs_0_.refs_2_), channel_id=1, source_target_pairs={{4,5},{5,6},{6,7},{12,13},{13,14},{14,15},{20,21},{21,22},{22,23},... | collective-permute-start | bytes 196616 | tf_op jit(solution)/shard_map/ppermute | solution.py:258
  8.3 6.6 %collective-permute-start = (bf16[128,256]{1,0:T(8,128)(2,1)S(1)}, bf16[128,256]{1,0:T(8,128)(2,1)S(1)}, u32[]{:S(2)}, u32[]{:S(2)}) collective-permute-start(bf16[128,256]{1,0:T(8,128)(2,1)S(1)} %get-tuple-element.31.refs_0_.refs_2_), channel_id=1, source_target_pairs={{0,2},{1,3},{2,4},{3,5},{4,6},{5,7},{8,10},{9,11},{10,12},{11,13},... | collective-permute-start | bytes 196616 | tf_op jit(solution)/shard_map/ppermute | solution.py:258
  16.2 9.9 %collective-permute-start.5 = (bf16[128,256]{1,0:T(8,128)(2,1)S(1)}, bf16[128,256]{1,0:T(8,128)(2,1)S(1)}, u32[]{:S(2)}, u32[]{:S(2)}) collective-permute-start(bf16[128,256]{1,0:T(8,128)(2,1)S(1)} %get-tuple-element.42), channel_id=1, source_target_pairs={{4,0},{5,1},{6,2},{7,3},{12,8},{13,9},{14,10},{15,11},{20,16},{21,... | collective-permute-start | bytes 196616 | tf_op jit(solution)/shard_map/ppermute | solution.py:356
  17.6 8.5 %collective-permute-start.6 = (bf16[128,256]{1,0:T(8,128)(2,1)S(1)}, bf16[128,256]{1,0:T(8,128)(2,1)S(1)}, u32[]{:S(2)}, u32[]{:S(2)}) collective-permute-start(bf16[128,256]{1,0:T(8,128)(2,1)S(1)} %get-tuple-element.43), channel_id=1, source_target_pairs={{3,0},{4,1},{5,2},{6,3},{7,4},{11,8},{12,9},{13,10},{14,11},{15,12... | collective-permute-start | bytes 196616 | tf_op jit(solution)/shard_map/ppermute | solution.py:356
  20.4 6.2 %collective-permute-start.7 = (bf16[128,256]{1,0:T(8,128)(2,1)S(1)}, bf16[128,256]{1,0:T(8,128)(2,1)S(1)}, u32[]{:S(2)}, u32[]{:S(2)}) collective-permute-start(bf16[128,256]{1,0:T(8,128)(2,1)S(1)} %get-tuple-element.44), channel_id=1, source_target_pairs={{2,0},{3,1},{4,2},{5,3},{6,4},{7,5},{10,8},{11,9},{12,10},{13,11},... | collective-permute-start | bytes 196616 | tf_op jit(solution)/shard_map/ppermute | solution.py:356
  22.4 7.1 %collective-permute-start.8 = (bf16[128,256]{1,0:T(8,128)(2,1)S(1)}, bf16[128,256]{1,0:T(8,128)(2,1)S(1)}, u32[]{:S(2)}, u32[]{:S(2)}) collective-permute-start(bf16[128,256]{1,0:T(8,128)(2,1)S(1)} %get-tuple-element.45), channel_id=1, source_target_pairs={{1,0},{2,1},{3,2},{4,3},{5,4},{6,5},{7,6},{9,8},{10,9},{11,10},{12... | collective-permute-start | bytes 196616 | tf_op jit(solution)/shard_map/ppermute | solution.py:356

commit v4 on v3

--- a/solution.py
+++ b/solution.py
@@ -126,7 +126,7 @@
 
 def late_kernel(early, late, query_ref, grad_ref, query_t_ref, grad_t_ref, bias_ref, *refs):
     late_kv_ref, early_weights_ref, grad_weights_ref, stats_ref = refs[:4]
-    weights_ref, scores_grad_ref, rescale_ref, late_term_ref, *term_refs = refs[4:]
+    weights_ref, scores_grad_ref, rescale_ref, late_term_ref, *term_refs, again_ref = refs[4:]
     tokens = late_kv_ref.shape[0]
     columns = parts(query_t_ref.shape[1], tokens)
     late_rows = block(len(early), tokens)
@@ -175,6 +175,7 @@
                 ref[...] = terms[block(index, tokens)]
             else:
                 ref[...] = jnp.zeros_like(ref)
+        again_ref[...] = terms[block(1, tokens)]
 
     exist = [sum(back <= reach for back in early) for reach in (late, max(early) - 1, max(early))]
     pl.when(place <= late)(lambda: with_blocks(exist[0]))
@@ -313,7 +314,7 @@
             functools.partial(late_kernel, early, late),
             "late",
             [((window, columns), low), ((window, columns), low), ((1, columns), jnp.float32)]
-            + [((tokens, 2 * HD), low)] * reach,
+            + [((tokens, 2 * HD), low)] * (reach + 1),
             [],
             2 * product,
             queries,
@@ -351,9 +352,14 @@
 
     far_places = [late] + sorted(early)[1:]
     total = side_by_side(totals)
-    for back in ordered(list(range(blocks)), OUT_ORDER)[1:]:
-        terms = side_by_side([own[far_places.index(back)] for own in far])
-        terms = lax.ppermute(terms, "ulysses", [(d, d - back) for d in range(back, devices)])
+    returns = [(back, 0, devices) for back in ordered(list(range(blocks)), OUT_ORDER)[1:]]
+    returns[-2:] = [(1, reach + 1, devices), returns[-2], (1, 0, reach + 1)]
+    for back, first, last in returns:
+        index = reach if last == reach + 1 else far_places.index(back)
+        terms = side_by_side([own[index] for own in far])
+        terms = lax.ppermute(
+            terms, "ulysses", [(d + back, d) for d in range(first, min(last, devices - back))]
+        )
         total = total + terms.astype(jnp.float32)
     total = total.astype(low)
     grad_keys = side_by_side([total[:, block(2 * g, HD)] for g in range(shared_heads)])

time: 30.4 us -> 30.3 us (level)
  the two profiles are of different devices: /device:TPU:18 before, /device:TPU:10 now
where the time goes in v4:
time: 30.3 us; the launch traced here: 30 us
  starting transfers between devices  18.4 us (61%)
  Pallas kernels  5.18 us (17%)
  waiting for transfers between devices  4.94 us (16%)
  between operations  0.79 us (3%)
  local copies, waits for them, and re-layouts  0.64 us (2%)
    ppermute x5, starting transfers between devices, forward(): lax.ppermute(kv, 'ulysses', [(d - back, d) for d in range(max(first, back...  10.2 us
    ppermute x5, starting transfers between devices, per_device(): lax.ppermute(terms, 'ulysses', [(d + back, d) for d in range(first, min(l...  8.21 us
    pallas_call x5, Pallas kernels, call(): pl.pallas_call(body, out_shape=[jax.ShapeDtypeStruct(shape, dtype) for sh...  5.18 us
    ppermute x5, waiting for transfers between devices, per_device(): lax.ppermute(terms, 'ulysses', [(d + back, d) for d in range(first, min(l...  3.41 us
    ppermute x5, waiting for transfers between devices, forward(): lax.ppermute(kv, 'ulysses', [(d - back, d) for d in range(max(first, back...  1.53 us
    slice x1, local copies, waits for them, and re-layouts, per_device(): total[:, block(2 * g + 1, HD)]  0.63 us
  transfers between devices with their start and end apart: 10, of which 5 were waited for; matrix products, arithmetic and copies ran while one was open for 0% of the time, Pallas kernels for 11%

profile of v4, /device:TPU:10, one launch (start us, length us, event | category | flops | bytes accessed | tf_op | source)
XLA Modules:
  0.0 30.0 jit_solution(11862377573631124385)
XLA Ops:
  0.6 0.0 copy-start.1
  0.6 0.0 copy-start
  0.7 0.9 %fetch.1 = (bf16[128,256]{1,0:T(8,128)(2,1)S(1)}, s32[1,128]{1,0:T(1,128)S(1)}) custom-call(s32[4,12]{1,0:T(4,128)} %doc_hbm.1, bf16[128,128]{1,0:T(8,128)(2,1)} %key_hbm.1, bf16[128,128]{1,0:T(8,128)(2,1)} %value_hbm.1), custom_call_target="tpu_custom_call" | custom-call | flops 2684354560 | bytes 131980 | tf_op jit(solution)/shard_map/fetch/pallas_call | solution.py:210
  1.5 3.5 %collective-permute-start.4 = (bf16[128,256]{1,0:T(8,128)(2,1)S(1)}, bf16[128,256]{1,0:T(8,128)(2,1)S(1)}, u32[]{:S(2)}, u32[]{:S(2)}) collective-permute-start(bf16[128,256]{1,0:T(8,128)(2,1)S(1)} %get-tuple-element.32.refs_0_.refs_2_), channel_id=1, source_target_pairs={{0,1},{1,2},{2,3},{3,4},{8,9},{9,10},{10,11},{11,12},{16,17},{17,1... | collective-permute-start | bytes 196616 | tf_op jit(solution)/shard_map/ppermute | solution.py:259
  5.0 1.9 %collective-permute-start.3 = (bf16[128,256]{1,0:T(8,128)(2,1)S(1)}, bf16[128,256]{1,0:T(8,128)(2,1)S(1)}, u32[]{:S(2)}, u32[]{:S(2)}) collective-permute-start(bf16[128,256]{1,0:T(8,128)(2,1)S(1)} %get-tuple-element.32.refs_0_.refs_2_), channel_id=1, source_target_pairs={{0,3},{1,4},{2,5},{3,6},{4,7},{8,11},{9,12},{10,13},{11,14},{12,15... | collective-permute-start | bytes 196616 | tf_op jit(solution)/shard_map/ppermute | solution.py:259
  6.9 1.3 %collective-permute-start.2 = (bf16[128,256]{1,0:T(8,128)(2,1)S(1)}, bf16[128,256]{1,0:T(8,128)(2,1)S(1)}, u32[]{:S(2)}, u32[]{:S(2)}) collective-permute-start(bf16[128,256]{1,0:T(8,128)(2,1)S(1)} %get-tuple-element.32.refs_0_.refs_2_), channel_id=1, source_target_pairs={{0,4},{1,5},{2,6},{3,7},{8,12},{9,13},{10,14},{11,15},{16,20},{17,... | collective-permute-start | bytes 196616 | tf_op jit(solution)/shard_map/ppermute | solution.py:259
  8.2 0.7 %collective-permute-start.1 = (bf16[128,256]{1,0:T(8,128)(2,1)S(1)}, bf16[128,256]{1,0:T(8,128)(2,1)S(1)}, u32[]{:S(2)}, u32[]{:S(2)}) collective-permute-start(bf16[128,256]{1,0:T(8,128)(2,1)S(1)} %get-tuple-element.32.refs_0_.refs_2_), channel_id=1, source_target_pairs={{4,5},{5,6},{6,7},{12,13},{13,14},{14,15},{20,21},{21,22},{22,23},... | collective-permute-start | bytes 196616 | tf_op jit(solution)/shard_map/ppermute | solution.py:259
  8.9 2.9 %collective-permute-start = (bf16[128,256]{1,0:T(8,128)(2,1)S(1)}, bf16[128,256]{1,0:T(8,128)(2,1)S(1)}, u32[]{:S(2)}, u32[]{:S(2)}) collective-permute-start(bf16[128,256]{1,0:T(8,128)(2,1)S(1)} %get-tuple-element.32.refs_0_.refs_2_), channel_id=1, source_target_pairs={{0,2},{1,3},{2,4},{3,5},{4,6},{5,7},{8,10},{9,11},{10,12},{11,13},... | collective-permute-start | bytes 196616 | tf_op jit(solution)/shard_map/ppermute | solution.py:259
  11.8 0.0 copy-done.1
  11.8 0.0 copy-done
  11.8 0.3 prepare.1
  12.1 0.0 collective-permute-done.4.refs_4_.refs_6_
  12.1 0.4 %collective-permute-done.3.refs_3_.refs_5_ = bf16[128,256]{1,0:T(8,128)(2,1)S(1)} collective-permute-done((bf16[128,256]{1,0:T(8,128)(2,1)S(1)}, bf16[128,256]{1,0:T(8,128)(2,1)S(1)}, u32[]{:S(2)}, u32[]{:S(2)}) %collective-permute-start.3) | collective-permute-done | bytes 65568 | tf_op jit(solution)/shard_map/ppermute | solution.py:259
  12.4 0.5 %collective-permute-done.2.refs_2_.refs_4_ = bf16[128,256]{1,0:T(8,128)(2,1)S(1)} collective-permute-done((bf16[128,256]{1,0:T(8,128)(2,1)S(1)}, bf16[128,256]{1,0:T(8,128)(2,1)S(1)}, u32[]{:S(2)}, u32[]{:S(2)}) %collective-permute-start.2) | collective-permute-done | bytes 65568 | tf_op jit(solution)/shard_map/ppermute | solution.py:259
  12.9 0.0 collective-permute-done.1.refs_1_.refs_3_
  13.0 1.4 %early.1 = (bf16[512,1024]{1,0:T(8,128)(2,1)S(1)}, f32[512,1024]{1,0:T(8,128)S(1)}, f32[3,1024]{1,0:T(4,128)S(1)}, f32[128,1024]{1,0:T(8,128)S(1)}) custom-call(bf16[256,1024]{1,0:T(8,128)(2,1)S(1)} %get-tuple-element.29.query_t_ref, bf16[128,1024]{1,0:T(8,128)(2,1)S(1)} %get-tuple-element.30.grad_t_ref, bf16[640,128]{1,0:T(8,128)(2,1)S(1)} %get-tuple-element.31.bias_ref, ...), custom_call_target="tpu_custom_call" | custom-call | flops 503316480 | bytes 7057408 | tf_op jit(solution)/shard_map/early/pallas_call | solution.py:210
  14.4 0.6 %collective-permute-done.refs_0_.refs_1_ = bf16[128,256]{1,0:T(8,128)(2,1)S(1)} collective-permute-done((bf16[128,256]{1,0:T(8,128)(2,1)S(1)}, bf16[128,256]{1,0:T(8,128)(2,1)S(1)}, u32[]{:S(2)}, u32[]{:S(2)}) %collective-permute-start) | collective-permute-done | bytes 65568 | tf_op jit(solution)/shard_map/ppermute | solution.py:259
  15.1 1.1 %late.1 = (bf16[640,1024]{1,0:T(8,128)(2,1)S(1)}, bf16[640,1024]{1,0:T(8,128)(2,1)S(1)}, f32[1,1024]{1,0:T(1,128)S(1)}, bf16[128,256]{1,0:T(8,128)(2,1)S(1)}, bf...) custom-call(bf16[1024,128]{1,0:T(8,128)(2,1)S(1)} %get-tuple-element, ...), custom_call_target="tpu_custom_call" | custom-call | flops 335544320 | bytes 7651328 | tf_op jit(solution)/shard_map/late/pallas_call | solution.py:210
  16.2 1.3 %collective-permute-start.5 = (bf16[128,256]{1,0:T(8,128)(2,1)S(1)}, bf16[128,256]{1,0:T(8,128)(2,1)S(1)}, u32[]{:S(2)}, u32[]{:S(2)}) collective-permute-start(bf16[128,256]{1,0:T(8,128)(2,1)S(1)} %get-tuple-element.43), channel_id=1, source_target_pairs={{4,0},{5,1},{6,2},{7,3},{12,8},{13,9},{14,10},{15,11},{20,16},{21,... | collective-permute-start | bytes 196616 | tf_op jit(solution)/shard_map/ppermute | solution.py:360
  17.5 2.1 %collective-permute-start.6 = (bf16[128,256]{1,0:T(8,128)(2,1)S(1)}, bf16[128,256]{1,0:T(8,128)(2,1)S(1)}, u32[]{:S(2)}, u32[]{:S(2)}) collective-permute-start(bf16[128,256]{1,0:T(8,128)(2,1)S(1)} %get-tuple-element.44), channel_id=1, source_target_pairs={{3,0},{4,1},{5,2},{6,3},{7,4},{11,8},{12,9},{13,10},{14,11},{15,12... | collective-permute-start | bytes 196616 | tf_op jit(solution)/shard_map/ppermute | solution.py:360
  19.7 0.7 %collective-permute-start.7 = (bf16[128,256]{1,0:T(8,128)(2,1)S(1)}, bf16[128,256]{1,0:T(8,128)(2,1)S(1)}, u32[]{:S(2)}, u32[]{:S(2)}) collective-permute-start(bf16[128,256]{1,0:T(8,128)(2,1)S(1)} %get-tuple-element.45), channel_id=1, source_target_pairs={{6,5},{7,6},{14,13},{15,14},{22,21},{23,22},{30,29},{31,30}} | collective-permute-start | bytes 196616 | tf_op jit(solution)/shard_map/ppermute | solution.py:360
  20.3 1.9 %collective-permute-start.8 = (bf16[128,256]{1,0:T(8,128)(2,1)S(1)}, bf16[128,256]{1,0:T(8,128)(2,1)S(1)}, u32[]{:S(2)}, u32[]{:S(2)}) collective-permute-start(bf16[128,256]{1,0:T(8,128)(2,1)S(1)} %get-tuple-element.46), channel_id=1, source_target_pairs={{2,0},{3,1},{4,2},{5,3},{6,4},{7,5},{10,8},{11,9},{12,10},{13,11},... | collective-permute-start | bytes 196616 | tf_op jit(solution)/shard_map/ppermute | solution.py:360
  22.3 2.2 %collective-permute-start.9 = (bf16[128,256]{1,0:T(8,128)(2,1)S(1)}, bf16[128,256]{1,0:T(8,128)(2,1)S(1)}, u32[]{:S(2)}, u32[]{:S(2)}) collective-permute-start(bf16[128,256]{1,0:T(8,128)(2,1)S(1)} %get-tuple-element.47), channel_id=1, source_target_pairs={{1,0},{2,1},{3,2},{4,3},{5,4},{9,8},{10,9},{11,10},{12,11},{13,12}... | collective-permute-start | bytes 196616 | tf_op jit(solution)/shard_map/ppermute | solution.py:360
  24.5 1.4 %near.1 = (bf16[128,1024]{1,0:T(8,128)(2,1)}, bf16[128,1024]{1,0:T(8,128)(2,1)}, f32[128,256]{1,0:T(8,128)S(1)}) custom-call(bf16[1024,128]{1,0:T(8,128)(2,1)S(1)} %get-tuple-element.27.query_ref, bf16[1024,128]{1,0:T(8,128)(2,1)S(1)} %get-tuple-element.28.grad_ref, bf16[640,1024]{1,0:T(8,128)(2,1)S(1)} %get-tuple-element.36.weights_ref, ...), custom_call_target="tpu_custom_call" | custom-call | flops 335544320 | bytes 4722688 | tf_op jit(solution)/shard_map/near/pallas_call | solution.py:210
  25.9 0.0 collective-permute-done.5
  25.9 0.0 collective-permute-done.6
  25.9 0.0 collective-permute-done.7
  25.9 1.5 %collective-permute-done.8 = bf16[128,256]{1,0:T(8,128)(2,1)S(1)} collective-permute-done((bf16[128,256]{1,0:T(8,128)(2,1)S(1)}, bf16[128,256]{1,0:T(8,128)(2,1)S(1)}, u32[]{:S(2)}, u32[]{:S(2)}) %collective-permute-start.8) | collective-permute-done | bytes 65568 | tf_op jit(solution)/shard_map/ppermute | solution.py:360
  27.5 1.9 %collective-permute-done.9 = bf16[128,256]{1,0:T(8,128)(2,1)S(1)} collective-permute-done((bf16[128,256]{1,0:T(8,128)(2,1)S(1)}, bf16[128,256]{1,0:T(8,128)(2,1)S(1)}, u32[]{:S(2)}, u32[]{:S(2)}) %collective-permute-start.9) | collective-permute-done | bytes 65568 | tf_op jit(solution)/shard_map/ppermute | solution.py:360
  29.3 0.1 add_convert_fusion
  29.4 0.6 %fusion = (bf16[128,128]{1,0:T(8,128)(2,1)}, bf16[128,128]{1,0:T(8,128)(2,1)}) fusion(bf16[128,256]{1,0:T(8,128)(2,1)S(1)} %add_convert_fusion), kind=kLoop, calls=%fused_computation.1 | loop fusion | bytes 131072 | tf_op jit(solution)/shard_map/slice | solution.py:366
Async XLA Ops:
  0.6 11.1 %copy-start.1 = (bf16[128,1024]{1,0:T(8,128)(2,1)S(1)}, bf16[128,1024]{1,0:T(8,128)(2,1)}, u32[]{:S(2)}) copy-start(bf16[128,1024]{1,0:T(8,128)(2,1)} %grad_ref.1) | copy-start | bytes 786436
  0.6 11.1 %copy-start = (bf16[128,1024]{1,0:T(8,128)(2,1)S(1)}, bf16[128,1024]{1,0:T(8,128)(2,1)}, u32[]{:S(2)}) copy-start(bf16[128,1024]{1,0:T(8,128)(2,1)} %query_ref.1) | copy-start | bytes 786436
  1.5 10.5 %collective-permute-start.4 = (bf16[128,256]{1,0:T(8,128)(2,1)S(1)}, bf16[128,256]{1,0:T(8,128)(2,1)S(1)}, u32[]{:S(2)}, u32[]{:S(2)}) collective-permute-start(bf16[128,256]{1,0:T(8,128)(2,1)S(1)} %get-tuple-element.32.refs_0_.refs_2_), channel_id=1, source_target_pairs={{0,1},{1,2},{2,3},{3,4},{8,9},{9,10},{10,11},{11,12},{16,17},{17,1... | collective-permute-start | bytes 196616 | tf_op jit(solution)/shard_map/ppermute | solution.py:259
  5.0 7.5 %collective-permute-start.3 = (bf16[128,256]{1,0:T(8,128)(2,1)S(1)}, bf16[128,256]{1,0:T(8,128)(2,1)S(1)}, u32[]{:S(2)}, u32[]{:S(2)}) collective-permute-start(bf16[128,256]{1,0:T(8,128)(2,1)S(1)} %get-tuple-element.32.refs_0_.refs_2_), channel_id=1, source_target_pairs={{0,3},{1,4},{2,5},{3,6},{4,7},{8,11},{9,12},{10,13},{11,14},{12,15... | collective-permute-start | bytes 196616 | tf_op jit(solution)/shard_map/ppermute | solution.py:259
  6.9 6.0 %collective-permute-start.2 = (bf16[128,256]{1,0:T(8,128)(2,1)S(1)}, bf16[128,256]{1,0:T(8,128)(2,1)S(1)}, u32[]{:S(2)}, u32[]{:S(2)}) collective-permute-start(bf16[128,256]{1,0:T(8,128)(2,1)S(1)} %get-tuple-element.32.refs_0_.refs_2_), channel_id=1, source_target_pairs={{0,4},{1,5},{2,6},{3,7},{8,12},{9,13},{10,14},{11,15},{16,20},{17,... | collective-permute-start | bytes 196616 | tf_op jit(solution)/shard_map/ppermute | solution.py:259
  8.2 4.7 %collective-permute-start.1 = (bf16[128,256]{1,0:T(8,128)(2,1)S(1)}, bf16[128,256]{1,0:T(8,128)(2,1)S(1)}, u32[]{:S(2)}, u32[]{:S(2)}) collective-permute-start(bf16[128,256]{1,0:T(8,128)(2,1)S(1)} %get-tuple-element.32.refs_0_.refs_2_), channel_id=1, source_target_pairs={{4,5},{5,6},{6,7},{12,13},{13,14},{14,15},{20,21},{21,22},{22,23},... | collective-permute-start | bytes 196616 | tf_op jit(solution)/shard_map/ppermute | solution.py:259
  8.9 6.2 %collective-permute-start = (bf16[128,256]{1,0:T(8,128)(2,1)S(1)}, bf16[128,256]{1,0:T(8,128)(2,1)S(1)}, u32[]{:S(2)}, u32[]{:S(2)}) collective-permute-start(bf16[128,256]{1,0:T(8,128)(2,1)S(1)} %get-tuple-element.32.refs_0_.refs_2_), channel_id=1, source_target_pairs={{0,2},{1,3},{2,4},{3,5},{4,6},{5,7},{8,10},{9,11},{10,12},{11,13},... | collective-permute-start | bytes 196616 | tf_op jit(solution)/shard_map/ppermute | solution.py:259
  16.2 9.7 %collective-permute-start.5 = (bf16[128,256]{1,0:T(8,128)(2,1)S(1)}, bf16[128,256]{1,0:T(8,128)(2,1)S(1)}, u32[]{:S(2)}, u32[]{:S(2)}) collective-permute-start(bf16[128,256]{1,0:T(8,128)(2,1)S(1)} %get-tuple-element.43), channel_id=1, source_target_pairs={{4,0},{5,1},{6,2},{7,3},{12,8},{13,9},{14,10},{15,11},{20,16},{21,... | collective-permute-start | bytes 196616 | tf_op jit(solution)/shard_map/ppermute | solution.py:360
  17.5 8.4 %collective-permute-start.6 = (bf16[128,256]{1,0:T(8,128)(2,1)S(1)}, bf16[128,256]{1,0:T(8,128)(2,1)S(1)}, u32[]{:S(2)}, u32[]{:S(2)}) collective-permute-start(bf16[128,256]{1,0:T(8,128)(2,1)S(1)} %get-tuple-element.44), channel_id=1, source_target_pairs={{3,0},{4,1},{5,2},{6,3},{7,4},{11,8},{12,9},{13,10},{14,11},{15,12... | collective-permute-start | bytes 196616 | tf_op jit(solution)/shard_map/ppermute | solution.py:360
  19.7 6.3 %collective-permute-start.7 = (bf16[128,256]{1,0:T(8,128)(2,1)S(1)}, bf16[128,256]{1,0:T(8,128)(2,1)S(1)}, u32[]{:S(2)}, u32[]{:S(2)}) collective-permute-start(bf16[128,256]{1,0:T(8,128)(2,1)S(1)} %get-tuple-element.45), channel_id=1, source_target_pairs={{6,5},{7,6},{14,13},{15,14},{22,21},{23,22},{30,29},{31,30}} | collective-permute-start | bytes 196616 | tf_op jit(solution)/shard_map/ppermute | solution.py:360
  20.3 7.1 %collective-permute-start.8 = (bf16[128,256]{1,0:T(8,128)(2,1)S(1)}, bf16[128,256]{1,0:T(8,128)(2,1)S(1)}, u32[]{:S(2)}, u32[]{:S(2)}) collective-permute-start(bf16[128,256]{1,0:T(8,128)(2,1)S(1)} %get-tuple-element.46), channel_id=1, source_target_pairs={{2,0},{3,1},{4,2},{5,3},{6,4},{7,5},{10,8},{11,9},{12,10},{13,11},... | collective-permute-start | bytes 196616 | tf_op jit(solution)/shard_map/ppermute | solution.py:360
  22.3 7.1 %collective-permute-start.9 = (bf16[128,256]{1,0:T(8,128)(2,1)S(1)}, bf16[128,256]{1,0:T(8,128)(2,1)S(1)}, u32[]{:S(2)}, u32[]{:S(2)}) collective-permute-start(bf16[128,256]{1,0:T(8,128)(2,1)S(1)} %get-tuple-element.47), channel_id=1, source_target_pairs={{1,0},{2,1},{3,2},{4,3},{5,4},{9,8},{10,9},{11,10},{12,11},{13,12}... | collective-permute-start | bytes 196616 | tf_op jit(solution)/shard_map/ppermute | solution.py:360

commit v5 on v4

--- a/solution.py
+++ b/solution.py
@@ -102,26 +102,34 @@
     return jnp.concatenate([keys, bias], axis=1)
 
 
-def early_kernel(early, query_t_ref, grad_t_ref, bias_ref, *refs):
+def early_kernel(early, late, query_t_ref, grad_t_ref, bias_ref, *refs):
     *kv_refs, weights_ref, grad_weights_ref, stats_ref, out_t_ref, scores_ref = refs
-    kv_blocks = joined(early, kv_refs)
-    tokens = kv_blocks[0].shape[0]
+    tokens = kv_refs[0].shape[0]
     columns = parts(query_t_ref.shape[1], tokens)
-    keys = biased_keys(kv_blocks, bias_ref, sorted(early))
-    values = jnp.concatenate([rows[:, HD:] for rows in kv_blocks], axis=0)
-    values_t = values.T
-    for part in columns:
-        scores_ref[:, part] = dot(keys, query_t_ref[:, part])
-    for part in columns:
-        grad_weights_ref[:, part] = dot(values, grad_t_ref[:, part])
-        top = jnp.max(scores_ref[:, part], axis=0, keepdims=True) * exponent_scale
-        weights = jnp.exp2(scores_ref[:, part] * exponent_scale - top)
-        stats_ref[0:1, part] = top
-        stats_ref[1:2, part] = jnp.sum(weights, axis=0, keepdims=True)
-        stats_ref[2:3, part] = jnp.sum(weights * grad_weights_ref[:, part], axis=0, keepdims=True)
-        weights_ref[:, part] = weights.astype(jnp.bfloat16)
-    for part in columns:
-        out_t_ref[:, part] = dot(values_t, weights_ref[:, part])
+    place = lax.axis_index("ulysses")
+
+    def with_blocks(count):
+        rows = slice(0, count * tokens)
+        kv_blocks = joined(early, kv_refs)[:count]
+        keys = biased_keys(kv_blocks, bias_ref, sorted(early)[:count])
+        values = jnp.concatenate([own[:, HD:] for own in kv_blocks], axis=0)
+        values_t = values.T
+        for part in columns:
+            scores_ref[rows, part] = dot(keys, query_t_ref[:, part])
+        for part in columns:
+            grad_weights = dot(values, grad_t_ref[:, part])
+            grad_weights_ref[rows, part] = grad_weights
+            top = jnp.max(scores_ref[rows, part], axis=0, keepdims=True) * exponent_scale
+            weights = jnp.exp2(scores_ref[rows, part] * exponent_scale - top)
+            stats_ref[0:1, part] = top
+            stats_ref[1:2, part] = jnp.sum(weights, axis=0, keepdims=True)
+            stats_ref[2:3, part] = jnp.sum(weights * grad_weights, axis=0, keepdims=True)
+            weights_ref[rows, part] = weights.astype(jnp.bfloat16)
+        for part in columns:
+            out_t_ref[:, part] = dot(values_t, weights_ref[rows, part])
+
+    pl.when(place <= late)(lambda: with_blocks(sum(back <= late for back in early)))
+    pl.when(place > late)(lambda: with_blocks(len(early)))
 
 
 def late_kernel(early, late, query_ref, grad_ref, query_t_ref, grad_t_ref, bias_ref, *refs):
@@ -295,7 +303,7 @@
             own_grads,
         )
         weights, grad_weights, stats, early_out_t = call(
-            functools.partial(early_kernel, early),
+            functools.partial(early_kernel, early, late),
             "early",
             [
                 ((window_early, columns), low),

time: 30.3 us -> 30.3 us (level)
  transfers between devices with their start and end apart: 10 -> 10, of which waited for: 5 -> 5; matrix products, arithmetic and copies ran while one was open for 0% -> 0% of each run, Pallas kernels for 11% -> 10%
where the time goes in v5:
time: 30.3 us; the launch traced here: 30 us
  starting transfers between devices  18.4 us (61%)
  waiting for transfers between devices  5.15 us (17%)
  Pallas kernels  4.98 us (16%)
  between operations  0.79 us (3%)
  local copies, waits for them, and re-layouts  0.64 us (2%)
    ppermute x5, starting transfers between devices, forward(): lax.ppermute(kv, 'ulysses', [(d - back, d) for d in range(max(first, back...  10.2 us
    ppermute x5, starting transfers between devices, per_device(): lax.ppermute(terms, 'ulysses', [(d + back, d) for d in range(first, min(l...  8.21 us
    pallas_call x5, Pallas kernels, call(): pl.pallas_call(body, out_shape=[jax.ShapeDtypeStruct(shape, dtype) for sh...  4.98 us
    ppermute x5, waiting for transfers between devices, per_device(): lax.ppermute(terms, 'ulysses', [(d + back, d) for d in range(first, min(l...  3.41 us
    ppermute x5, waiting for transfers between devices, forward(): lax.ppermute(kv, 'ulysses', [(d - back, d) for d in range(max(first, back...  1.74 us
    slice x1, local copies, waits for them, and re-layouts, per_device(): total[:, block(2 * g + 1, HD)]  0.63 us
  transfers between devices with their start and end apart: 10, of which 5 were waited for; matrix products, arithmetic and copies ran while one was open for 0% of the time, Pallas kernels for 10%

profile of v5, /device:TPU:10, one launch (start us, length us, event | category | flops | bytes accessed | tf_op | source)
XLA Modules:
  0.0 30.0 jit_solution(6563299507865378113)
XLA Ops:
  0.6 0.0 copy-start.1
  0.6 0.0 copy-start
  0.7 0.9 %fetch.1 = (bf16[128,256]{1,0:T(8,128)(2,1)S(1)}, s32[1,128]{1,0:T(1,128)S(1)}) custom-call(s32[4,12]{1,0:T(4,128)} %doc_hbm.1, bf16[128,128]{1,0:T(8,128)(2,1)} %key_hbm.1, bf16[128,128]{1,0:T(8,128)(2,1)} %value_hbm.1), custom_call_target="tpu_custom_call" | custom-call | flops 2684354560 | bytes 131980 | tf_op jit(solution)/shard_map/fetch/pallas_call | solution.py:218
  1.5 3.5 %collective-permute-start.4 = (bf16[128,256]{1,0:T(8,128)(2,1)S(1)}, bf16[128,256]{1,0:T(8,128)(2,1)S(1)}, u32[]{:S(2)}, u32[]{:S(2)}) collective-permute-start(bf16[128,256]{1,0:T(8,128)(2,1)S(1)} %get-tuple-element.32.refs_0_.refs_2_), channel_id=1, source_target_pairs={{0,1},{1,2},{2,3},{3,4},{8,9},{9,10},{10,11},{11,12},{16,17},{17,1... | collective-permute-start | bytes 196616 | tf_op jit(solution)/shard_map/ppermute | solution.py:267
  5.0 1.9 %collective-permute-start.3 = (bf16[128,256]{1,0:T(8,128)(2,1)S(1)}, bf16[128,256]{1,0:T(8,128)(2,1)S(1)}, u32[]{:S(2)}, u32[]{:S(2)}) collective-permute-start(bf16[128,256]{1,0:T(8,128)(2,1)S(1)} %get-tuple-element.32.refs_0_.refs_2_), channel_id=1, source_target_pairs={{0,3},{1,4},{2,5},{3,6},{4,7},{8,11},{9,12},{10,13},{11,14},{12,15... | collective-permute-start | bytes 196616 | tf_op jit(solution)/shard_map/ppermute | solution.py:267
  6.9 1.3 %collective-permute-start.2 = (bf16[128,256]{1,0:T(8,128)(2,1)S(1)}, bf16[128,256]{1,0:T(8,128)(2,1)S(1)}, u32[]{:S(2)}, u32[]{:S(2)}) collective-permute-start(bf16[128,256]{1,0:T(8,128)(2,1)S(1)} %get-tuple-element.32.refs_0_.refs_2_), channel_id=1, source_target_pairs={{0,4},{1,5},{2,6},{3,7},{8,12},{9,13},{10,14},{11,15},{16,20},{17,... | collective-permute-start | bytes 196616 | tf_op jit(solution)/shard_map/ppermute | solution.py:267
  8.2 0.7 %collective-permute-start.1 = (bf16[128,256]{1,0:T(8,128)(2,1)S(1)}, bf16[128,256]{1,0:T(8,128)(2,1)S(1)}, u32[]{:S(2)}, u32[]{:S(2)}) collective-permute-start(bf16[128,256]{1,0:T(8,128)(2,1)S(1)} %get-tuple-element.32.refs_0_.refs_2_), channel_id=1, source_target_pairs={{4,5},{5,6},{6,7},{12,13},{13,14},{14,15},{20,21},{21,22},{22,23},... | collective-permute-start | bytes 196616 | tf_op jit(solution)/shard_map/ppermute | solution.py:267
  8.9 2.9 %collective-permute-start = (bf16[128,256]{1,0:T(8,128)(2,1)S(1)}, bf16[128,256]{1,0:T(8,128)(2,1)S(1)}, u32[]{:S(2)}, u32[]{:S(2)}) collective-permute-start(bf16[128,256]{1,0:T(8,128)(2,1)S(1)} %get-tuple-element.32.refs_0_.refs_2_), channel_id=1, source_target_pairs={{0,2},{1,3},{2,4},{3,5},{4,6},{5,7},{8,10},{9,11},{10,12},{11,13},... | collective-permute-start | bytes 196616 | tf_op jit(solution)/shard_map/ppermute | solution.py:267
  11.8 0.0 copy-done.1
  11.8 0.0 copy-done
  11.8 0.3 prepare.1
  12.1 0.0 collective-permute-done.4.refs_4_.refs_6_
  12.1 0.4 %collective-permute-done.3.refs_3_.refs_5_ = bf16[128,256]{1,0:T(8,128)(2,1)S(1)} collective-permute-done((bf16[128,256]{1,0:T(8,128)(2,1)S(1)}, bf16[128,256]{1,0:T(8,128)(2,1)S(1)}, u32[]{:S(2)}, u32[]{:S(2)}) %collective-permute-start.3) | collective-permute-done | bytes 65568 | tf_op jit(solution)/shard_map/ppermute | solution.py:267
  12.4 0.5 %collective-permute-done.2.refs_2_.refs_4_ = bf16[128,256]{1,0:T(8,128)(2,1)S(1)} collective-permute-done((bf16[128,256]{1,0:T(8,128)(2,1)S(1)}, bf16[128,256]{1,0:T(8,128)(2,1)S(1)}, u32[]{:S(2)}, u32[]{:S(2)}) %collective-permute-start.2) | collective-permute-done | bytes 65568 | tf_op jit(solution)/shard_map/ppermute | solution.py:267
  12.9 0.0 collective-permute-done.1.refs_1_.refs_3_
  13.0 1.2 %early.1 = (bf16[512,1024]{1,0:T(8,128)(2,1)S(1)}, f32[512,1024]{1,0:T(8,128)S(1)}, f32[3,1024]{1,0:T(4,128)S(1)}, f32[128,1024]{1,0:T(8,128)S(1)}) custom-call(bf16[256,1024]{1,0:T(8,128)(2,1)S(1)} %get-tuple-element.29.query_t_ref, bf16[128,1024]{1,0:T(8,128)(2,1)S(1)} %get-tuple-element.30.grad_t_ref, bf16[640,128]{1,0:T(8,128)(2,1)S(1)} %get-tuple-element.31.bias_ref, ...), custom_call_target="tpu_custom_call" | custom-call | flops 503316480 | bytes 7057408 | tf_op jit(solution)/shard_map/early/pallas_call | solution.py:218
  14.2 0.9 %collective-permute-done.refs_0_.refs_1_ = bf16[128,256]{1,0:T(8,128)(2,1)S(1)} collective-permute-done((bf16[128,256]{1,0:T(8,128)(2,1)S(1)}, bf16[128,256]{1,0:T(8,128)(2,1)S(1)}, u32[]{:S(2)}, u32[]{:S(2)}) %collective-permute-start) | collective-permute-done | bytes 65568 | tf_op jit(solution)/shard_map/ppermute | solution.py:267
  15.1 1.1 %late.1 = (bf16[640,1024]{1,0:T(8,128)(2,1)S(1)}, bf16[640,1024]{1,0:T(8,128)(2,1)S(1)}, f32[1,1024]{1,0:T(1,128)S(1)}, bf16[128,256]{1,0:T(8,128)(2,1)S(1)}, bf...) custom-call(bf16[1024,128]{1,0:T(8,128)(2,1)S(1)} %get-tuple-element, ...), custom_call_target="tpu_custom_call" | custom-call | flops 335544320 | bytes 7651328 | tf_op jit(solution)/shard_map/late/pallas_call | solution.py:218
  16.2 1.3 %collective-permute-start.5 = (bf16[128,256]{1,0:T(8,128)(2,1)S(1)}, bf16[128,256]{1,0:T(8,128)(2,1)S(1)}, u32[]{:S(2)}, u32[]{:S(2)}) collective-permute-start(bf16[128,256]{1,0:T(8,128)(2,1)S(1)} %get-tuple-element.43), channel_id=1, source_target_pairs={{4,0},{5,1},{6,2},{7,3},{12,8},{13,9},{14,10},{15,11},{20,16},{21,... | collective-permute-start | bytes 196616 | tf_op jit(solution)/shard_map/ppermute | solution.py:368
  17.5 2.1 %collective-permute-start.6 = (bf16[128,256]{1,0:T(8,128)(2,1)S(1)}, bf16[128,256]{1,0:T(8,128)(2,1)S(1)}, u32[]{:S(2)}, u32[]{:S(2)}) collective-permute-start(bf16[128,256]{1,0:T(8,128)(2,1)S(1)} %get-tuple-element.44), channel_id=1, source_target_pairs={{3,0},{4,1},{5,2},{6,3},{7,4},{11,8},{12,9},{13,10},{14,11},{15,12... | collective-permute-start | bytes 196616 | tf_op jit(solution)/shard_map/ppermute | solution.py:368
  19.7 0.7 %collective-permute-start.7 = (bf16[128,256]{1,0:T(8,128)(2,1)S(1)}, bf16[128,256]{1,0:T(8,128)(2,1)S(1)}, u32[]{:S(2)}, u32[]{:S(2)}) collective-permute-start(bf16[128,256]{1,0:T(8,128)(2,1)S(1)} %get-tuple-element.45), channel_id=1, source_target_pairs={{6,5},{7,6},{14,13},{15,14},{22,21},{23,22},{30,29},{31,30}} | collective-permute-start | bytes 196616 | tf_op jit(solution)/shard_map/ppermute | solution.py:368
  20.3 1.9 %collective-permute-start.8 = (bf16[128,256]{1,0:T(8,128)(2,1)S(1)}, bf16[128,256]{1,0:T(8,128)(2,1)S(1)}, u32[]{:S(2)}, u32[]{:S(2)}) collective-permute-start(bf16[128,256]{1,0:T(8,128)(2,1)S(1)} %get-tuple-element.46), channel_id=1, source_target_pairs={{2,0},{3,1},{4,2},{5,3},{6,4},{7,5},{10,8},{11,9},{12,10},{13,11},... | collective-permute-start | bytes 196616 | tf_op jit(solution)/shard_map/ppermute | solution.py:368
  22.3 2.2 %collective-permute-start.9 = (bf16[128,256]{1,0:T(8,128)(2,1)S(1)}, bf16[128,256]{1,0:T(8,128)(2,1)S(1)}, u32[]{:S(2)}, u32[]{:S(2)}) collective-permute-start(bf16[128,256]{1,0:T(8,128)(2,1)S(1)} %get-tuple-element.47), channel_id=1, source_target_pairs={{1,0},{2,1},{3,2},{4,3},{5,4},{9,8},{10,9},{11,10},{12,11},{13,12}... | collective-permute-start | bytes 196616 | tf_op jit(solution)/shard_map/ppermute | solution.py:368
  24.5 1.4 %near.1 = (bf16[128,1024]{1,0:T(8,128)(2,1)}, bf16[128,1024]{1,0:T(8,128)(2,1)}, f32[128,256]{1,0:T(8,128)S(1)}) custom-call(bf16[1024,128]{1,0:T(8,128)(2,1)S(1)} %get-tuple-element.27.query_ref, bf16[1024,128]{1,0:T(8,128)(2,1)S(1)} %get-tuple-element.28.grad_ref, bf16[640,1024]{1,0:T(8,128)(2,1)S(1)} %get-tuple-element.36.weights_ref, ...), custom_call_target="tpu_custom_call" | custom-call | flops 335544320 | bytes 4722688 | tf_op jit(solution)/shard_map/near/pallas_call | solution.py:218
  25.9 0.0 collective-permute-done.5
  25.9 0.0 collective-permute-done.6
  25.9 0.0 collective-permute-done.7
  25.9 1.5 %collective-permute-done.8 = bf16[128,256]{1,0:T(8,128)(2,1)S(1)} collective-permute-done((bf16[128,256]{1,0:T(8,128)(2,1)S(1)}, bf16[128,256]{1,0:T(8,128)(2,1)S(1)}, u32[]{:S(2)}, u32[]{:S(2)}) %collective-permute-start.8) | collective-permute-done | bytes 65568 | tf_op jit(solution)/shard_map/ppermute | solution.py:368
  27.5 1.9 %collective-permute-done.9 = bf16[128,256]{1,0:T(8,128)(2,1)S(1)} collective-permute-done((bf16[128,256]{1,0:T(8,128)(2,1)S(1)}, bf16[128,256]{1,0:T(8,128)(2,1)S(1)}, u32[]{:S(2)}, u32[]{:S(2)}) %collective-permute-start.9) | collective-permute-done | bytes 65568 | tf_op jit(solution)/shard_map/ppermute | solution.py:368
  29.3 0.1 add_convert_fusion
  29.4 0.6 %fusion = (bf16[128,128]{1,0:T(8,128)(2,1)}, bf16[128,128]{1,0:T(8,128)(2,1)}) fusion(bf16[128,256]{1,0:T(8,128)(2,1)S(1)} %add_convert_fusion), kind=kLoop, calls=%fused_computation.1 | loop fusion | bytes 131072 | tf_op jit(solution)/shard_map/slice | solution.py:374
Async XLA Ops:
  0.6 11.1 %copy-start.1 = (bf16[128,1024]{1,0:T(8,128)(2,1)S(1)}, bf16[128,1024]{1,0:T(8,128)(2,1)}, u32[]{:S(2)}) copy-start(bf16[128,1024]{1,0:T(8,128)(2,1)} %grad_ref.1) | copy-start | bytes 786436
  0.6 11.1 %copy-start = (bf16[128,1024]{1,0:T(8,128)(2,1)S(1)}, bf16[128,1024]{1,0:T(8,128)(2,1)}, u32[]{:S(2)}) copy-start(bf16[128,1024]{1,0:T(8,128)(2,1)} %query_ref.1) | copy-start | bytes 786436
  1.5 10.5 %collective-permute-start.4 = (bf16[128,256]{1,0:T(8,128)(2,1)S(1)}, bf16[128,256]{1,0:T(8,128)(2,1)S(1)}, u32[]{:S(2)}, u32[]{:S(2)}) collective-permute-start(bf16[128,256]{1,0:T(8,128)(2,1)S(1)} %get-tuple-element.32.refs_0_.refs_2_), channel_id=1, source_target_pairs={{0,1},{1,2},{2,3},{3,4},{8,9},{9,10},{10,11},{11,12},{16,17},{17,1... | collective-permute-start | bytes 196616 | tf_op jit(solution)/shard_map/ppermute | solution.py:267
  5.0 7.5 %collective-permute-start.3 = (bf16[128,256]{1,0:T(8,128)(2,1)S(1)}, bf16[128,256]{1,0:T(8,128)(2,1)S(1)}, u32[]{:S(2)}, u32[]{:S(2)}) collective-permute-start(bf16[128,256]{1,0:T(8,128)(2,1)S(1)} %get-tuple-element.32.refs_0_.refs_2_), channel_id=1, source_target_pairs={{0,3},{1,4},{2,5},{3,6},{4,7},{8,11},{9,12},{10,13},{11,14},{12,15... | collective-permute-start | bytes 196616 | tf_op jit(solution)/shard_map/ppermute | solution.py:267
  6.9 6.0 %collective-permute-start.2 = (bf16[128,256]{1,0:T(8,128)(2,1)S(1)}, bf16[128,256]{1,0:T(8,128)(2,1)S(1)}, u32[]{:S(2)}, u32[]{:S(2)}) collective-permute-start(bf16[128,256]{1,0:T(8,128)(2,1)S(1)} %get-tuple-element.32.refs_0_.refs_2_), channel_id=1, source_target_pairs={{0,4},{1,5},{2,6},{3,7},{8,12},{9,13},{10,14},{11,15},{16,20},{17,... | collective-permute-start | bytes 196616 | tf_op jit(solution)/shard_map/ppermute | solution.py:267
  8.2 4.7 %collective-permute-start.1 = (bf16[128,256]{1,0:T(8,128)(2,1)S(1)}, bf16[128,256]{1,0:T(8,128)(2,1)S(1)}, u32[]{:S(2)}, u32[]{:S(2)}) collective-permute-start(bf16[128,256]{1,0:T(8,128)(2,1)S(1)} %get-tuple-element.32.refs_0_.refs_2_), channel_id=1, source_target_pairs={{4,5},{5,6},{6,7},{12,13},{13,14},{14,15},{20,21},{21,22},{22,23},... | collective-permute-start | bytes 196616 | tf_op jit(solution)/shard_map/ppermute | solution.py:267
  8.9 6.2 %collective-permute-start = (bf16[128,256]{1,0:T(8,128)(2,1)S(1)}, bf16[128,256]{1,0:T(8,128)(2,1)S(1)}, u32[]{:S(2)}, u32[]{:S(2)}) collective-permute-start(bf16[128,256]{1,0:T(8,128)(2,1)S(1)} %get-tuple-element.32.refs_0_.refs_2_), channel_id=1, source_target_pairs={{0,2},{1,3},{2,4},{3,5},{4,6},{5,7},{8,10},{9,11},{10,12},{11,13},... | collective-permute-start | bytes 196616 | tf_op jit(solution)/shard_map/ppermute | solution.py:267
  16.2 9.7 %collective-permute-start.5 = (bf16[128,256]{1,0:T(8,128)(2,1)S(1)}, bf16[128,256]{1,0:T(8,128)(2,1)S(1)}, u32[]{:S(2)}, u32[]{:S(2)}) collective-permute-start(bf16[128,256]{1,0:T(8,128)(2,1)S(1)} %get-tuple-element.43), channel_id=1, source_target_pairs={{4,0},{5,1},{6,2},{7,3},{12,8},{13,9},{14,10},{15,11},{20,16},{21,... | collective-permute-start | bytes 196616 | tf_op jit(solution)/shard_map/ppermute | solution.py:368
  17.5 8.4 %collective-permute-start.6 = (bf16[128,256]{1,0:T(8,128)(2,1)S(1)}, bf16[128,256]{1,0:T(8,128)(2,1)S(1)}, u32[]{:S(2)}, u32[]{:S(2)}) collective-permute-start(bf16[128,256]{1,0:T(8,128)(2,1)S(1)} %get-tuple-element.44), channel_id=1, source_target_pairs={{3,0},{4,1},{5,2},{6,3},{7,4},{11,8},{12,9},{13,10},{14,11},{15,12... | collective-permute-start | bytes 196616 | tf_op jit(solution)/shard_map/ppermute | solution.py:368
  19.7 6.3 %collective-permute-start.7 = (bf16[128,256]{1,0:T(8,128)(2,1)S(1)}, bf16[128,256]{1,0:T(8,128)(2,1)S(1)}, u32[]{:S(2)}, u32[]{:S(2)}) collective-permute-start(bf16[128,256]{1,0:T(8,128)(2,1)S(1)} %get-tuple-element.45), channel_id=1, source_target_pairs={{6,5},{7,6},{14,13},{15,14},{22,21},{23,22},{30,29},{31,30}} | collective-permute-start | bytes 196616 | tf_op jit(solution)/shard_map/ppermute | solution.py:368
  20.3 7.1 %collective-permute-start.8 = (bf16[128,256]{1,0:T(8,128)(2,1)S(1)}, bf16[128,256]{1,0:T(8,128)(2,1)S(1)}, u32[]{:S(2)}, u32[]{:S(2)}) collective-permute-start(bf16[128,256]{1,0:T(8,128)(2,1)S(1)} %get-tuple-element.46), channel_id=1, source_target_pairs={{2,0},{3,1},{4,2},{5,3},{6,4},{7,5},{10,8},{11,9},{12,10},{13,11},... | collective-permute-start | bytes 196616 | tf_op jit(solution)/shard_map/ppermute | solution.py:368
  22.3 7.1 %collective-permute-start.9 = (bf16[128,256]{1,0:T(8,128)(2,1)S(1)}, bf16[128,256]{1,0:T(8,128)(2,1)S(1)}, u32[]{:S(2)}, u32[]{:S(2)}) collective-permute-start(bf16[128,256]{1,0:T(8,128)(2,1)S(1)} %get-tuple-element.47), channel_id=1, source_target_pairs={{1,0},{2,1},{3,2},{4,3},{5,4},{9,8},{10,9},{11,10},{12,11},{13,12}... | collective-permute-start | bytes 196616 | tf_op jit(solution)/shard_map/ppermute | solution.py:368

commit v6 on v5

--- a/solution.py
+++ b/solution.py
@@ -140,35 +140,47 @@
     late_rows = block(len(early), tokens)
     place = lax.axis_index("ulysses")
 
-    def with_blocks(count):
+    def with_blocks(count, has_late=True):
         early_rows = slice(0, count * tokens)
         far_rows = slice(tokens, count * tokens)
-        keys = biased_keys([late_kv_ref[...]], bias_ref, [late])
-        values = late_kv_ref[:, HD:]
-        scores = [dot(keys, query_t_ref[:, part]) for part in columns]
-        grad_weights = [dot(values, grad_t_ref[:, part]) for part in columns]
-        key_terms = value_terms = jnp.zeros((count * tokens, HD), jnp.float32)
-        for part, own, own_grad in zip(columns, scores, grad_weights):
-            early_top = stats_ref[0:1, part]
-            top = jnp.maximum(early_top, jnp.max(own, axis=0, keepdims=True) * exponent_scale)
-            rescale = jnp.exp2(early_top - top)
-            own = jnp.exp2(own * exponent_scale - top)
-            total = rescale * stats_ref[1:2, part] + jnp.sum(own, axis=0, keepdims=True)
+        term_rows = ([late_rows] if has_late else []) + [far_rows]
+        if has_late:
+            keys = biased_keys([late_kv_ref[...]], bias_ref, [late])
+            values = late_kv_ref[:, HD:]
+            scores = [dot(keys, query_t_ref[:, part]) for part in columns]
+            grad_weights = [dot(values, grad_t_ref[:, part]) for part in columns]
+        else:
+            for ref in (weights_ref, scores_grad_ref):
+                ref[late_rows, :] = jnp.zeros((tokens, ref.shape[1]), jnp.bfloat16)
+        key_terms = value_terms = jnp.zeros(((count - 1 + has_late) * tokens, HD), jnp.float32)
+        for index, part in enumerate(columns):
+            rescale = 1.0
+            total = stats_ref[1:2, part]
+            if has_late:
+                own, own_grad = scores[index], grad_weights[index]
+                early_top = stats_ref[0:1, part]
+                top = jnp.maximum(early_top, jnp.max(own, axis=0, keepdims=True) * exponent_scale)
+                rescale = jnp.exp2(early_top - top)
+                own = jnp.exp2(own * exponent_scale - top)
+                total = rescale * total + jnp.sum(own, axis=0, keepdims=True)
             inverse = 1.0 / total
-            own = own * inverse
             rescale = rescale * inverse
             row_dots = rescale * stats_ref[2:3, part]
-            row_dots += jnp.sum(own * own_grad, axis=0, keepdims=True)
             rescale_ref[:, part] = rescale
-            weights_ref[late_rows, part] = own.astype(jnp.bfloat16)
-            scores_grad_ref[late_rows, part] = (own * (own_grad - row_dots)).astype(jnp.bfloat16)
+            if has_late:
+                own = own * inverse
+                row_dots += jnp.sum(own * own_grad, axis=0, keepdims=True)
+                weights_ref[late_rows, part] = own.astype(jnp.bfloat16)
+                scores_grad_ref[late_rows, part] = (own * (own_grad - row_dots)).astype(
+                    jnp.bfloat16
+                )
             own = early_weights_ref[early_rows, part].astype(jnp.float32) * rescale
             weights_ref[early_rows, part] = own.astype(jnp.bfloat16)
             scores_grad_ref[early_rows, part] = (
                 own * (grad_weights_ref[early_rows, part] - row_dots)
             ).astype(jnp.bfloat16)
-            low_grad = [scores_grad_ref[rows, part] for rows in (late_rows, far_rows)]
-            low = [weights_ref[rows, part] for rows in (late_rows, far_rows)]
+            low_grad = [scores_grad_ref[rows, part] for rows in term_rows]
+            low = [weights_ref[rows, part] for rows in term_rows]
             key_terms += dot(jnp.concatenate(low_grad, axis=0), query_ref[part, :])
             value_terms += dot(jnp.concatenate(low, axis=0), grad_ref[part, :])
         missing = len(early) - count
@@ -178,15 +190,16 @@
             )
         terms = jnp.concatenate([key_terms * score_scale, value_terms], axis=1)
         terms = terms.astype(jnp.bfloat16)
-        for index, ref in enumerate([late_term_ref, *term_refs]):
-            if index < count:
-                ref[...] = terms[block(index, tokens)]
-            else:
-                ref[...] = jnp.zeros_like(ref)
-        again_ref[...] = terms[block(1, tokens)]
+        existing = ([late_term_ref] if has_late else []) + term_refs[: count - 1]
+        for index, ref in enumerate(existing):
+            ref[...] = terms[block(index, tokens)]
+        for ref in term_refs[count - 1 :] + ([] if has_late else [late_term_ref]):
+            ref[...] = jnp.zeros_like(ref)
+        again_ref[...] = term_refs[0][...]
 
     exist = [sum(back <= reach for back in early) for reach in (late, max(early) - 1, max(early))]
-    pl.when(place <= late)(lambda: with_blocks(exist[0]))
+    pl.when(place < late)(lambda: with_blocks(exist[0], has_late=False))
+    pl.when(place == late)(lambda: with_blocks(exist[0]))
     pl.when((place > late) & (place < max(early)))(lambda: with_blocks(exist[1]))
     pl.when(place >= max(early))(lambda: with_blocks(exist[2]))
 

time: 30.3 us -> 30.1 us (level)
  no operation moved by 1% of the time
where the time goes in v6:
time: 30.1 us; the launch traced here: 29.8 us
  starting transfers between devices  18.4 us (61%)
  Pallas kernels  4.99 us (17%)
  waiting for transfers between devices  4.91 us (16%)
  between operations  0.79 us (3%)
  local copies, waits for them, and re-layouts  0.64 us (2%)
    ppermute x5, starting transfers between devices, forward(): lax.ppermute(kv, 'ulysses', [(d - back, d) for d in range(max(first, back...  10.2 us
    ppermute x5, starting transfers between devices, per_device(): lax.ppermute(terms, 'ulysses', [(d + back, d) for d in range(first, min(l...  8.21 us
    pallas_call x5, Pallas kernels, call(): pl.pallas_call(body, out_shape=[jax.ShapeDtypeStruct(shape, dtype) for sh...  4.99 us
    ppermute x5, waiting for transfers between devices, per_device(): lax.ppermute(terms, 'ulysses', [(d + back, d) for d in range(first, min(l...  3.18 us
    ppermute x5, waiting for transfers between devices, forward(): lax.ppermute(kv, 'ulysses', [(d - back, d) for d in range(max(first, back...  1.74 us
    slice x1, local copies, waits for them, and re-layouts, per_device(): total[:, block(2 * g + 1, HD)]  0.63 us
  transfers between devices with their start and end apart: 10, of which 5 were waited for; matrix products, arithmetic and copies ran while one was open for 0% of the time, Pallas kernels for 10%

profile of v6, /device:TPU:10, one launch (start us, length us, event | category | flops | bytes accessed | tf_op | source)
XLA Modules:
  0.0 29.8 jit_solution(13343382168106790310)
XLA Ops:
  0.6 0.0 copy-start.1
  0.6 0.0 copy-start
  0.7 0.9 %fetch.1 = (bf16[128,256]{1,0:T(8,128)(2,1)S(1)}, s32[1,128]{1,0:T(1,128)S(1)}) custom-call(s32[4,12]{1,0:T(4,128)} %doc_hbm.1, bf16[128,128]{1,0:T(8,128)(2,1)} %key_hbm.1, bf16[128,128]{1,0:T(8,128)(2,1)} %value_hbm.1), custom_call_target="tpu_custom_call" | custom-call | flops 2684354560 | bytes 131980 | tf_op jit(solution)/shard_map/fetch/pallas_call | solution.py:231
  1.5 3.5 %collective-permute-start.4 = (bf16[128,256]{1,0:T(8,128)(2,1)S(1)}, bf16[128,256]{1,0:T(8,128)(2,1)S(1)}, u32[]{:S(2)}, u32[]{:S(2)}) collective-permute-start(bf16[128,256]{1,0:T(8,128)(2,1)S(1)} %get-tuple-element.32.refs_0_.refs_2_), channel_id=1, source_target_pairs={{0,1},{1,2},{2,3},{3,4},{8,9},{9,10},{10,11},{11,12},{16,17},{17,1... | collective-permute-start | bytes 196616 | tf_op jit(solution)/shard_map/ppermute | solution.py:280
  5.0 1.9 %collective-permute-start.3 = (bf16[128,256]{1,0:T(8,128)(2,1)S(1)}, bf16[128,256]{1,0:T(8,128)(2,1)S(1)}, u32[]{:S(2)}, u32[]{:S(2)}) collective-permute-start(bf16[128,256]{1,0:T(8,128)(2,1)S(1)} %get-tuple-element.32.refs_0_.refs_2_), channel_id=1, source_target_pairs={{0,3},{1,4},{2,5},{3,6},{4,7},{8,11},{9,12},{10,13},{11,14},{12,15... | collective-permute-start | bytes 196616 | tf_op jit(solution)/shard_map/ppermute | solution.py:280
  6.9 1.3 %collective-permute-start.2 = (bf16[128,256]{1,0:T(8,128)(2,1)S(1)}, bf16[128,256]{1,0:T(8,128)(2,1)S(1)}, u32[]{:S(2)}, u32[]{:S(2)}) collective-permute-start(bf16[128,256]{1,0:T(8,128)(2,1)S(1)} %get-tuple-element.32.refs_0_.refs_2_), channel_id=1, source_target_pairs={{0,4},{1,5},{2,6},{3,7},{8,12},{9,13},{10,14},{11,15},{16,20},{17,... | collective-permute-start | bytes 196616 | tf_op jit(solution)/shard_map/ppermute | solution.py:280
  8.2 0.7 %collective-permute-start.1 = (bf16[128,256]{1,0:T(8,128)(2,1)S(1)}, bf16[128,256]{1,0:T(8,128)(2,1)S(1)}, u32[]{:S(2)}, u32[]{:S(2)}) collective-permute-start(bf16[128,256]{1,0:T(8,128)(2,1)S(1)} %get-tuple-element.32.refs_0_.refs_2_), channel_id=1, source_target_pairs={{4,5},{5,6},{6,7},{12,13},{13,14},{14,15},{20,21},{21,22},{22,23},... | collective-permute-start | bytes 196616 | tf_op jit(solution)/shard_map/ppermute | solution.py:280
  8.9 2.9 %collective-permute-start = (bf16[128,256]{1,0:T(8,128)(2,1)S(1)}, bf16[128,256]{1,0:T(8,128)(2,1)S(1)}, u32[]{:S(2)}, u32[]{:S(2)}) collective-permute-start(bf16[128,256]{1,0:T(8,128)(2,1)S(1)} %get-tuple-element.32.refs_0_.refs_2_), channel_id=1, source_target_pairs={{0,2},{1,3},{2,4},{3,5},{4,6},{5,7},{8,10},{9,11},{10,12},{11,13},... | collective-permute-start | bytes 196616 | tf_op jit(solution)/shard_map/ppermute | solution.py:280
  11.8 0.0 copy-done.1
  11.8 0.0 copy-done
  11.8 0.3 prepare.1
  12.1 0.0 collective-permute-done.4.refs_4_.refs_6_
  12.1 0.4 %collective-permute-done.3.refs_3_.refs_5_ = bf16[128,256]{1,0:T(8,128)(2,1)S(1)} collective-permute-done((bf16[128,256]{1,0:T(8,128)(2,1)S(1)}, bf16[128,256]{1,0:T(8,128)(2,1)S(1)}, u32[]{:S(2)}, u32[]{:S(2)}) %collective-permute-start.3) | collective-permute-done | bytes 65568 | tf_op jit(solution)/shard_map/ppermute | solution.py:280
  12.4 0.5 %collective-permute-done.2.refs_2_.refs_4_ = bf16[128,256]{1,0:T(8,128)(2,1)S(1)} collective-permute-done((bf16[128,256]{1,0:T(8,128)(2,1)S(1)}, bf16[128,256]{1,0:T(8,128)(2,1)S(1)}, u32[]{:S(2)}, u32[]{:S(2)}) %collective-permute-start.2) | collective-permute-done | bytes 65568 | tf_op jit(solution)/shard_map/ppermute | solution.py:280
  12.9 0.0 collective-permute-done.1.refs_1_.refs_3_
  13.0 1.2 %early.1 = (bf16[512,1024]{1,0:T(8,128)(2,1)S(1)}, f32[512,1024]{1,0:T(8,128)S(1)}, f32[3,1024]{1,0:T(4,128)S(1)}, f32[128,1024]{1,0:T(8,128)S(1)}) custom-call(bf16[256,1024]{1,0:T(8,128)(2,1)S(1)} %get-tuple-element.29.query_t_ref, bf16[128,1024]{1,0:T(8,128)(2,1)S(1)} %get-tuple-element.30.grad_t_ref, bf16[640,128]{1,0:T(8,128)(2,1)S(1)} %get-tuple-element.31.bias_ref, ...), custom_call_target="tpu_custom_call" | custom-call | flops 503316480 | bytes 7057408 | tf_op jit(solution)/shard_map/early/pallas_call | solution.py:231
  14.2 0.9 %collective-permute-done.refs_0_.refs_1_ = bf16[128,256]{1,0:T(8,128)(2,1)S(1)} collective-permute-done((bf16[128,256]{1,0:T(8,128)(2,1)S(1)}, bf16[128,256]{1,0:T(8,128)(2,1)S(1)}, u32[]{:S(2)}, u32[]{:S(2)}) %collective-permute-start) | collective-permute-done | bytes 65568 | tf_op jit(solution)/shard_map/ppermute | solution.py:280
  15.1 1.2 %late.1 = (bf16[640,1024]{1,0:T(8,128)(2,1)S(1)}, bf16[640,1024]{1,0:T(8,128)(2,1)S(1)}, f32[1,1024]{1,0:T(1,128)S(1)}, bf16[128,256]{1,0:T(8,128)(2,1)S(1)}, bf...) custom-call(bf16[1024,128]{1,0:T(8,128)(2,1)S(1)} %get-tuple-element, ...), custom_call_target="tpu_custom_call" | custom-call | flops 335544320 | bytes 7651328 | tf_op jit(solution)/shard_map/late/pallas_call | solution.py:231
  16.2 1.3 %collective-permute-start.5 = (bf16[128,256]{1,0:T(8,128)(2,1)S(1)}, bf16[128,256]{1,0:T(8,128)(2,1)S(1)}, u32[]{:S(2)}, u32[]{:S(2)}) collective-permute-start(bf16[128,256]{1,0:T(8,128)(2,1)S(1)} %get-tuple-element.43), channel_id=1, source_target_pairs={{4,0},{5,1},{6,2},{7,3},{12,8},{13,9},{14,10},{15,11},{20,16},{21,... | collective-permute-start | bytes 196616 | tf_op jit(solution)/shard_map/ppermute | solution.py:381
  17.5 1.9 %collective-permute-start.6 = (bf16[128,256]{1,0:T(8,128)(2,1)S(1)}, bf16[128,256]{1,0:T(8,128)(2,1)S(1)}, u32[]{:S(2)}, u32[]{:S(2)}) collective-permute-start(bf16[128,256]{1,0:T(8,128)(2,1)S(1)} %get-tuple-element.44), channel_id=1, source_target_pairs={{3,0},{4,1},{5,2},{6,3},{7,4},{11,8},{12,9},{13,10},{14,11},{15,12... | collective-permute-start | bytes 196616 | tf_op jit(solution)/shard_map/ppermute | solution.py:381
  19.4 0.7 %collective-permute-start.7 = (bf16[128,256]{1,0:T(8,128)(2,1)S(1)}, bf16[128,256]{1,0:T(8,128)(2,1)S(1)}, u32[]{:S(2)}, u32[]{:S(2)}) collective-permute-start(bf16[128,256]{1,0:T(8,128)(2,1)S(1)} %get-tuple-element.45), channel_id=1, source_target_pairs={{6,5},{7,6},{14,13},{15,14},{22,21},{23,22},{30,29},{31,30}} | collective-permute-start | bytes 196616 | tf_op jit(solution)/shard_map/ppermute | solution.py:381
  20.1 1.9 %collective-permute-start.8 = (bf16[128,256]{1,0:T(8,128)(2,1)S(1)}, bf16[128,256]{1,0:T(8,128)(2,1)S(1)}, u32[]{:S(2)}, u32[]{:S(2)}) collective-permute-start(bf16[128,256]{1,0:T(8,128)(2,1)S(1)} %get-tuple-element.46), channel_id=1, source_target_pairs={{2,0},{3,1},{4,2},{5,3},{6,4},{7,5},{10,8},{11,9},{12,10},{13,11},... | collective-permute-start | bytes 196616 | tf_op jit(solution)/shard_map/ppermute | solution.py:381
  22.0 2.4 %collective-permute-start.9 = (bf16[128,256]{1,0:T(8,128)(2,1)S(1)}, bf16[128,256]{1,0:T(8,128)(2,1)S(1)}, u32[]{:S(2)}, u32[]{:S(2)}) collective-permute-start(bf16[128,256]{1,0:T(8,128)(2,1)S(1)} %get-tuple-element.47), channel_id=1, source_target_pairs={{1,0},{2,1},{3,2},{4,3},{5,4},{9,8},{10,9},{11,10},{12,11},{13,12}... | collective-permute-start | bytes 196616 | tf_op jit(solution)/shard_map/ppermute | solution.py:381
  24.5 1.5 %near.1 = (bf16[128,1024]{1,0:T(8,128)(2,1)}, bf16[128,1024]{1,0:T(8,128)(2,1)}, f32[128,256]{1,0:T(8,128)S(1)}) custom-call(bf16[1024,128]{1,0:T(8,128)(2,1)S(1)} %get-tuple-element.27.query_ref, bf16[1024,128]{1,0:T(8,128)(2,1)S(1)} %get-tuple-element.28.grad_ref, bf16[640,1024]{1,0:T(8,128)(2,1)S(1)} %get-tuple-element.36.weights_ref, ...), custom_call_target="tpu_custom_call" | custom-call | flops 335544320 | bytes 4722688 | tf_op jit(solution)/shard_map/near/pallas_call | solution.py:231
  25.9 0.0 collective-permute-done.5
  25.9 0.0 collective-permute-done.6
  25.9 0.0 collective-permute-done.7
  25.9 1.5 %collective-permute-done.8 = bf16[128,256]{1,0:T(8,128)(2,1)S(1)} collective-permute-done((bf16[128,256]{1,0:T(8,128)(2,1)S(1)}, bf16[128,256]{1,0:T(8,128)(2,1)S(1)}, u32[]{:S(2)}, u32[]{:S(2)}) %collective-permute-start.8) | collective-permute-done | bytes 65568 | tf_op jit(solution)/shard_map/ppermute | solution.py:381
  27.5 1.6 %collective-permute-done.9 = bf16[128,256]{1,0:T(8,128)(2,1)S(1)} collective-permute-done((bf16[128,256]{1,0:T(8,128)(2,1)S(1)}, bf16[128,256]{1,0:T(8,128)(2,1)S(1)}, u32[]{:S(2)}, u32[]{:S(2)}) %collective-permute-start.9) | collective-permute-done | bytes 65568 | tf_op jit(solution)/shard_map/ppermute | solution.py:381
  29.1 0.1 add_convert_fusion
  29.2 0.6 %fusion = (bf16[128,128]{1,0:T(8,128)(2,1)}, bf16[128,128]{1,0:T(8,128)(2,1)}) fusion(bf16[128,256]{1,0:T(8,128)(2,1)S(1)} %add_convert_fusion), kind=kLoop, calls=%fused_computation.1 | loop fusion | bytes 131072 | tf_op jit(solution)/shard_map/slice | solution.py:387
Async XLA Ops:
  0.6 11.1 %copy-start.1 = (bf16[128,1024]{1,0:T(8,128)(2,1)S(1)}, bf16[128,1024]{1,0:T(8,128)(2,1)}, u32[]{:S(2)}) copy-start(bf16[128,1024]{1,0:T(8,128)(2,1)} %grad_ref.1) | copy-start | bytes 786436
  0.6 11.1 %copy-start = (bf16[128,1024]{1,0:T(8,128)(2,1)S(1)}, bf16[128,1024]{1,0:T(8,128)(2,1)}, u32[]{:S(2)}) copy-start(bf16[128,1024]{1,0:T(8,128)(2,1)} %query_ref.1) | copy-start | bytes 786436
  1.5 10.5 %collective-permute-start.4 = (bf16[128,256]{1,0:T(8,128)(2,1)S(1)}, bf16[128,256]{1,0:T(8,128)(2,1)S(1)}, u32[]{:S(2)}, u32[]{:S(2)}) collective-permute-start(bf16[128,256]{1,0:T(8,128)(2,1)S(1)} %get-tuple-element.32.refs_0_.refs_2_), channel_id=1, source_target_pairs={{0,1},{1,2},{2,3},{3,4},{8,9},{9,10},{10,11},{11,12},{16,17},{17,1... | collective-permute-start | bytes 196616 | tf_op jit(solution)/shard_map/ppermute | solution.py:280
  5.0 7.5 %collective-permute-start.3 = (bf16[128,256]{1,0:T(8,128)(2,1)S(1)}, bf16[128,256]{1,0:T(8,128)(2,1)S(1)}, u32[]{:S(2)}, u32[]{:S(2)}) collective-permute-start(bf16[128,256]{1,0:T(8,128)(2,1)S(1)} %get-tuple-element.32.refs_0_.refs_2_), channel_id=1, source_target_pairs={{0,3},{1,4},{2,5},{3,6},{4,7},{8,11},{9,12},{10,13},{11,14},{12,15... | collective-permute-start | bytes 196616 | tf_op jit(solution)/shard_map/ppermute | solution.py:280
  6.9 6.0 %collective-permute-start.2 = (bf16[128,256]{1,0:T(8,128)(2,1)S(1)}, bf16[128,256]{1,0:T(8,128)(2,1)S(1)}, u32[]{:S(2)}, u32[]{:S(2)}) collective-permute-start(bf16[128,256]{1,0:T(8,128)(2,1)S(1)} %get-tuple-element.32.refs_0_.refs_2_), channel_id=1, source_target_pairs={{0,4},{1,5},{2,6},{3,7},{8,12},{9,13},{10,14},{11,15},{16,20},{17,... | collective-permute-start | bytes 196616 | tf_op jit(solution)/shard_map/ppermute | solution.py:280
  8.2 4.7 %collective-permute-start.1 = (bf16[128,256]{1,0:T(8,128)(2,1)S(1)}, bf16[128,256]{1,0:T(8,128)(2,1)S(1)}, u32[]{:S(2)}, u32[]{:S(2)}) collective-permute-start(bf16[128,256]{1,0:T(8,128)(2,1)S(1)} %get-tuple-element.32.refs_0_.refs_2_), channel_id=1, source_target_pairs={{4,5},{5,6},{6,7},{12,13},{13,14},{14,15},{20,21},{21,22},{22,23},... | collective-permute-start | bytes 196616 | tf_op jit(solution)/shard_map/ppermute | solution.py:280
  8.9 6.2 %collective-permute-start = (bf16[128,256]{1,0:T(8,128)(2,1)S(1)}, bf16[128,256]{1,0:T(8,128)(2,1)S(1)}, u32[]{:S(2)}, u32[]{:S(2)}) collective-permute-start(bf16[128,256]{1,0:T(8,128)(2,1)S(1)} %get-tuple-element.32.refs_0_.refs_2_), channel_id=1, source_target_pairs={{0,2},{1,3},{2,4},{3,5},{4,6},{5,7},{8,10},{9,11},{10,12},{11,13},... | collective-permute-start | bytes 196616 | tf_op jit(solution)/shard_map/ppermute | solution.py:280
  16.2 9.7 %collective-permute-start.5 = (bf16[128,256]{1,0:T(8,128)(2,1)S(1)}, bf16[128,256]{1,0:T(8,128)(2,1)S(1)}, u32[]{:S(2)}, u32[]{:S(2)}) collective-permute-start(bf16[128,256]{1,0:T(8,128)(2,1)S(1)} %get-tuple-element.43), channel_id=1, source_target_pairs={{4,0},{5,1},{6,2},{7,3},{12,8},{13,9},{14,10},{15,11},{20,16},{21,... | collective-permute-start | bytes 196616 | tf_op jit(solution)/shard_map/ppermute | solution.py:381
  17.5 8.4 %collective-permute-start.6 = (bf16[128,256]{1,0:T(8,128)(2,1)S(1)}, bf16[128,256]{1,0:T(8,128)(2,1)S(1)}, u32[]{:S(2)}, u32[]{:S(2)}) collective-permute-start(bf16[128,256]{1,0:T(8,128)(2,1)S(1)} %get-tuple-element.44), channel_id=1, source_target_pairs={{3,0},{4,1},{5,2},{6,3},{7,4},{11,8},{12,9},{13,10},{14,11},{15,12... | collective-permute-start | bytes 196616 | tf_op jit(solution)/shard_map/ppermute | solution.py:381
  19.4 6.5 %collective-permute-start.7 = (bf16[128,256]{1,0:T(8,128)(2,1)S(1)}, bf16[128,256]{1,0:T(8,128)(2,1)S(1)}, u32[]{:S(2)}, u32[]{:S(2)}) collective-permute-start(bf16[128,256]{1,0:T(8,128)(2,1)S(1)} %get-tuple-element.45), channel_id=1, source_target_pairs={{6,5},{7,6},{14,13},{15,14},{22,21},{23,22},{30,29},{31,30}} | collective-permute-start | bytes 196616 | tf_op jit(solution)/shard_map/ppermute | solution.py:381
  20.1 7.4 %collective-permute-start.8 = (bf16[128,256]{1,0:T(8,128)(2,1)S(1)}, bf16[128,256]{1,0:T(8,128)(2,1)S(1)}, u32[]{:S(2)}, u32[]{:S(2)}) collective-permute-start(bf16[128,256]{1,0:T(8,128)(2,1)S(1)} %get-tuple-element.46), channel_id=1, source_target_pairs={{2,0},{3,1},{4,2},{5,3},{6,4},{7,5},{10,8},{11,9},{12,10},{13,11},... | collective-permute-start | bytes 196616 | tf_op jit(solution)/shard_map/ppermute | solution.py:381
  22.0 7.1 %collective-permute-start.9 = (bf16[128,256]{1,0:T(8,128)(2,1)S(1)}, bf16[128,256]{1,0:T(8,128)(2,1)S(1)}, u32[]{:S(2)}, u32[]{:S(2)}) collective-permute-start(bf16[128,256]{1,0:T(8,128)(2,1)S(1)} %get-tuple-element.47), channel_id=1, source_target_pairs={{1,0},{2,1},{3,2},{4,3},{5,4},{9,8},{10,9},{11,10},{12,11},{13,12}... | collective-permute-start | bytes 196616 | tf_op jit(solution)/shard_map/ppermute | solution.py:381

commit v7 on v6

--- a/solution.py
+++ b/solution.py
@@ -28,8 +28,8 @@
     return slice(index * size, (index + 1) * size)
 
 
-def fetch_kernel(doc_hbm, key_hbm, value_hbm, kv_ref, first_key_ref, doc_ref, sems):
-    pairs = [(doc_hbm, doc_ref)]
+def fetch_kernel(key_hbm, value_hbm, kv_ref, sems):
+    pairs = []
     for shared in range(key_hbm.shape[1] // HD):
         for part, ref in enumerate((key_hbm, value_hbm)):
             pairs.append(
@@ -38,28 +38,23 @@
     copies = [pltpu.make_async_copy(src, dst, sems.at[i]) for i, (src, dst) in enumerate(pairs)]
     for copy in copies:
         copy.start()
-    tokens = key_hbm.shape[0]
-    row = lax.axis_index("dp")
-    place = lax.axis_index("ulysses")
-    query_pos = place * tokens + lax.broadcasted_iota(jnp.int32, (1, tokens), 1)
-    first_key = jnp.zeros((1, tokens), jnp.int32)
-    copies[0].wait()
-    doc_end = jnp.int32(0)
-    for doc in range(doc_ref.shape[1]):
-        doc_end = doc_end + doc_ref[row, doc]
-        first_key = jnp.where(doc_end <= query_pos, doc_end, first_key)
-    first_key_ref[...] = first_key
-    for copy in copies[1:]:
+    for copy in copies:
         copy.wait()
 
 
-def prepare_kernel(reach, first_key_ref, query_ref, grad_ref, *refs):
+def prepare_kernel(reach, doc_ref, query_ref, grad_ref, *refs):
     query_rows_ref, grad_rows_ref, query_t_ref, grad_t_ref, bias_ref = refs
     tokens = query_ref.shape[0]
     place = lax.axis_index("ulysses")
     inner = lax.broadcasted_iota(jnp.int32, (tokens, tokens), 0)
     lanes = lax.broadcasted_iota(jnp.int32, (tokens, tokens), 1)
-    first_key = first_key_ref[...] - place * tokens
+    row = lax.axis_index("dp")
+    first_key = jnp.zeros((1, tokens), jnp.int32)
+    doc_end = jnp.int32(0)
+    for doc in range(doc_ref.shape[1]):
+        doc_end = doc_end + doc_ref[row, doc]
+        first_key = jnp.where(doc_end <= place * tokens + lanes[:1], doc_end, first_key)
+    first_key = first_key - place * tokens
     for back in range(reach + 1):
         key_pos = inner - back * tokens
         allowed = (key_pos >= first_key) & (key_pos <= lanes)
@@ -231,7 +226,14 @@
     return pl.pallas_call(
         body,
         out_shape=[jax.ShapeDtypeStruct(shape, dtype) for shape, dtype in outs],
-        in_specs=[pl.BlockSpec(memory_space=pltpu.HBM) if fetched else vmem] * len(operands),
+        in_specs=[
+            pl.BlockSpec(memory_space=pltpu.HBM)
+            if fetched
+            else pl.BlockSpec(memory_space=pltpu.SMEM)
+            if a.dtype == jnp.int32
+            else vmem
+            for a in operands
+        ],
         out_specs=[vmem] * len(outs),
         scratch_shapes=scratch,
         compiler_params=pltpu.CompilerParams(
@@ -259,19 +261,14 @@
     group_width = query_width // shared_heads
     columns = group_width // HD * tokens
     product = 2 * window * columns * HD
-    kv, first_key = call(
+    (kv,) = call(
         fetch_kernel,
         "fetch",
         [
             ((tokens, 2 * shared_heads * HD), low),
-            ((1, tokens), jnp.int32),
         ],
-        [
-            pltpu.SMEM(doc_lengths.shape, jnp.int32),
-            pltpu.SemaphoreType.DMA((2 * shared_heads + 1,)),
-        ],
+        [pltpu.SemaphoreType.DMA((2 * shared_heads,))],
         16 * product,
-        doc_lengths,
         key_rows,
         value_rows,
         fetched=True,
@@ -311,7 +308,7 @@
             ],
             [],
             product // 4,
-            first_key,
+            doc_lengths,
             own_queries,
             own_grads,
         )

time: 30.1 us -> 30.1 us (level)
  waiting for transfers between devices: 4.91 us -> 4.33 us
  Pallas kernels: 4.99 us -> 5.54 us
    ppermute x5, waiting for transfers between devices: 1.74 us -> 1.15 us  [forward(): lax.ppermute(kv, 'ulysses', [(d - back, d) for d in range(max(first, back...]
    pallas_call x5, Pallas kernels: 4.99 us -> 5.54 us  [call(): pl.pallas_call(body, out_shape=[jax.ShapeDtypeStruct(shape, dtype) for sh...]
  transfers between devices with their start and end apart: 10 -> 10, of which waited for: 5 -> 4; matrix products, arithmetic and copies ran while one was open for 0% -> 0% of each run, Pallas kernels for 10% -> 12%
where the time goes in v7:
time: 30.1 us; the launch traced here: 29.8 us
  starting transfers between devices  18.4 us (61%)
  Pallas kernels  5.54 us (18%)
  waiting for transfers between devices  4.33 us (14%)
  between operations  0.81 us (3%)
  local copies, waits for them, and re-layouts  0.64 us (2%)
    ppermute x5, starting transfers between devices, forward(): lax.ppermute(kv, 'ulysses', [(d - back, d) for d in range(max(first, back...  10.2 us
    ppermute x5, starting transfers between devices, per_device(): lax.ppermute(terms, 'ulysses', [(d + back, d) for d in range(first, min(l...  8.21 us
    pallas_call x5, Pallas kernels, call(): pl.pallas_call(body, out_shape=[jax.ShapeDtypeStruct(shape, dtype) for sh...  5.54 us
    ppermute x5, waiting for transfers between devices, per_device(): lax.ppermute(terms, 'ulysses', [(d + back, d) for d in range(first, min(l...  3.18 us
    ppermute x5, waiting for transfers between devices, forward(): lax.ppermute(kv, 'ulysses', [(d - back, d) for d in range(max(first, back...  1.15 us
    slice x1, local copies, waits for them, and re-layouts, per_device(): total[:, block(2 * g + 1, HD)]  0.63 us
  transfers between devices with their start and end apart: 10, of which 4 were waited for; matrix products, arithmetic and copies ran while one was open for 0% of the time, Pallas kernels for 12%

profile of v7, /device:TPU:10, one launch (start us, length us, event | category | flops | bytes accessed | tf_op | source)
XLA Modules:
  0.0 29.8 jit_solution(2449054977571564999)
XLA Ops:
  0.6 0.0 copy-start.2
  0.6 0.0 copy-start.1
  0.7 0.0 copy-start
  0.7 0.8 %fetch.1.refs_0_.refs_2_ = bf16[128,256]{1,0:T(8,128)(2,1)S(1)} custom-call(bf16[128,128]{1,0:T(8,128)(2,1)} %key_hbm.1, bf16[128,128]{1,0:T(8,128)(2,1)} %value_hbm.1), custom_call_target="tpu_custom_call" | custom-call | flops 2684354560 | bytes 131080 | tf_op jit(solution)/shard_map/fetch/pallas_call | solution.py:226
  1.5 3.5 %collective-permute-start.4 = (bf16[128,256]{1,0:T(8,128)(2,1)S(1)}, bf16[128,256]{1,0:T(8,128)(2,1)S(1)}, u32[]{:S(2)}, u32[]{:S(2)}) collective-permute-start(bf16[128,256]{1,0:T(8,128)(2,1)S(1)} %fetch.1.refs_0_.refs_2_), channel_id=1, source_target_pairs={{0,1},{1,2},{2,3},{3,4},{8,9},{9,10},{10,11},{11,12},{16,17},{17,1... | collective-permute-start | bytes 196616 | tf_op jit(solution)/shard_map/ppermute | solution.py:277
  5.0 1.9 %collective-permute-start.3 = (bf16[128,256]{1,0:T(8,128)(2,1)S(1)}, bf16[128,256]{1,0:T(8,128)(2,1)S(1)}, u32[]{:S(2)}, u32[]{:S(2)}) collective-permute-start(bf16[128,256]{1,0:T(8,128)(2,1)S(1)} %fetch.1.refs_0_.refs_2_), channel_id=1, source_target_pairs={{0,3},{1,4},{2,5},{3,6},{4,7},{8,11},{9,12},{10,13},{11,14},{12,15... | collective-permute-start | bytes 196616 | tf_op jit(solution)/shard_map/ppermute | solution.py:277
  6.9 1.3 %collective-permute-start.2 = (bf16[128,256]{1,0:T(8,128)(2,1)S(1)}, bf16[128,256]{1,0:T(8,128)(2,1)S(1)}, u32[]{:S(2)}, u32[]{:S(2)}) collective-permute-start(bf16[128,256]{1,0:T(8,128)(2,1)S(1)} %fetch.1.refs_0_.refs_2_), channel_id=1, source_target_pairs={{0,4},{1,5},{2,6},{3,7},{8,12},{9,13},{10,14},{11,15},{16,20},{17,... | collective-permute-start | bytes 196616 | tf_op jit(solution)/shard_map/ppermute | solution.py:277
  8.2 0.7 %collective-permute-start.1 = (bf16[128,256]{1,0:T(8,128)(2,1)S(1)}, bf16[128,256]{1,0:T(8,128)(2,1)S(1)}, u32[]{:S(2)}, u32[]{:S(2)}) collective-permute-start(bf16[128,256]{1,0:T(8,128)(2,1)S(1)} %fetch.1.refs_0_.refs_2_), channel_id=1, source_target_pairs={{4,5},{5,6},{6,7},{12,13},{13,14},{14,15},{20,21},{21,22},{22,23},... | collective-permute-start | bytes 196616 | tf_op jit(solution)/shard_map/ppermute | solution.py:277
  8.9 2.9 %collective-permute-start = (bf16[128,256]{1,0:T(8,128)(2,1)S(1)}, bf16[128,256]{1,0:T(8,128)(2,1)S(1)}, u32[]{:S(2)}, u32[]{:S(2)}) collective-permute-start(bf16[128,256]{1,0:T(8,128)(2,1)S(1)} %fetch.1.refs_0_.refs_2_), channel_id=1, source_target_pairs={{0,2},{1,3},{2,4},{3,5},{4,6},{5,7},{8,10},{9,11},{10,12},{11,13},... | collective-permute-start | bytes 196616 | tf_op jit(solution)/shard_map/ppermute | solution.py:277
  11.7 0.0 copy-done.2
  11.8 0.0 copy-done.1
  11.8 0.8 %prepare.1 = (bf16[1024,128]{1,0:T(8,128)(2,1)S(1)}, bf16[1024,128]{1,0:T(8,128)(2,1)S(1)}, bf16[256,1024]{1,0:T(8,128)(2,1)S(1)}, bf16[128,1024]{1,0:T(8,128)(2,1)S(1)}, bf16[640,128]{1,0:T(8,128)(2,1)S(1)}) custom-call(s32[4,12]{1,0:T(4,128)S(1)} %copy-done.2, bf16[128,1024]{1,0:T(8,128)(2,1)S(1)} %copy-done, bf16[128,1024]{1,0:T(8,128)(2,1)S(1)} %copy-done.1), custom_call_target="tpu_custom_call" | custom-call | flops 41943040 | bytes 1999040 | tf_op jit(solution)/shard_map/prepare/pallas_call | solution.py:226
  12.6 0.0 collective-permute-done.4.refs_4_.refs_6_
  12.6 0.0 collective-permute-done.3.refs_3_.refs_5_
  12.6 0.3 collective-permute-done.2.refs_2_.refs_4_
  12.9 0.0 collective-permute-done.1.refs_1_.refs_3_
  12.9 1.2 %early.1 = (bf16[512,1024]{1,0:T(8,128)(2,1)S(1)}, f32[512,1024]{1,0:T(8,128)S(1)}, f32[3,1024]{1,0:T(4,128)S(1)}, f32[128,1024]{1,0:T(8,128)S(1)}) custom-call(bf16[256,1024]{1,0:T(8,128)(2,1)S(1)} %get-tuple-element.26.query_t_ref, bf16[128,1024]{1,0:T(8,128)(2,1)S(1)} %get-tuple-element.27.grad_t_ref, bf16[640,128]{1,0:T(8,128)(2,1)S(1)} %get-tuple-element.28.bias_ref, ...), custom_call_target="tpu_custom_call" | custom-call | flops 503316480 | bytes 7057408 | tf_op jit(solution)/shard_map/early/pallas_call | solution.py:226
  14.2 0.8 %collective-permute-done.refs_0_.refs_1_ = bf16[128,256]{1,0:T(8,128)(2,1)S(1)} collective-permute-done((bf16[128,256]{1,0:T(8,128)(2,1)S(1)}, bf16[128,256]{1,0:T(8,128)(2,1)S(1)}, u32[]{:S(2)}, u32[]{:S(2)}) %collective-permute-start) | collective-permute-done | bytes 65568 | tf_op jit(solution)/shard_map/ppermute | solution.py:277
  15.0 1.2 %late.1 = (bf16[640,1024]{1,0:T(8,128)(2,1)S(1)}, bf16[640,1024]{1,0:T(8,128)(2,1)S(1)}, f32[1,1024]{1,0:T(1,128)S(1)}, bf16[128,256]{1,0:T(8,128)(2,1)S(1)}, bf...) custom-call(bf16[1024,128]{1,0:T(8,128)(2,1)S(1)} %get-tuple-element, ...), custom_call_target="tpu_custom_call" | custom-call | flops 335544320 | bytes 7651328 | tf_op jit(solution)/shard_map/late/pallas_call | solution.py:226
  16.2 1.3 %collective-permute-start.5 = (bf16[128,256]{1,0:T(8,128)(2,1)S(1)}, bf16[128,256]{1,0:T(8,128)(2,1)S(1)}, u32[]{:S(2)}, u32[]{:S(2)}) collective-permute-start(bf16[128,256]{1,0:T(8,128)(2,1)S(1)} %get-tuple-element.39), channel_id=1, source_target_pairs={{4,0},{5,1},{6,2},{7,3},{12,8},{13,9},{14,10},{15,11},{20,16},{21,... | collective-permute-start | bytes 196616 | tf_op jit(solution)/shard_map/ppermute | solution.py:378
  17.5 1.9 %collective-permute-start.6 = (bf16[128,256]{1,0:T(8,128)(2,1)S(1)}, bf16[128,256]{1,0:T(8,128)(2,1)S(1)}, u32[]{:S(2)}, u32[]{:S(2)}) collective-permute-start(bf16[128,256]{1,0:T(8,128)(2,1)S(1)} %get-tuple-element.40), channel_id=1, source_target_pairs={{3,0},{4,1},{5,2},{6,3},{7,4},{11,8},{12,9},{13,10},{14,11},{15,12... | collective-permute-start | bytes 196616 | tf_op jit(solution)/shard_map/ppermute | solution.py:378
  19.4 0.7 %collective-permute-start.7 = (bf16[128,256]{1,0:T(8,128)(2,1)S(1)}, bf16[128,256]{1,0:T(8,128)(2,1)S(1)}, u32[]{:S(2)}, u32[]{:S(2)}) collective-permute-start(bf16[128,256]{1,0:T(8,128)(2,1)S(1)} %get-tuple-element.41), channel_id=1, source_target_pairs={{6,5},{7,6},{14,13},{15,14},{22,21},{23,22},{30,29},{31,30}} | collective-permute-start | bytes 196616 | tf_op jit(solution)/shard_map/ppermute | solution.py:378
  20.1 1.9 %collective-permute-start.8 = (bf16[128,256]{1,0:T(8,128)(2,1)S(1)}, bf16[128,256]{1,0:T(8,128)(2,1)S(1)}, u32[]{:S(2)}, u32[]{:S(2)}) collective-permute-start(bf16[128,256]{1,0:T(8,128)(2,1)S(1)} %get-tuple-element.42), channel_id=1, source_target_pairs={{2,0},{3,1},{4,2},{5,3},{6,4},{7,5},{10,8},{11,9},{12,10},{13,11},... | collective-permute-start | bytes 196616 | tf_op jit(solution)/shard_map/ppermute | solution.py:378
  22.0 2.4 %collective-permute-start.9 = (bf16[128,256]{1,0:T(8,128)(2,1)S(1)}, bf16[128,256]{1,0:T(8,128)(2,1)S(1)}, u32[]{:S(2)}, u32[]{:S(2)}) collective-permute-start(bf16[128,256]{1,0:T(8,128)(2,1)S(1)} %get-tuple-element.43), channel_id=1, source_target_pairs={{1,0},{2,1},{3,2},{4,3},{5,4},{9,8},{10,9},{11,10},{12,11},{13,12}... | collective-permute-start | bytes 196616 | tf_op jit(solution)/shard_map/ppermute | solution.py:378
  24.5 1.5 %near.1 = (bf16[128,1024]{1,0:T(8,128)(2,1)}, bf16[128,1024]{1,0:T(8,128)(2,1)}, f32[128,256]{1,0:T(8,128)S(1)}) custom-call(bf16[1024,128]{1,0:T(8,128)(2,1)S(1)} %get-tuple-element.24.query_ref, bf16[1024,128]{1,0:T(8,128)(2,1)S(1)} %get-tuple-element.25.grad_ref, bf16[640,1024]{1,0:T(8,128)(2,1)S(1)} %get-tuple-element.32.weights_ref, ...), custom_call_target="tpu_custom_call" | custom-call | flops 335544320 | bytes 4722688 | tf_op jit(solution)/shard_map/near/pallas_call | solution.py:226
  25.9 0.0 collective-permute-done.5
  25.9 0.0 collective-permute-done.6
  25.9 0.0 collective-permute-done.7
  25.9 1.5 %collective-permute-done.8 = bf16[128,256]{1,0:T(8,128)(2,1)S(1)} collective-permute-done((bf16[128,256]{1,0:T(8,128)(2,1)S(1)}, bf16[128,256]{1,0:T(8,128)(2,1)S(1)}, u32[]{:S(2)}, u32[]{:S(2)}) %collective-permute-start.8) | collective-permute-done | bytes 65568 | tf_op jit(solution)/shard_map/ppermute | solution.py:378
  27.5 1.6 %collective-permute-done.9 = bf16[128,256]{1,0:T(8,128)(2,1)S(1)} collective-permute-done((bf16[128,256]{1,0:T(8,128)(2,1)S(1)}, bf16[128,256]{1,0:T(8,128)(2,1)S(1)}, u32[]{:S(2)}, u32[]{:S(2)}) %collective-permute-start.9) | collective-permute-done | bytes 65568 | tf_op jit(solution)/shard_map/ppermute | solution.py:378
  29.1 0.1 add_convert_fusion
  29.1 0.6 %fusion = (bf16[128,128]{1,0:T(8,128)(2,1)}, bf16[128,128]{1,0:T(8,128)(2,1)}) fusion(bf16[128,256]{1,0:T(8,128)(2,1)S(1)} %add_convert_fusion), kind=kLoop, calls=%fused_computation.1 | loop fusion | bytes 131072 | tf_op jit(solution)/shard_map/slice | solution.py:384
  (1 shorter events, 0.0 us)
Async XLA Ops:
  0.6 11.1 %copy-start.2 = (s32[4,12]{1,0:T(4,128)S(1)}, s32[4,12]{1,0:T(4,128)}, u32[]{:S(2)}) copy-start(s32[4,12]{1,0:T(4,128)} %doc_ref.1) | copy-start | bytes 580
  0.6 11.1 %copy-start.1 = (bf16[128,1024]{1,0:T(8,128)(2,1)S(1)}, bf16[128,1024]{1,0:T(8,128)(2,1)}, u32[]{:S(2)}) copy-start(bf16[128,1024]{1,0:T(8,128)(2,1)} %grad_ref.1) | copy-start | bytes 786436
  0.7 11.1 %copy-start = (bf16[128,1024]{1,0:T(8,128)(2,1)S(1)}, bf16[128,1024]{1,0:T(8,128)(2,1)}, u32[]{:S(2)}) copy-start(bf16[128,1024]{1,0:T(8,128)(2,1)} %query_ref.1) | copy-start | bytes 786436
  1.5 11.1 %collective-permute-start.4 = (bf16[128,256]{1,0:T(8,128)(2,1)S(1)}, bf16[128,256]{1,0:T(8,128)(2,1)S(1)}, u32[]{:S(2)}, u32[]{:S(2)}) collective-permute-start(bf16[128,256]{1,0:T(8,128)(2,1)S(1)} %fetch.1.refs_0_.refs_2_), channel_id=1, source_target_pairs={{0,1},{1,2},{2,3},{3,4},{8,9},{9,10},{10,11},{11,12},{16,17},{17,1... | collective-permute-start | bytes 196616 | tf_op jit(solution)/shard_map/ppermute | solution.py:277
  5.0 7.7 %collective-permute-start.3 = (bf16[128,256]{1,0:T(8,128)(2,1)S(1)}, bf16[128,256]{1,0:T(8,128)(2,1)S(1)}, u32[]{:S(2)}, u32[]{:S(2)}) collective-permute-start(bf16[128,256]{1,0:T(8,128)(2,1)S(1)} %fetch.1.refs_0_.refs_2_), channel_id=1, source_target_pairs={{0,3},{1,4},{2,5},{3,6},{4,7},{8,11},{9,12},{10,13},{11,14},{12,15... | collective-permute-start | bytes 196616 | tf_op jit(solution)/shard_map/ppermute | solution.py:277
  6.9 6.0 %collective-permute-start.2 = (bf16[128,256]{1,0:T(8,128)(2,1)S(1)}, bf16[128,256]{1,0:T(8,128)(2,1)S(1)}, u32[]{:S(2)}, u32[]{:S(2)}) collective-permute-start(bf16[128,256]{1,0:T(8,128)(2,1)S(1)} %fetch.1.refs_0_.refs_2_), channel_id=1, source_target_pairs={{0,4},{1,5},{2,6},{3,7},{8,12},{9,13},{10,14},{11,15},{16,20},{17,... | collective-permute-start | bytes 196616 | tf_op jit(solution)/shard_map/ppermute | solution.py:277
  8.2 4.7 %collective-permute-start.1 = (bf16[128,256]{1,0:T(8,128)(2,1)S(1)}, bf16[128,256]{1,0:T(8,128)(2,1)S(1)}, u32[]{:S(2)}, u32[]{:S(2)}) collective-permute-start(bf16[128,256]{1,0:T(8,128)(2,1)S(1)} %fetch.1.refs_0_.refs_2_), channel_id=1, source_target_pairs={{4,5},{5,6},{6,7},{12,13},{13,14},{14,15},{20,21},{21,22},{22,23},... | collective-permute-start | bytes 196616 | tf_op jit(solution)/shard_map/ppermute | solution.py:277
  8.9 6.2 %collective-permute-start = (bf16[128,256]{1,0:T(8,128)(2,1)S(1)}, bf16[128,256]{1,0:T(8,128)(2,1)S(1)}, u32[]{:S(2)}, u32[]{:S(2)}) collective-permute-start(bf16[128,256]{1,0:T(8,128)(2,1)S(1)} %fetch.1.refs_0_.refs_2_), channel_id=1, source_target_pairs={{0,2},{1,3},{2,4},{3,5},{4,6},{5,7},{8,10},{9,11},{10,12},{11,13},... | collective-permute-start | bytes 196616 | tf_op jit(solution)/shard_map/ppermute | solution.py:277
  16.2 9.7 %collective-permute-start.5 = (bf16[128,256]{1,0:T(8,128)(2,1)S(1)}, bf16[128,256]{1,0:T(8,128)(2,1)S(1)}, u32[]{:S(2)}, u32[]{:S(2)}) collective-permute-start(bf16[128,256]{1,0:T(8,128)(2,1)S(1)} %get-tuple-element.39), channel_id=1, source_target_pairs={{4,0},{5,1},{6,2},{7,3},{12,8},{13,9},{14,10},{15,11},{20,16},{21,... | collective-permute-start | bytes 196616 | tf_op jit(solution)/shard_map/ppermute | solution.py:378
  17.5 8.4 %collective-permute-start.6 = (bf16[128,256]{1,0:T(8,128)(2,1)S(1)}, bf16[128,256]{1,0:T(8,128)(2,1)S(1)}, u32[]{:S(2)}, u32[]{:S(2)}) collective-permute-start(bf16[128,256]{1,0:T(8,128)(2,1)S(1)} %get-tuple-element.40), channel_id=1, source_target_pairs={{3,0},{4,1},{5,2},{6,3},{7,4},{11,8},{12,9},{13,10},{14,11},{15,12... | collective-permute-start | bytes 196616 | tf_op jit(solution)/shard_map/ppermute | solution.py:378
  19.4 6.5 %collective-permute-start.7 = (bf16[128,256]{1,0:T(8,128)(2,1)S(1)}, bf16[128,256]{1,0:T(8,128)(2,1)S(1)}, u32[]{:S(2)}, u32[]{:S(2)}) collective-permute-start(bf16[128,256]{1,0:T(8,128)(2,1)S(1)} %get-tuple-element.41), channel_id=1, source_target_pairs={{6,5},{7,6},{14,13},{15,14},{22,21},{23,22},{30,29},{31,30}} | collective-permute-start | bytes 196616 | tf_op jit(solution)/shard_map/ppermute | solution.py:378
  20.1 7.4 %collective-permute-start.8 = (bf16[128,256]{1,0:T(8,128)(2,1)S(1)}, bf16[128,256]{1,0:T(8,128)(2,1)S(1)}, u32[]{:S(2)}, u32[]{:S(2)}) collective-permute-start(bf16[128,256]{1,0:T(8,128)(2,1)S(1)} %get-tuple-element.42), channel_id=1, source_target_pairs={{2,0},{3,1},{4,2},{5,3},{6,4},{7,5},{10,8},{11,9},{12,10},{13,11},... | collective-permute-start | bytes 196616 | tf_op jit(solution)/shard_map/ppermute | solution.py:378
  22.0 7.1 %collective-permute-start.9 = (bf16[128,256]{1,0:T(8,128)(2,1)S(1)}, bf16[128,256]{1,0:T(8,128)(2,1)S(1)}, u32[]{:S(2)}, u32[]{:S(2)}) collective-permute-start(bf16[128,256]{1,0:T(8,128)(2,1)S(1)} %get-tuple-element.43), channel_id=1, source_target_pairs={{1,0},{2,1},{3,2},{4,3},{5,4},{9,8},{10,9},{11,10},{12,11},{13,12}... | collective-permute-start | bytes 196616 | tf_op jit(solution)/shard_map/ppermute | solution.py:378

commit v8 on v7

--- a/solution.py
+++ b/solution.py
@@ -12,7 +12,7 @@
 PAIR = 2
 masked_score = -1e30
 IN_ORDER = (0, 2, 1, 4, 3)
-OUT_ORDER = (0, 4, 3, 2, 1)
+OUT_ORDER = (0, 4, 2, 3, 1)
 score_scale = 1.0 / math.sqrt(HD)
 exponent_scale = score_scale * math.log2(math.e)
 
@@ -371,9 +371,9 @@
     far_places = [late] + sorted(early)[1:]
     total = side_by_side(totals)
     returns = [(back, 0, devices) for back in ordered(list(range(blocks)), OUT_ORDER)[1:]]
-    returns[-2:] = [(1, reach + 1, devices), returns[-2], (1, 0, reach + 1)]
+    returns[-1:] = [(1, reach, devices), (1, 0, reach)]
     for back, first, last in returns:
-        index = reach if last == reach + 1 else far_places.index(back)
+        index = reach if last == reach else far_places.index(back)
         terms = side_by_side([own[index] for own in far])
         terms = lax.ppermute(
             terms, "ulysses", [(d + back, d) for d in range(first, min(last, devices - back))]

time: 30.1 us -> 30.4 us (level)
  the two profiles are of different devices: /device:TPU:10 before, /device:TPU:22 now
where the time goes in v8:
time: 30.4 us; the launch traced here: 30.1 us
  starting transfers between devices  18 us (59%)
  Pallas kernels  5.71 us (19%)
  waiting for transfers between devices  4.93 us (16%)
  between operations  0.81 us (3%)
  local copies, waits for them, and re-layouts  0.64 us (2%)
    ppermute x5, starting transfers between devices, per_device(): lax.ppermute(terms, 'ulysses', [(d + back, d) for d in range(first, min(l...  9.34 us
    ppermute x5, starting transfers between devices, forward(): lax.ppermute(kv, 'ulysses', [(d - back, d) for d in range(max(first, back...  8.63 us
    pallas_call x5, Pallas kernels, call(): pl.pallas_call(body, out_shape=[jax.ShapeDtypeStruct(shape, dtype) for sh...  5.71 us
    ppermute x5, waiting for transfers between devices, forward(): lax.ppermute(kv, 'ulysses', [(d - back, d) for d in range(max(first, back...  2.48 us
    ppermute x5, waiting for transfers between devices, per_device(): lax.ppermute(terms, 'ulysses', [(d + back, d) for d in range(first, min(l...  2.45 us
    slice x1, local copies, waits for them, and re-layouts, per_device(): total[:, block(2 * g + 1, HD)]  0.63 us
  transfers between devices with their start and end apart: 10, of which 4 were waited for; matrix products, arithmetic and copies ran while one was open for 0% of the time, Pallas kernels for 12%

profile of v8, /device:TPU:22, one launch (start us, length us, event | category | flops | bytes accessed | tf_op | source)
XLA Modules:
  0.0 30.1 jit_solution(15058350669458020315)
XLA Ops:
  0.6 0.0 copy-start.2
  0.6 0.0 copy-start.1
  0.7 0.0 copy-start
  0.7 0.8 %fetch.1.refs_0_.refs_2_ = bf16[128,256]{1,0:T(8,128)(2,1)S(1)} custom-call(bf16[128,128]{1,0:T(8,128)(2,1)} %key_hbm.1, bf16[128,128]{1,0:T(8,128)(2,1)} %value_hbm.1), custom_call_target="tpu_custom_call" | custom-call | flops 2684354560 | bytes 131080 | tf_op jit(solution)/shard_map/fetch/pallas_call | solution.py:226
  1.5 0.7 %collective-permute-start.4 = (bf16[128,256]{1,0:T(8,128)(2,1)S(1)}, bf16[128,256]{1,0:T(8,128)(2,1)S(1)}, u32[]{:S(2)}, u32[]{:S(2)}) collective-permute-start(bf16[128,256]{1,0:T(8,128)(2,1)S(1)} %fetch.1.refs_0_.refs_2_), channel_id=1, source_target_pairs={{0,1},{1,2},{2,3},{3,4},{8,9},{9,10},{10,11},{11,12},{16,17},{17,1... | collective-permute-start | bytes 196616 | tf_op jit(solution)/shard_map/ppermute | solution.py:277
  2.2 1.3 %collective-permute-start.3 = (bf16[128,256]{1,0:T(8,128)(2,1)S(1)}, bf16[128,256]{1,0:T(8,128)(2,1)S(1)}, u32[]{:S(2)}, u32[]{:S(2)}) collective-permute-start(bf16[128,256]{1,0:T(8,128)(2,1)S(1)} %fetch.1.refs_0_.refs_2_), channel_id=1, source_target_pairs={{0,3},{1,4},{2,5},{3,6},{4,7},{8,11},{9,12},{10,13},{11,14},{12,15... | collective-permute-start | bytes 196616 | tf_op jit(solution)/shard_map/ppermute | solution.py:277
  3.5 1.3 %collective-permute-start.2 = (bf16[128,256]{1,0:T(8,128)(2,1)S(1)}, bf16[128,256]{1,0:T(8,128)(2,1)S(1)}, u32[]{:S(2)}, u32[]{:S(2)}) collective-permute-start(bf16[128,256]{1,0:T(8,128)(2,1)S(1)} %fetch.1.refs_0_.refs_2_), channel_id=1, source_target_pairs={{0,4},{1,5},{2,6},{3,7},{8,12},{9,13},{10,14},{11,15},{16,20},{17,... | collective-permute-start | bytes 196616 | tf_op jit(solution)/shard_map/ppermute | solution.py:277
  4.8 3.5 %collective-permute-start.1 = (bf16[128,256]{1,0:T(8,128)(2,1)S(1)}, bf16[128,256]{1,0:T(8,128)(2,1)S(1)}, u32[]{:S(2)}, u32[]{:S(2)}) collective-permute-start(bf16[128,256]{1,0:T(8,128)(2,1)S(1)} %fetch.1.refs_0_.refs_2_), channel_id=1, source_target_pairs={{4,5},{5,6},{6,7},{12,13},{13,14},{14,15},{20,21},{21,22},{22,23},... | collective-permute-start | bytes 196616 | tf_op jit(solution)/shard_map/ppermute | solution.py:277
  8.3 1.9 %collective-permute-start = (bf16[128,256]{1,0:T(8,128)(2,1)S(1)}, bf16[128,256]{1,0:T(8,128)(2,1)S(1)}, u32[]{:S(2)}, u32[]{:S(2)}) collective-permute-start(bf16[128,256]{1,0:T(8,128)(2,1)S(1)} %fetch.1.refs_0_.refs_2_), channel_id=1, source_target_pairs={{0,2},{1,3},{2,4},{3,5},{4,6},{5,7},{8,10},{9,11},{10,12},{11,13},... | collective-permute-start | bytes 196616 | tf_op jit(solution)/shard_map/ppermute | solution.py:277
  10.2 0.0 copy-done.2
  10.2 0.0 copy-done.1
  10.2 0.8 %prepare.1 = (bf16[1024,128]{1,0:T(8,128)(2,1)S(1)}, bf16[1024,128]{1,0:T(8,128)(2,1)S(1)}, bf16[256,1024]{1,0:T(8,128)(2,1)S(1)}, bf16[128,1024]{1,0:T(8,128)(2,1)S(1)}, bf16[640,128]{1,0:T(8,128)(2,1)S(1)}) custom-call(s32[4,12]{1,0:T(4,128)S(1)} %copy-done.2, bf16[128,1024]{1,0:T(8,128)(2,1)S(1)} %copy-done, bf16[128,1024]{1,0:T(8,128)(2,1)S(1)} %copy-done.1), custom_call_target="tpu_custom_call" | custom-call | flops 41943040 | bytes 1999040 | tf_op jit(solution)/shard_map/prepare/pallas_call | solution.py:226
  11.1 0.0 collective-permute-done.4.refs_4_.refs_6_
  11.1 0.0 collective-permute-done.3.refs_3_.refs_5_
  11.1 0.2 collective-permute-done.2.refs_2_.refs_4_
  11.3 0.7 %collective-permute-done.1.refs_1_.refs_3_ = bf16[128,256]{1,0:T(8,128)(2,1)S(1)} collective-permute-done((bf16[128,256]{1,0:T(8,128)(2,1)S(1)}, bf16[128,256]{1,0:T(8,128)(2,1)S(1)}, u32[]{:S(2)}, u32[]{:S(2)}) %collective-permute-start.1) | collective-permute-done | bytes 65568 | tf_op jit(solution)/shard_map/ppermute | solution.py:277
  12.0 1.2 %early.1 = (bf16[512,1024]{1,0:T(8,128)(2,1)S(1)}, f32[512,1024]{1,0:T(8,128)S(1)}, f32[3,1024]{1,0:T(4,128)S(1)}, f32[128,1024]{1,0:T(8,128)S(1)}) custom-call(bf16[256,1024]{1,0:T(8,128)(2,1)S(1)} %get-tuple-element.26.query_t_ref, bf16[128,1024]{1,0:T(8,128)(2,1)S(1)} %get-tuple-element.27.grad_t_ref, bf16[640,128]{1,0:T(8,128)(2,1)S(1)} %get-tuple-element.28.bias_ref, ...), custom_call_target="tpu_custom_call" | custom-call | flops 503316480 | bytes 7057408 | tf_op jit(solution)/shard_map/early/pallas_call | solution.py:226
  13.2 1.6 %collective-permute-done.refs_0_.refs_1_ = bf16[128,256]{1,0:T(8,128)(2,1)S(1)} collective-permute-done((bf16[128,256]{1,0:T(8,128)(2,1)S(1)}, bf16[128,256]{1,0:T(8,128)(2,1)S(1)}, u32[]{:S(2)}, u32[]{:S(2)}) %collective-permute-start) | collective-permute-done | bytes 65568 | tf_op jit(solution)/shard_map/ppermute | solution.py:277
  14.8 1.3 %late.1 = (bf16[640,1024]{1,0:T(8,128)(2,1)S(1)}, bf16[640,1024]{1,0:T(8,128)(2,1)S(1)}, f32[1,1024]{1,0:T(1,128)S(1)}, bf16[128,256]{1,0:T(8,128)(2,1)S(1)}, bf...) custom-call(bf16[1024,128]{1,0:T(8,128)(2,1)S(1)} %get-tuple-element, ...), custom_call_target="tpu_custom_call" | custom-call | flops 335544320 | bytes 7651328 | tf_op jit(solution)/shard_map/late/pallas_call | solution.py:226
  16.1 1.3 %collective-permute-start.5 = (bf16[128,256]{1,0:T(8,128)(2,1)S(1)}, bf16[128,256]{1,0:T(8,128)(2,1)S(1)}, u32[]{:S(2)}, u32[]{:S(2)}) collective-permute-start(bf16[128,256]{1,0:T(8,128)(2,1)S(1)} %get-tuple-element.39), channel_id=1, source_target_pairs={{4,0},{5,1},{6,2},{7,3},{12,8},{13,9},{14,10},{15,11},{20,16},{21,... | collective-permute-start | bytes 196616 | tf_op jit(solution)/shard_map/ppermute | solution.py:378
  17.4 2.4 %collective-permute-start.6 = (bf16[128,256]{1,0:T(8,128)(2,1)S(1)}, bf16[128,256]{1,0:T(8,128)(2,1)S(1)}, u32[]{:S(2)}, u32[]{:S(2)}) collective-permute-start(bf16[128,256]{1,0:T(8,128)(2,1)S(1)} %get-tuple-element.40), channel_id=1, source_target_pairs={{2,0},{3,1},{4,2},{5,3},{6,4},{7,5},{10,8},{11,9},{12,10},{13,11},... | collective-permute-start | bytes 196616 | tf_op jit(solution)/shard_map/ppermute | solution.py:378
  19.9 2.5 %collective-permute-start.7 = (bf16[128,256]{1,0:T(8,128)(2,1)S(1)}, bf16[128,256]{1,0:T(8,128)(2,1)S(1)}, u32[]{:S(2)}, u32[]{:S(2)}) collective-permute-start(bf16[128,256]{1,0:T(8,128)(2,1)S(1)} %get-tuple-element.41), channel_id=1, source_target_pairs={{3,0},{4,1},{5,2},{6,3},{7,4},{11,8},{12,9},{13,10},{14,11},{15,12... | collective-permute-start | bytes 196616 | tf_op jit(solution)/shard_map/ppermute | solution.py:378
  22.4 2.5 %collective-permute-start.8 = (bf16[128,256]{1,0:T(8,128)(2,1)S(1)}, bf16[128,256]{1,0:T(8,128)(2,1)S(1)}, u32[]{:S(2)}, u32[]{:S(2)}) collective-permute-start(bf16[128,256]{1,0:T(8,128)(2,1)S(1)} %get-tuple-element.42), channel_id=1, source_target_pairs={{5,4},{6,5},{7,6},{13,12},{14,13},{15,14},{21,20},{22,21},{23,22},... | collective-permute-start | bytes 196616 | tf_op jit(solution)/shard_map/ppermute | solution.py:378
  24.8 0.7 %collective-permute-start.9 = (bf16[128,256]{1,0:T(8,128)(2,1)S(1)}, bf16[128,256]{1,0:T(8,128)(2,1)S(1)}, u32[]{:S(2)}, u32[]{:S(2)}) collective-permute-start(bf16[128,256]{1,0:T(8,128)(2,1)S(1)} %get-tuple-element.43), channel_id=1, source_target_pairs={{1,0},{2,1},{3,2},{4,3},{9,8},{10,9},{11,10},{12,11},{17,16},{18,1... | collective-permute-start | bytes 196616 | tf_op jit(solution)/shard_map/ppermute | solution.py:378
  25.5 1.5 %near.1 = (bf16[128,1024]{1,0:T(8,128)(2,1)}, bf16[128,1024]{1,0:T(8,128)(2,1)}, f32[128,256]{1,0:T(8,128)S(1)}) custom-call(bf16[1024,128]{1,0:T(8,128)(2,1)S(1)} %get-tuple-element.24.query_ref, bf16[1024,128]{1,0:T(8,128)(2,1)S(1)} %get-tuple-element.25.grad_ref, bf16[640,1024]{1,0:T(8,128)(2,1)S(1)} %get-tuple-element.32.weights_ref, ...), custom_call_target="tpu_custom_call" | custom-call | flops 335544320 | bytes 4722688 | tf_op jit(solution)/shard_map/near/pallas_call | solution.py:226
  27.0 0.0 collective-permute-done.5
  27.0 0.0 collective-permute-done.6
  27.0 0.0 collective-permute-done.7
  27.0 2.4 %collective-permute-done.8 = bf16[128,256]{1,0:T(8,128)(2,1)S(1)} collective-permute-done((bf16[128,256]{1,0:T(8,128)(2,1)S(1)}, bf16[128,256]{1,0:T(8,128)(2,1)S(1)}, u32[]{:S(2)}, u32[]{:S(2)}) %collective-permute-start.8) | collective-permute-done | bytes 65568 | tf_op jit(solution)/shard_map/ppermute | solution.py:378
  29.4 0.0 collective-permute-done.9
  29.4 0.1 add_convert_fusion
  29.5 0.6 %fusion = (bf16[128,128]{1,0:T(8,128)(2,1)}, bf16[128,128]{1,0:T(8,128)(2,1)}) fusion(bf16[128,256]{1,0:T(8,128)(2,1)S(1)} %add_convert_fusion), kind=kLoop, calls=%fused_computation.1 | loop fusion | bytes 131072 | tf_op jit(solution)/shard_map/slice | solution.py:384
  (1 shorter events, 0.0 us)
Async XLA Ops:
  0.6 9.6 %copy-start.2 = (s32[4,12]{1,0:T(4,128)S(1)}, s32[4,12]{1,0:T(4,128)}, u32[]{:S(2)}) copy-start(s32[4,12]{1,0:T(4,128)} %doc_ref.1) | copy-start | bytes 580
  0.6 9.6 %copy-start.1 = (bf16[128,1024]{1,0:T(8,128)(2,1)S(1)}, bf16[128,1024]{1,0:T(8,128)(2,1)}, u32[]{:S(2)}) copy-start(bf16[128,1024]{1,0:T(8,128)(2,1)} %grad_ref.1) | copy-start | bytes 786436
  0.7 9.6 %copy-start = (bf16[128,1024]{1,0:T(8,128)(2,1)S(1)}, bf16[128,1024]{1,0:T(8,128)(2,1)}, u32[]{:S(2)}) copy-start(bf16[128,1024]{1,0:T(8,128)(2,1)} %query_ref.1) | copy-start | bytes 786436
  1.5 9.5 %collective-permute-start.4 = (bf16[128,256]{1,0:T(8,128)(2,1)S(1)}, bf16[128,256]{1,0:T(8,128)(2,1)S(1)}, u32[]{:S(2)}, u32[]{:S(2)}) collective-permute-start(bf16[128,256]{1,0:T(8,128)(2,1)S(1)} %fetch.1.refs_0_.refs_2_), channel_id=1, source_target_pairs={{0,1},{1,2},{2,3},{3,4},{8,9},{9,10},{10,11},{11,12},{16,17},{17,1... | collective-permute-start | bytes 196616 | tf_op jit(solution)/shard_map/ppermute | solution.py:277
  2.2 8.9 %collective-permute-start.3 = (bf16[128,256]{1,0:T(8,128)(2,1)S(1)}, bf16[128,256]{1,0:T(8,128)(2,1)S(1)}, u32[]{:S(2)}, u32[]{:S(2)}) collective-permute-start(bf16[128,256]{1,0:T(8,128)(2,1)S(1)} %fetch.1.refs_0_.refs_2_), channel_id=1, source_target_pairs={{0,3},{1,4},{2,5},{3,6},{4,7},{8,11},{9,12},{10,13},{11,14},{12,15... | collective-permute-start | bytes 196616 | tf_op jit(solution)/shard_map/ppermute | solution.py:277
  3.5 7.8 %collective-permute-start.2 = (bf16[128,256]{1,0:T(8,128)(2,1)S(1)}, bf16[128,256]{1,0:T(8,128)(2,1)S(1)}, u32[]{:S(2)}, u32[]{:S(2)}) collective-permute-start(bf16[128,256]{1,0:T(8,128)(2,1)S(1)} %fetch.1.refs_0_.refs_2_), channel_id=1, source_target_pairs={{0,4},{1,5},{2,6},{3,7},{8,12},{9,13},{10,14},{11,15},{16,20},{17,... | collective-permute-start | bytes 196616 | tf_op jit(solution)/shard_map/ppermute | solution.py:277
  4.8 7.2 %collective-permute-start.1 = (bf16[128,256]{1,0:T(8,128)(2,1)S(1)}, bf16[128,256]{1,0:T(8,128)(2,1)S(1)}, u32[]{:S(2)}, u32[]{:S(2)}) collective-permute-start(bf16[128,256]{1,0:T(8,128)(2,1)S(1)} %fetch.1.refs_0_.refs_2_), channel_id=1, source_target_pairs={{4,5},{5,6},{6,7},{12,13},{13,14},{14,15},{20,21},{21,22},{22,23},... | collective-permute-start | bytes 196616 | tf_op jit(solution)/shard_map/ppermute | solution.py:277
  8.3 6.6 %collective-permute-start = (bf16[128,256]{1,0:T(8,128)(2,1)S(1)}, bf16[128,256]{1,0:T(8,128)(2,1)S(1)}, u32[]{:S(2)}, u32[]{:S(2)}) collective-permute-start(bf16[128,256]{1,0:T(8,128)(2,1)S(1)} %fetch.1.refs_0_.refs_2_), channel_id=1, source_target_pairs={{0,2},{1,3},{2,4},{3,5},{4,6},{5,7},{8,10},{9,11},{10,12},{11,13},... | collective-permute-start | bytes 196616 | tf_op jit(solution)/shard_map/ppermute | solution.py:277
  16.1 10.8 %collective-permute-start.5 = (bf16[128,256]{1,0:T(8,128)(2,1)S(1)}, bf16[128,256]{1,0:T(8,128)(2,1)S(1)}, u32[]{:S(2)}, u32[]{:S(2)}) collective-permute-start(bf16[128,256]{1,0:T(8,128)(2,1)S(1)} %get-tuple-element.39), channel_id=1, source_target_pairs={{4,0},{5,1},{6,2},{7,3},{12,8},{13,9},{14,10},{15,11},{20,16},{21,... | collective-permute-start | bytes 196616 | tf_op jit(solution)/shard_map/ppermute | solution.py:378
  17.4 9.5 %collective-permute-start.6 = (bf16[128,256]{1,0:T(8,128)(2,1)S(1)}, bf16[128,256]{1,0:T(8,128)(2,1)S(1)}, u32[]{:S(2)}, u32[]{:S(2)}) collective-permute-start(bf16[128,256]{1,0:T(8,128)(2,1)S(1)} %get-tuple-element.40), channel_id=1, source_target_pairs={{2,0},{3,1},{4,2},{5,3},{6,4},{7,5},{10,8},{11,9},{12,10},{13,11},... | collective-permute-start | bytes 196616 | tf_op jit(solution)/shard_map/ppermute | solution.py:378
  19.9 7.1 %collective-permute-start.7 = (bf16[128,256]{1,0:T(8,128)(2,1)S(1)}, bf16[128,256]{1,0:T(8,128)(2,1)S(1)}, u32[]{:S(2)}, u32[]{:S(2)}) collective-permute-start(bf16[128,256]{1,0:T(8,128)(2,1)S(1)} %get-tuple-element.41), channel_id=1, source_target_pairs={{3,0},{4,1},{5,2},{6,3},{7,4},{11,8},{12,9},{13,10},{14,11},{15,12... | collective-permute-start | bytes 196616 | tf_op jit(solution)/shard_map/ppermute | solution.py:378
  22.4 7.1 %collective-permute-start.8 = (bf16[128,256]{1,0:T(8,128)(2,1)S(1)}, bf16[128,256]{1,0:T(8,128)(2,1)S(1)}, u32[]{:S(2)}, u32[]{:S(2)}) collective-permute-start(bf16[128,256]{1,0:T(8,128)(2,1)S(1)} %get-tuple-element.42), channel_id=1, source_target_pairs={{5,4},{6,5},{7,6},{13,12},{14,13},{15,14},{21,20},{22,21},{23,22},... | collective-permute-start | bytes 196616 | tf_op jit(solution)/shard_map/ppermute | solution.py:378
  24.8 4.6 %collective-permute-start.9 = (bf16[128,256]{1,0:T(8,128)(2,1)S(1)}, bf16[128,256]{1,0:T(8,128)(2,1)S(1)}, u32[]{:S(2)}, u32[]{:S(2)}) collective-permute-start(bf16[128,256]{1,0:T(8,128)(2,1)S(1)} %get-tuple-element.43), channel_id=1, source_target_pairs={{1,0},{2,1},{3,2},{4,3},{9,8},{10,9},{11,10},{12,11},{17,16},{18,1... | collective-permute-start | bytes 196616 | tf_op jit(solution)/shard_map/ppermute | solution.py:378
